TPU v7x, 32 devices: a whole 2x2x4 slice. The times are simulated.
32 devices in a mesh: items: 8 (over y, x, core), band: 4 (over z).
Axes of the slice: x: 2, y: 2, z: 4, core: 2. Of those that a mesh axis runs over, the one named last changes fastest.
Arguments:
- tokens: bfloat16 [640, 64, 768], P('band', 'items'), may hold values from -6 to 6
- lengths: int32 [64], P('items'), may hold values from 257 to 577, as said below
- norm_attn: float32 [768], replicated, may hold values from 0.5 to 1.5
- w_query: bfloat16 [768, 768], replicated, may hold values from -0.21875 to 0.21875
- w_key: bfloat16 [768, 768], replicated, may hold values from -0.21875 to 0.21875
- w_value: bfloat16 [768, 768], replicated, may hold values from -0.21875 to 0.21875
- w_out: bfloat16 [768, 768], replicated, may hold values from -0.875 to 0.875
- norm_ffn: float32 [768], replicated, may hold values from 0.5 to 1.5
- w_gate: bfloat16 [768, 2048], replicated, may hold values from -0.21875 to 0.21875
- w_up: bfloat16 [768, 2048], replicated, may hold values from -0.21875 to 0.21875
- w_down: bfloat16 [2048, 768], replicated, may hold values from -0.125 to 0.125
- cotangent: bfloat16 [640, 64, 768], P('band', 'items'), may hold values from -6 to 6
Outputs:
- output: bfloat16 [640, 64, 768], P('band', 'items')
- grad_tokens: bfloat16 [640, 64, 768], P('band', 'items')
- grad_norm_attn: float32 [768], P(('items', 'band'))
- grad_w_query: float32 [768, 768], P(('items', 'band'))
- grad_w_key: float32 [768, 768], P(('items', 'band'))
- grad_w_value: float32 [768, 768], P(('items', 'band'))
- grad_w_out: float32 [768, 768], P(('items', 'band'))
- grad_norm_ffn: float32 [768], P(('items', 'band'))
- grad_w_gate: float32 [768, 2048], P(('items', 'band'))
- grad_w_up: float32 [768, 2048], P(('items', 'band'))
- grad_w_down: float32 [2048, 768], P(('items', 'band'))
Inputs may be any that keep to these rules, and one draw needn't show every extreme that they name: `lengths`: each item has 257 or 577 real tokens; every aligned group of 8 items holds both values.
All inputs are finite; a program needn't handle non-finite values.
Results may differ from a plain program's by a relative error of at most 0.018.
Values may be sent and summed in bfloat16 or wider, within the bound.
A program may use at most 320 MiB of HBM per device.

v0:
```python
import jax
import jax.numpy as jnp
from jax import lax
from jax.sharding import PartitionSpec as P

HEAD_DIM = 64


EPS = 1e-05
NEG = -1e30
ROPE_BASE = 10000.0


def rope_tables(positions, head_size):
    half_dim = head_size // 2
    frequency = jnp.exp(
        -jnp.log(ROPE_BASE) * (2.0 * jnp.arange(half_dim, dtype=jnp.float32) / head_size)
    )
    angles = positions.astype(jnp.float32)[:, None] * frequency[None, :]
    return (jnp.cos(angles), jnp.sin(angles))


def rotate(vector, cos_table, sin_table):
    half_dim = vector.shape[-1] // 2
    lower_half = vector[..., :half_dim]
    upper_half = vector[..., half_dim:]
    return jnp.concatenate(
        [
            lower_half * cos_table - upper_half * sin_table,
            lower_half * sin_table + upper_half * cos_table,
        ],
        -1,
    )


def product(left, right):
    return jnp.dot(left, right, preferred_element_type=jnp.float32)


def norm_forward(activations, gain_vec):
    inv_rms = lax.rsqrt(jnp.mean(activations * activations, -1, keepdims=True) + EPS)
    return (activations * inv_rms * gain_vec, inv_rms)


def norm_backward(incoming, activations, inv_rms, gain_vec):
    weighted = incoming * gain_vec
    gain_grad = jnp.sum(incoming * activations * inv_rms, 0)
    input_grad = inv_rms * weighted - activations * inv_rms**3 * jnp.mean(
        weighted * activations, -1, keepdims=True
    )
    return (input_grad, gain_grad)


def attention_scores(queries, key_rows, query_pos, key_pos, lengths):
    scores = jnp.einsum(
        "qihd,kihd->qihk", queries, key_rows, preferred_element_type=jnp.float32
    ) * queries.shape[-1] ** (-0.5)
    allowed = (key_pos[None, None, :] <= query_pos[:, None, None]) & (
        key_pos[None, None, :] < lengths[None, :, None]
    )
    allowed = allowed[:, :, None, :]
    return (jnp.where(allowed, scores, NEG), allowed)


def per_device(
    tokens,
    lengths,
    norm_attn,
    w_query,
    w_key,
    w_value,
    w_out,
    norm_ffn,
    w_gate,
    w_up,
    w_down,
    cotangent,
):
    band_rows, items_here, width = tokens.shape
    head_count = width // HEAD_DIM
    row_count = band_rows * items_here
    head_shape = (band_rows, items_here, head_count, HEAD_DIM)
    first_row = lax.axis_index("band") * band_rows
    query_pos = first_row + jnp.arange(band_rows, dtype=jnp.int32)
    cos_table, sin_table = rope_tables(query_pos, HEAD_DIM)
    cos_table = cos_table[:, None, None, :]
    sin_table = sin_table[:, None, None, :]
    inputs = tokens.astype(jnp.float32).reshape(row_count, width)
    normed, inv_one = norm_forward(inputs, norm_attn)
    normed_low = normed.astype(jnp.bfloat16)
    queries = rotate(product(normed_low, w_query).reshape(head_shape), cos_table, sin_table).astype(
        jnp.bfloat16
    )
    key_rows = rotate(product(normed_low, w_key).reshape(head_shape), cos_table, sin_table).astype(
        jnp.bfloat16
    )
    values = product(normed_low, w_value).astype(jnp.bfloat16).reshape(head_shape)
    running_max = jnp.full(head_shape[:3], NEG, jnp.float32)
    key_piece = lax.all_gather(key_rows, "band", axis=0, tiled=True)
    value_piece = lax.all_gather(values, "band", axis=0, tiled=True)
    key_pos = jnp.arange(key_piece.shape[0], dtype=jnp.int32)
    scores, allowed = attention_scores(queries, key_piece, query_pos, key_pos, lengths)
    new_max = jnp.maximum(running_max, jnp.max(scores, -1))
    block_weights = jnp.where(allowed, jnp.exp(scores - new_max[..., None]), 0.0)
    new_sum = jnp.sum(block_weights, -1)
    new_acc = jnp.einsum(
        "qihk,kihd->qihd",
        block_weights.astype(jnp.bfloat16),
        value_piece,
        preferred_element_type=jnp.float32,
    )
    attended = new_acc / new_sum[..., None]
    log_total = new_max + jnp.log(new_sum)
    attended_low = attended.astype(jnp.bfloat16).reshape(row_count, width)
    resid = inputs + product(attended_low, w_out)
    normed_two, inv_two = norm_forward(resid, norm_ffn)
    normed_two_low = normed_two.astype(jnp.bfloat16)
    gate_pre = product(normed_two_low, w_gate)
    upward = product(normed_two_low, w_up)
    sigmoid_gate = jax.nn.sigmoid(gate_pre)
    silu_gate = gate_pre * sigmoid_gate
    hidden = (silu_gate * upward).astype(jnp.bfloat16)
    output = (resid + product(hidden, w_down)).astype(jnp.bfloat16).reshape(tokens.shape)
    out_grad = cotangent.reshape(row_count, width)
    grad_down = jnp.einsum("nf,nd->fd", hidden, out_grad, preferred_element_type=jnp.float32)
    grad_hidden = jnp.einsum("nd,fd->nf", out_grad, w_down, preferred_element_type=jnp.float32)
    grad_gate = (
        grad_hidden * upward * sigmoid_gate * (1.0 + gate_pre * (1.0 - sigmoid_gate))
    ).astype(jnp.bfloat16)
    grad_upward = (grad_hidden * silu_gate).astype(jnp.bfloat16)
    grad_w_gate = jnp.einsum(
        "nd,nf->df", normed_two_low, grad_gate, preferred_element_type=jnp.float32
    )
    grad_w_up = jnp.einsum(
        "nd,nf->df", normed_two_low, grad_upward, preferred_element_type=jnp.float32
    )
    grad_normed_two = jnp.einsum(
        "nf,df->nd", grad_gate, w_gate, preferred_element_type=jnp.float32
    ) + jnp.einsum("nf,df->nd", grad_upward, w_up, preferred_element_type=jnp.float32)
    grad_resid, grad_norm_ffn = norm_backward(grad_normed_two, resid, inv_two, norm_ffn)
    grad_resid = grad_resid + out_grad.astype(jnp.float32)
    grad_resid_low = grad_resid.astype(jnp.bfloat16)
    grad_w_out = jnp.einsum(
        "nd,ne->de", attended_low, grad_resid_low, preferred_element_type=jnp.float32
    )
    grad_attended = (
        jnp.einsum("ne,de->nd", grad_resid_low, w_out, preferred_element_type=jnp.float32)
        .astype(jnp.bfloat16)
        .reshape(head_shape)
    )
    keys_all, values_all = (
        lax.all_gather(key_rows, "band", axis=0, tiled=True),
        lax.all_gather(values, "band", axis=0, tiled=True),
    )
    key_pos_all = jnp.arange(keys_all.shape[0], dtype=jnp.int32)
    scores, allowed = attention_scores(queries, keys_all, query_pos, key_pos_all, lengths)
    attn_prob = jnp.where(allowed, jnp.exp(scores - log_total[..., None]), 0.0)
    grad_prob = jnp.einsum(
        "qihd,kihd->qihk", grad_attended, values_all, preferred_element_type=jnp.float32
    )
    row_delta = jnp.sum(attn_prob * grad_prob, -1, keepdims=True)
    grad_scores = (attn_prob * (grad_prob - row_delta)).astype(jnp.bfloat16)
    inv_root = HEAD_DIM ** (-0.5)
    grad_queries = (
        jnp.einsum("qihk,kihd->qihd", grad_scores, keys_all, preferred_element_type=jnp.float32)
        * inv_root
    )
    prob_low = attn_prob.astype(jnp.bfloat16)
    row_span = lax.axis_size("band") * band_rows
    key_grads = (
        jnp.einsum("qihk,qihd->kihd", grad_scores, queries, preferred_element_type=jnp.float32)
        * inv_root
    )
    value_grads = jnp.einsum(
        "qihk,qihd->kihd", prob_low, grad_attended, preferred_element_type=jnp.float32
    )
    own_grads = lax.psum_scatter(
        jnp.concatenate(
            [
                key_grads.reshape(row_span, items_here, width),
                value_grads.reshape(row_span, items_here, width),
            ],
            -1,
        ).astype(jnp.bfloat16),
        "band",
        scatter_dimension=0,
        tiled=True,
    ).astype(jnp.float32)
    grad_keys_own = own_grads[..., :width].reshape(head_shape)
    grad_values_own = own_grads[..., width:].reshape(row_count, width)
    grad_query_pre = (
        rotate(grad_queries, cos_table, -sin_table).astype(jnp.bfloat16).reshape(row_count, width)
    )
    grad_key_pre = (
        rotate(grad_keys_own, cos_table, -sin_table).astype(jnp.bfloat16).reshape(row_count, width)
    )
    grad_value_pre = grad_values_own.astype(jnp.bfloat16)
    grad_w_query = jnp.einsum(
        "nd,ne->de", normed_low, grad_query_pre, preferred_element_type=jnp.float32
    )
    grad_w_key = jnp.einsum(
        "nd,ne->de", normed_low, grad_key_pre, preferred_element_type=jnp.float32
    )
    grad_w_value = jnp.einsum(
        "nd,ne->de", normed_low, grad_value_pre, preferred_element_type=jnp.float32
    )
    grad_normed = (
        jnp.einsum("ne,de->nd", grad_query_pre, w_query, preferred_element_type=jnp.float32)
        + jnp.einsum("ne,de->nd", grad_key_pre, w_key, preferred_element_type=jnp.float32)
        + jnp.einsum("ne,de->nd", grad_value_pre, w_value, preferred_element_type=jnp.float32)
    )
    grad_input, grad_norm_attn = norm_backward(grad_normed, inputs, inv_one, norm_attn)
    grad_tokens = (grad_resid + grad_input).astype(jnp.bfloat16).reshape(tokens.shape)
    summed = (
        lax.psum_scatter(grad_norm_attn, ("items", "band"), scatter_dimension=0, tiled=True),
        lax.psum_scatter(grad_w_query, ("items", "band"), scatter_dimension=0, tiled=True),
        lax.psum_scatter(grad_w_key, ("items", "band"), scatter_dimension=0, tiled=True),
        lax.psum_scatter(grad_w_value, ("items", "band"), scatter_dimension=0, tiled=True),
        lax.psum_scatter(grad_w_out, ("items", "band"), scatter_dimension=0, tiled=True),
        lax.psum_scatter(grad_norm_ffn, ("items", "band"), scatter_dimension=0, tiled=True),
        lax.psum_scatter(grad_w_gate, ("items", "band"), scatter_dimension=0, tiled=True),
        lax.psum_scatter(grad_w_up, ("items", "band"), scatter_dimension=0, tiled=True),
        lax.psum_scatter(grad_down, ("items", "band"), scatter_dimension=0, tiled=True),
    )
    return (
        output,
        grad_tokens,
        summed[0],
        summed[1],
        summed[2],
        summed[3],
        summed[4],
        summed[5],
        summed[6],
        summed[7],
        summed[8],
    )


def solution(mesh):
    placed = (
        P("band", "items", None),
        P("items"),
        P(),
        P(),
        P(),
        P(),
        P(),
        P(),
        P(),
        P(),
        P(),
        P("band", "items", None),
    )
    return jax.shard_map(
        per_device,
        mesh=mesh,
        in_specs=placed,
        out_specs=(
            P("band", "items", None),
            P("band", "items", None),
            P(("items", "band")),
            P(("items", "band"), None),
            P(("items", "band"), None),
            P(("items", "band"), None),
            P(("items", "band"), None),
            P(("items", "band")),
            P(("items", "band"), None),
            P(("items", "band"), None),
            P(("items", "band"), None),
        ),
        check_vma=False,
    )
```

profile of v0, /device:TPU:0, one launch (start us, length us, event | category | flops | bytes accessed | tf_op | source)
XLA Modules:
  0.0 1891.1 jit_solution(7667269399777474558)
XLA Ops:
  57.3 250.6 %all-gather.5.cloned.1.call-done = bf16[640,8,12,64]{3,1,2,0:T(8,128)(2,1)} async-done(((bf16[160,8,12,64]{3,1,2,0:T(8,128)(2,1)}), bf16[640,8,12,64]{3,1,2,0:T(8,128)(2,1)}) %all-gather.5.cloned.1.call-update) | async-done | bytes 7864336 | tf_op jit(solution)/shard_map/all_gather | solution.py:99
  307.9 20.7 %copy.84 = bf16[640,8,12,64]{0,3,2,1:T(8,128)(2,1)} copy(bf16[640,8,12,64]{3,1,2,0:T(8,128)(2,1)} %all-gather.5.cloned.1.call-done) | data formatting | bytes 15728640 | tf_op jit(solution)/shard_map/all_gather | solution.py:99
  328.6 19.6 %fusion.16 = (f32[160,8,12]{0,2,1:T(8,128)S(1)}, f32[8,12,640,160]{2,3,1,0:T(8,128)}) fusion(pred[160,8,640]{2,0,1:T(8,128)(4,1)} %broadcast_and_fusion, bf16[640,8,12,64]{0,3,2,1:T(8,128)(2,1)} %copy.84, bf16[160,8,12,32]{0,3,2,1:T(8,128)(2,1)} %get-tuple-element.25, bf16[160,8,12,32]{0,3,2,1:T(8,128)(2,1)} %get-tuple-element.24), kind=kOutput, calls=%fused_computation.19 | convolution fusion | flops 1291699200 | bytes 50032640 | tf_op jit(solution)/shard_map/qihd,kihd->qihk/dot_general | solution.py:55
  348.3 20.2 %fusion.3 = f32[160,8,12]{0,2,1:T(8,128)S(1)} fusion(f32[160,8,12]{0,2,1:T(8,128)S(1)} %broadcast_maximum_fusion, pred[160,8,640]{2,0,1:T(8,128)(4,1)S(1)} %copy-done.5, f32[8,12,640,160]{2,3,1,0:T(8,128)} %get-tuple-element.38), kind=kLoop, calls=%fused_computation.8 | loop fusion | flops 49136640 | bytes 40263680 | tf_op jit(solution)/shard_map/reduce_sum | solution.py:105
  368.5 208.8 %all-gather.3.cloned.1.call-done = bf16[640,8,12,64]{3,1,2,0:T(8,128)(2,1)} async-done(((bf16[160,8,12,64]{3,1,2,0:T(8,128)(2,1)}), bf16[640,8,12,64]{3,1,2,0:T(8,128)(2,1)}) %all-gather.3.cloned.1.call-update) | async-done | bytes 7864336 | tf_op jit(solution)/shard_map/all_gather | solution.py:100
  577.3 20.0 %copy.85 = bf16[640,8,12,64]{0,3,2,1:T(8,128)(2,1)} copy(bf16[640,8,12,64]{3,1,2,0:T(8,128)(2,1)} %all-gather.3.cloned.1.call-done) | data formatting | bytes 15728640 | tf_op jit(solution)/shard_map/all_gather | solution.py:100
  597.3 21.0 %fusion.21 = bf16[160,8,12,64]{0,3,2,1:T(8,128)(2,1)} fusion(f32[160,8,12]{0,2,1:T(8,128)S(1)} %fusion.3, bf16[640,8,12,64]{0,3,2,1:T(8,128)(2,1)} %copy.85, f32[160,8,12]{0,2,1:T(8,128)S(1)} %broadcast_maximum_fusion, pred[160,8,640]{2,0,1:T(8,128)(4,1)} %broadcast_and_fusion, f32[8,12,640,160]{2,3,1,0:T(8,128)} %get-tuple-element.38), kind=kOutput, calls=%fused_computation.31 | convolution fusion | flops 1309409280 | bytes 50094080 | tf_op jit(solution)/shard_map/qihk,kihd->qihd/dot_general | solution.py:106
  618.3 8.4 copy.86
  655.7 17.7 multiply_convert_fusion.1
  699.6 8.0 copy.88
  707.6 22.3 %fusion.18 = bf16[8,12,64,640]{3,2,1,0:T(8,128)(2,1)} fusion(bf16[160,8,12,64]{0,3,2,1:T(8,128)(2,1)} %copy.88, f32[160,8,12]{0,2,1:T(8,128)S(1)} %log_add_fusion, pred[160,8,640]{2,0,1:T(8,128)(4,1)} %broadcast_and_fusion, f32[8,12,640,160]{2,3,1,0:T(8,128)} %get-tuple-element.38), kind=kOutput, calls=%fused_computation.27 | convolution fusion | flops 1311375360 | bytes 50032640 | tf_op jit(solution)/shard_map/qihk,qihd->kihd/dot_general | solution.py:174
  730.0 32.5 %fusion = (f32[160,8,12]{0,2,1:T(8,128)S(1)}, f32[8,12,640,160]{2,3,1,0:T(8,128)}) fusion(f32[160,8,12]{0,2,1:T(8,128)S(1)} %log_add_fusion, pred[160,8,640]{2,0,1:T(8,128)(4,1)} %broadcast_and_fusion, f32[8,12,640,160]{2,3,1,0:T(8,128)} %get-tuple-element.38, bf16[640,8,12,64]{0,3,2,1:T(8,128)(2,1)} %copy.85, bf16[160,8,12,64]{0,3,2,1:T(8,128)(2,1)} %copy.88), kind=kOutput, calls=%fused_computation.2 | convolution fusion | flops 1317258240 | bytes 89415680 | tf_op jit(solution)/shard_map/qihd,kihd->qihk/dot_general | solution.py:158
  762.4 11.2 copy.93
  773.6 32.2 %fusion.2 = bf16[160,8,12,640]{3,0,2,1:T(8,128)(2,1)} fusion(f32[8,12,640,160]{2,3,1,0:T(8,128)} %get-tuple-element.43, f32[160,8,12]{0,2,1:T(8,128)S(1)} %get-tuple-element.42, f32[160,8,12]{0,2,1:T(8,128)S(1)} %log_add_fusion, pred[160,8,640]{2,0,1:T(8,128)(4,1)} %broadcast_and_fusion, f32[8,12,640,160]{2,3,1,0:T(8,128)} %get-tuple-element.38), kind=kLoop, calls=%fused_computation.4 | loop fusion | flops 68812800 | bytes 99246080 | tf_op jit(solution)/shard_map/convert_element_type | solution.py:162
  805.8 13.8 multiply_convert_fusion
  819.6 11.1 copy.92
  830.7 13.0 pad_maximum_fusion
  850.2 10.2 fusion.49
  860.5 10.2 fusion.82
  870.9 10.2 fusion.83
  881.1 223.7 %reduce-scatter.9.cloned.1.call-done = bf16[160,8,1536]{2,1,0:T(8,128)(2,1)} async-done(((bf16[640,8,1536]{2,1,0:T(8,128)(2,1)}), bf16[160,8,1536]{2,1,0:T(8,128)(2,1)}) %reduce-scatter.9.cloned.1.call-update) | async-done | bytes 3932176 | tf_op jit(solution)/shard_map/reduce_scatter | solution.py:177
  1110.5 14.7 multiply_bitcast_fusion
  1145.2 8.4 copy.95
  1171.4 8.4 copy.90
  1192.8 8.5 fusion.59
  1210.2 41.3 %all-reduce.2 = (f32[768]{0:T(1024)S(1)}, f32[768]{0:T(1024)S(1)}) all-reduce(f32[768]{0:T(1024)S(1)} %get-tuple-element.13, f32[768]{0:T(1024)S(1)} %copy-done.26), channel_id=3, replica_groups=mesh['items'=8,'band'=4] {'items','band'}, use_global_device_ids=true, to_apply=%region_9.10.clone | all-reduce | flops 1536 | bytes 12288
  1258.4 72.5 %reduce-scatter.23.cloned.1.call-done = f32[64,768]{1,0:T(8,128)} async-done(((f32[2048,768]{1,0:T(8,128)}), f32[64,768]{1,0:T(8,128)}) %reduce-scatter.23.cloned.1.call-update) | async-done | bytes 196624 | tf_op jit(solution)/shard_map/reduce_scatter | solution.py:223
  1330.9 119.6 %reduce-scatter.19.cloned.1.call-done = f32[24,2048]{1,0:T(8,128)} async-done(((f32[768,2048]{1,0:T(8,128)}), f32[24,2048]{1,0:T(8,128)}) %reduce-scatter.19.cloned.1.call-update) | async-done | bytes 196624 | tf_op jit(solution)/shard_map/reduce_scatter | solution.py:221
  1450.5 120.7 %reduce-scatter.21.cloned.1.call-done = f32[24,2048]{1,0:T(8,128)} async-done(((f32[768,2048]{1,0:T(8,128)}), f32[24,2048]{1,0:T(8,128)}) %reduce-scatter.21.cloned.1.call-update) | async-done | bytes 196624 | tf_op jit(solution)/shard_map/reduce_scatter | solution.py:222
  1571.3 104.2 %reduce-scatter.15.cloned.1.call-done = f32[24,768]{1,0:T(8,128)} async-done(((f32[768,768]{1,0:T(8,128)}), f32[24,768]{1,0:T(8,128)}) %reduce-scatter.15.cloned.1.call-update) | async-done | bytes 73744 | tf_op jit(solution)/shard_map/reduce_scatter | solution.py:218
  1675.4 104.8 %reduce-scatter.13.cloned.1.call-done = f32[24,768]{1,0:T(8,128)} async-done(((f32[768,768]{1,0:T(8,128)}), f32[24,768]{1,0:T(8,128)}) %reduce-scatter.13.cloned.1.call-update) | async-done | bytes 73744 | tf_op jit(solution)/shard_map/reduce_scatter | solution.py:217
  1780.2 103.8 %reduce-scatter.11.cloned.1.call-done = f32[24,768]{1,0:T(8,128)} async-done(((f32[768,768]{1,0:T(8,128)}), f32[24,768]{1,0:T(8,128)}) %reduce-scatter.11.cloned.1.call-update) | async-done | bytes 73744 | tf_op jit(solution)/shard_map/reduce_scatter | solution.py:216
  (140 shorter events, 184.1 us)
Async XLA Ops:
  7.2 648.5 %copy-start = (bf16[2048,768]{1,0:T(8,128)(2,1)S(1)}, bf16[2048,768]{1,0:T(8,128)(2,1)}, u32[]{:S(2)}) copy-start(bf16[2048,768]{1,0:T(8,128)(2,1)} %param.22) | copy-start | bytes 9437188
  7.2 7.1 copy-start.23
  7.2 300.7 %all-gather.5.cloned.1.call-start = ((), (), s32[]{:S(2)}) async-start(), calls=%async_computation.9 | async-start | bytes 19660800 | tf_op jit(solution)/shard_map/all_gather | solution.py:99
  9.5 26.1 %copy-start.16 = (f32[160,8]{1,0:T(8,128)}, f32[160,8]{1,0:T(8,128)S(1)}, u32[]{:S(2)}) copy-start(f32[160,8]{1,0:T(8,128)S(1)} %add_rsqrt_fusion) | copy-start | bytes 15364
  22.5 3.5 copy-start.18
  35.4 541.9 %all-gather.3.cloned.1.call-start = ((), (), s32[]{:S(2)}) async-start(), calls=%async_computation.8 | async-start | bytes 19660800 | tf_op jit(solution)/shard_map/all_gather | solution.py:100
  35.7 4.9 copy-start.21
  55.1 1049.7 %reduce-scatter.9.cloned.1.call-start = ((), (), s32[]{:S(2)}) async-start(), calls=%async_computation.10 | async-start | bytes 19660800 | tf_op jit(solution)/shard_map/reduce_scatter | solution.py:177
  328.6 19.6 %copy-start.5 = (pred[160,8,640]{2,0,1:T(8,128)(4,1)S(1)}, pred[160,8,640]{2,0,1:T(8,128)(4,1)}, u32[]{:S(2)}) copy-start(pred[160,8,640]{2,0,1:T(8,128)(4,1)} %broadcast_and_fusion) | copy-start | bytes 2457604
  634.6 4.4 copy-start.25
  639.0 10.0 copy-start.2
  642.3 6.7 copy-start.8
  642.3 6.7 copy-start.28
  648.9 6.7 copy-start.7
  673.3 7.5 copy-start.3
  673.3 7.5 copy-start.30
  673.3 7.5 copy-start.32
  843.8 414.6 %reduce-scatter.17.cloned.1.call-start = ((), (), s32[]{:S(2)}) async-start(), calls=%async_computation.14 | async-start | bytes 2433024 | tf_op jit(solution)/shard_map/reduce_scatter | solution.py:219
  849.8 481.2 %reduce-scatter.23.cloned.1.call-start = ((), (), s32[]{:S(2)}) async-start(), calls=%async_computation.17 | async-start | bytes 6488064 | tf_op jit(solution)/shard_map/reduce_scatter | solution.py:223
  860.4 590.1 %reduce-scatter.19.cloned.1.call-start = ((), (), s32[]{:S(2)}) async-start(), calls=%async_computation.15 | async-start | bytes 6488064 | tf_op jit(solution)/shard_map/reduce_scatter | solution.py:221
  870.6 700.6 %reduce-scatter.21.cloned.1.call-start = ((), (), s32[]{:S(2)}) async-start(), calls=%async_computation.16 | async-start | bytes 6488064 | tf_op jit(solution)/shard_map/reduce_scatter | solution.py:222
  881.0 223.8 %copy-start.17 = (f32[160,8]{1,0:T(8,128)S(1)}, f32[160,8]{1,0:T(8,128)}, u32[]{:S(2)}) copy-start(f32[160,8]{1,0:T(8,128)} %copy-done.16) | copy-start | bytes 15364
  881.0 223.8 %copy-start.24 = (f32[768]{0:T(1024)S(1)}, f32[768]{0:T(1024)}, u32[]{:S(2)}) copy-start(f32[768]{0:T(1024)} %param.14) | copy-start | bytes 9220
  881.0 794.4 %reduce-scatter.15.cloned.1.call-start = ((), (), s32[]{:S(2)}) async-start(), calls=%async_computation.13 | async-start | bytes 2433024 | tf_op jit(solution)/shard_map/reduce_scatter | solution.py:218
  1110.2 670.0 %reduce-scatter.13.cloned.1.call-start = ((), (), s32[]{:S(2)}) async-start(), calls=%async_computation.12 | async-start | bytes 2433024 | tf_op jit(solution)/shard_map/reduce_scatter | solution.py:217
  1128.9 6.7 copy-start.19
  1128.9 6.7 copy-start.20
  1161.2 5.8 copy-start.22
  1166.6 717.3 %reduce-scatter.11.cloned.1.call-start = ((), (), s32[]{:S(2)}) async-start(), calls=%async_computation.11 | async-start | bytes 2433024 | tf_op jit(solution)/shard_map/reduce_scatter | solution.py:216
  1192.7 8.6 copy-start.9
  1192.8 8.6 copy-start.12
  1206.2 4.0 copy-start.26
  (11 other events, 24.9 us)
Sparse Core Ops, SparseCore 0:
  35.5 272.3 all-gather.4
  309.4 267.8 all-gather.2
  843.9 260.7 reduce-scatter.8
  1110.5 100.0 reduce-scatter.16
  1217.6 113.3 reduce-scatter.22
  1337.0 113.4 reduce-scatter.18
  1457.7 113.5 reduce-scatter.20
  1577.1 98.2 reduce-scatter.14
  1682.2 97.9 reduce-scatter.12
  1785.9 98.0 reduce-scatter.10
where the time goes:
time: 1900 us; the launch traced here: 1890 us
  waiting for transfers between devices  1310 us (69%)
  matrix products  254 us (13%)
  local copies, waits for them, and re-layouts  171 us (9%)
  other arithmetic  99.6 us (5%)
  blocking collectives  41.3 us (2%)
    all_gather x1, waiting for transfers between devices, per_device(): key_piece = lax.all_gather(key_rows, 'band', axis=0, tiled=True)  251 us
    reduce_scatter x1, waiting for transfers between devices, per_device(): lax.psum_scatter(jnp.concatenate([key_grads.reshape(row_span, items_here,...  224 us
    all_gather x1, waiting for transfers between devices, per_device(): value_piece = lax.all_gather(values, 'band', axis=0, tiled=True)  209 us
    reduce_scatter x1, waiting for transfers between devices, per_device(): lax.psum_scatter(grad_w_up, ('items', 'band'), scatter_dimension=0, tiled...  121 us
    reduce_scatter x1, waiting for transfers between devices, per_device(): lax.psum_scatter(grad_w_gate, ('items', 'band'), scatter_dimension=0, til...  120 us
    reduce_scatter x1, waiting for transfers between devices, per_device(): lax.psum_scatter(grad_w_key, ('items', 'band'), scatter_dimension=0, tile...  105 us
    reduce_scatter x1, waiting for transfers between devices, per_device(): lax.psum_scatter(grad_w_value, ('items', 'band'), scatter_dimension=0, ti...  104 us
    reduce_scatter x1, waiting for transfers between devices, per_device(): lax.psum_scatter(grad_w_query, ('items', 'band'), scatter_dimension=0, ti...  104 us
  transfers between devices with their start and end apart: 10, of which 9 were waited for; matrix products, arithmetic and copies ran while one was open for 12% of the time, Pallas kernels for 0%

commit v1 on v0

v1 whole, which is shorter than its diff:
```python
import functools

import jax
import jax.numpy as jnp
from jax import lax
from jax.experimental import pallas as pl
from jax.experimental.pallas import tpu as pltpu
from jax.sharding import PartitionSpec as P

HEAD_DIM = 64
HALF = HEAD_DIM // 2
EPS = 1e-05
NEG = -1e30
ROPE_BASE = 10000.0
LOG2E = 1.4426950408889634
SCALE = HEAD_DIM**-0.5
BLOCK = 256
F32 = jnp.float32
LOW = jnp.bfloat16


def dot_nn(left, right):
    return lax.dot_general(left, right, (((1,), (0,)), ((), ())), preferred_element_type=F32)


def dot_nt(left, right):
    return lax.dot_general(left, right, (((1,), (1,)), ((), ())), preferred_element_type=F32)


def dot_tn(left, right):
    return lax.dot_general(left, right, (((0,), (0,)), ((), ())), preferred_element_type=F32)


def vmem(count):
    return [pl.BlockSpec(memory_space=pltpu.VMEM)] * count


def smem():
    return pl.BlockSpec(memory_space=pltpu.SMEM)


def params(mib):
    return pltpu.CompilerParams(vmem_limit_bytes=mib * 2**20)


def log2_of(number):
    return number.bit_length() - 1


def split_kernel(items, chunk, band_items_ref, rows_ref, *outs):
    size = items * chunk
    row = lax.broadcasted_iota(jnp.int32, (size, size), 0)
    col = lax.broadcasted_iota(jnp.int32, (size, size), 1)
    item = (row >> log2_of(chunk)) + band_items_ref[0]
    item = jnp.where(item >= items, item - items, item)
    order = jnp.where(col == (row & (chunk - 1)) * items + item, 1.0, 0.0).astype(LOW)
    for block in range(rows_ref.shape[0] // size):
        moved = dot_nn(order, rows_ref[block * size : (block + 1) * size, :]).astype(LOW)
        for at, out in enumerate(outs):
            out[block * chunk : (block + 1) * chunk, :] = moved[at * chunk : (at + 1) * chunk]


def split_items(array, band, bands):
    band_rows, items, width = array.shape
    chunk = 32 if band_rows % 32 == 0 else 16
    per = items // bands
    return pl.pallas_call(
        functools.partial(split_kernel, items, chunk),
        name="split_items",
        out_shape=[jax.ShapeDtypeStruct((band_rows, width), LOW)] * items,
        in_specs=[smem()] + vmem(1),
        out_specs=vmem(items),
        compiler_params=params(32),
    )(jnp.reshape(band * per, (1,)), array.reshape(band_rows * items, width))


def merge_kernel(items, per, chunk, band_ref, *refs):
    ins, out = refs[:-1], refs[-1]
    size, bands = items * chunk, items // per
    row = lax.broadcasted_iota(jnp.int32, (size, size), 0)
    col = lax.broadcasted_iota(jnp.int32, (size, size), 1)
    number = col >> log2_of(chunk)
    source = band_ref[0] - (number >> log2_of(per))
    source = jnp.where(source < 0, source + bands, source)
    item = source * per + (number & (per - 1))
    order = jnp.where(row == (col & (chunk - 1)) * items + item, 1.0, 0.0).astype(LOW)
    for block in range(out.shape[0] // size):
        parts = jnp.concatenate([part[block * chunk : (block + 1) * chunk, :] for part in ins], 0)
        out[block * size : (block + 1) * size, :] = dot_nn(order, parts).astype(LOW)


def merge_items(parts, band, bands):
    items = len(parts)
    band_rows, width = parts[0].shape
    chunk = 32 if band_rows % 32 == 0 else 16
    return pl.pallas_call(
        functools.partial(merge_kernel, items, items // bands, chunk),
        name="merge_items",
        out_shape=jax.ShapeDtypeStruct((band_rows * items, width), LOW),
        in_specs=[smem()] + vmem(items),
        out_specs=vmem(1)[0],
        compiler_params=params(32),
    )(jnp.reshape(band, (1,)), *parts).reshape(band_rows, items, width)


def band_start(band, shift, bands, band_rows):
    return pl.multiple_of(lax.rem(band + shift + bands, bands) * band_rows, band_rows)


def exchange(parts, bands, per, item):
    kept = [parts[item]]
    for shift in range(1, bands):
        kept.append(
            lax.ppermute(
                parts[shift * per + item], "band", [(i, (i + shift) % bands) for i in range(bands)]
            )
        )
    return kept


def rope(vector, cos, sin):
    parts = []
    for at in range(0, vector.shape[0], HEAD_DIM):
        lower, upper = vector[at : at + HALF], vector[at + HALF : at + HEAD_DIM]
        parts += [lower * cos - upper * sin, lower * sin + upper * cos]
    return jnp.concatenate(parts, 0)


def query_blocks(seq):
    return [(start, min(start + BLOCK, seq)) for start in range(0, seq, BLOCK)]


def limits(start, stop, length):
    position = start + lax.broadcasted_iota(jnp.int32, (1, stop - start), 1)
    return jnp.minimum(position, length - 1)


def score_parts(keys, queries, start, stop, length):
    parts = []
    if start:
        parts.append((0, BLOCK, dot_tn(keys[:, :BLOCK], queries)))
    first = min(start, BLOCK)
    late = dot_tn(keys[:, first:stop], queries)
    position = first + lax.broadcasted_iota(jnp.int32, late.shape, 0)
    late = jnp.where(position <= limits(start, stop, length), late, NEG)
    parts.append((first, stop, late))
    return parts


def norm_rows(inputs):
    return lax.rsqrt(jnp.mean(inputs * inputs, -1, keepdims=True) + EPS)


def attend_kernel(bands, scalars, *refs):
    chunks, refs = refs[:bands], refs[bands:]
    weights, gain, cos, sin, x, query, key, value, attended_t, attended, log_total, normed = refs
    seq, width = x.shape
    band_rows = seq // bands
    band, length = scalars[0], scalars[1]
    for shift, chunk in enumerate(chunks):
        x[pl.ds(band_start(band, -shift, bands, band_rows), band_rows), :] = chunk[...]
    tile = 128
    for at in range(0, seq, tile):
        inputs = x[at : at + tile, :].astype(F32)
        normed[at : at + tile, :] = (inputs * norm_rows(inputs) * gain[...]).astype(LOW)

    project = 256

    def project_tile(at, _):
        rows = pl.ds(pl.multiple_of(at * project, project), project)
        for part, out, scaled in ((0, query, SCALE * LOG2E), (1, key, 1.0)):
            source = pl.ds(pl.multiple_of(part * width + at * project, project), project)
            out[rows, :] = (rope(dot_nt(weights[source, :], normed[...]), cos[...], sin[...]) * scaled).astype(LOW)
        source = pl.ds(pl.multiple_of(2 * width + at * project, project), project)
        value[rows, :] = dot_nt(weights[source, :], normed[...]).astype(LOW)
        return 0

    lax.fori_loop(0, width // project, project_tile, 0)

    def head(at, _):
        for which in range(2):
            number = at * 2 + which
            rows = pl.ds(pl.multiple_of(number * HEAD_DIM, HEAD_DIM), HEAD_DIM)
            keys, values = key[rows, :], value[rows, :]
            for start, stop in query_blocks(seq):
                parts = score_parts(keys, query[rows, start:stop], start, stop, length)
                top = functools.reduce(jnp.maximum, [jnp.max(s, 0, keepdims=True) for _, _, s in parts])
                total = jnp.zeros_like(top)
                acc = jnp.zeros((HEAD_DIM, stop - start), F32)
                for first, last, scores in parts:
                    prob = jnp.exp2(scores - top)
                    total += jnp.sum(prob, 0, keepdims=True)
                    acc += dot_nn(values[:, first:last], prob.astype(LOW))
                attended_t[rows, start:stop] = (acc / total).astype(LOW)
                log_total[number, :, start:stop] = top + jnp.log2(total)
        return 0

    lax.fori_loop(0, width // HEAD_DIM // 2, head, 0)
    for at in range(0, width, project):
        attended[:, at : at + project] = attended_t[at : at + project, :].T


def attend(chunks, scalars, weights_t, gain, cos, sin):
    bands = len(chunks)
    band_rows, width = chunks[0].shape
    seq = bands * band_rows
    low_t = jax.ShapeDtypeStruct((width, seq), LOW)
    low = jax.ShapeDtypeStruct((seq, width), LOW)
    pairs = seq * seq * width
    return pl.pallas_call(
        functools.partial(attend_kernel, bands),
        name="attend",
        out_shape=[low, low_t, low_t, low_t, low_t, low, jax.ShapeDtypeStruct((width // HEAD_DIM, 1, seq), F32)],
        in_specs=[smem()] + vmem(bands + 4),
        out_specs=vmem(7),
        scratch_shapes=[pltpu.VMEM((seq, width), LOW)],
        compiler_params=params(48),
        cost_estimate=pl.CostEstimate(
            flops=6 * seq * width * width + 12 * pairs, bytes_accessed=20 * seq * width, transcendentals=0
        ),
    )(scalars, *chunks, weights_t, gain, cos, sin)


def feed_kernel(bands, follows, scalars, *refs):
    chunks, refs = refs[:bands], refs[bands:]
    x, attended, attended_t, w_out, gain, w_gate, w_up, w_down = refs[:8]
    refs = refs[8:]
    prev = None
    if follows:
        prev, refs = refs[:5], refs[5:]
    outs, refs = refs[:bands], refs[bands:]
    grad_resid_low, grad_attended_t, g_gate, g_up, g_down, g_out, g_norm = refs[:7]
    cot, resid, normed, normed_t, out_acc, back_acc = refs[7:]
    seq, width = x.shape
    band_rows = seq // bands
    band = scalars[0]
    step = pl.program_id(0)
    tile = 128

    @pl.when(step == 0)
    def _():
        for shift, chunk in enumerate(chunks):
            cot[pl.ds(band_start(band, -shift, bands, band_rows), band_rows), :] = chunk[...]
        for at in range(0, seq, tile):
            rows = slice(at, at + tile)
            total = x[rows, :].astype(F32) + dot_nn(attended[rows, :], w_out[...])
            resid[rows, :] = total
            out_acc[rows, :] = total
            low = (total * norm_rows(total) * gain[...]).astype(LOW)
            normed[rows, :] = low
            normed_t[:, rows] = low.T
        back_acc[...] = jnp.zeros_like(back_acc)

    gate = dot_nn(normed[...], w_gate[...])
    upward = dot_nn(normed[...], w_up[...])
    grad_hidden = dot_nt(cot[...], w_down[...])
    sig = 0.5 * jnp.tanh(0.5 * gate) + 0.5
    silu = gate * sig
    hidden = (silu * upward).astype(LOW)
    grad_gate = (grad_hidden * upward * (sig + silu * (1.0 - sig))).astype(LOW)
    grad_upward = (grad_hidden * silu).astype(LOW)
    out_acc[...] += dot_nn(hidden, w_down[...])
    back_acc[...] += dot_nt(grad_gate, w_gate[...]) + dot_nt(grad_upward, w_up[...])

    def put(out, at, grad):
        if follows:
            grad += prev[at][...].astype(F32)
        out[...] = grad.astype(LOW)

    put(g_down, 2, dot_nn(hidden.T, cot[...]))
    put(g_gate, 0, dot_nn(normed_t[...], grad_gate))
    put(g_up, 1, dot_nn(normed_t[...], grad_upward))

    @pl.when(step == pl.num_programs(0) - 1)
    def _():
        norm_sum = jnp.zeros((1, width), F32)
        for at in range(0, seq, tile):
            rows = slice(at, at + tile)
            total, incoming = resid[rows, :], back_acc[rows, :]
            inv = norm_rows(total)
            scaled = total * inv
            norm_sum += jnp.sum(incoming * scaled, 0, keepdims=True)
            weighted = incoming * gain[...]
            grad = cot[rows, :].astype(F32) + inv * (
                weighted - scaled * jnp.mean(weighted * scaled, -1, keepdims=True)
            )
            grad_resid_low[rows, :] = grad.astype(LOW)
        if follows:
            norm_sum += prev[4][...]
        g_norm[...] = norm_sum
        grad_attended_t[...] = dot_nt(w_out[...], grad_resid_low[...]).astype(LOW)
        put(g_out, 3, dot_nn(attended_t[...], grad_resid_low[...]))
        for shift, out in enumerate(outs):
            out[...] = out_acc[pl.ds(band_start(band, shift, bands, band_rows), band_rows), :].astype(LOW)


def feed(chunks, scalars, x, attended, attended_t, w_out, gain, w_gate, w_up, w_down, prev):
    bands = len(chunks)
    seq, width = x.shape
    ff = w_gate.shape[1]
    wide = 512
    whole = lambda *shape: pl.BlockSpec(shape, lambda i: (0,) * len(shape))
    columns = pl.BlockSpec((width, wide), lambda i: (0, i))
    rows = pl.BlockSpec((wide, width), lambda i: (i, 0))
    grad_specs = [columns, columns, rows, whole(width, width), whole(1, width)]
    band_rows = seq // bands
    return pl.pallas_call(
        functools.partial(feed_kernel, bands, prev is not None),
        name="feed",
        grid=(ff // wide,),
        out_shape=[jax.ShapeDtypeStruct((band_rows, width), LOW)] * bands
        + [
            jax.ShapeDtypeStruct((seq, width), LOW),
            jax.ShapeDtypeStruct((width, seq), LOW),
            jax.ShapeDtypeStruct((width, ff), LOW),
            jax.ShapeDtypeStruct((width, ff), LOW),
            jax.ShapeDtypeStruct((ff, width), LOW),
            jax.ShapeDtypeStruct((width, width), LOW),
            jax.ShapeDtypeStruct((1, width), F32),
        ],
        in_specs=[smem()]
        + [whole(band_rows, width)] * bands
        + [whole(seq, width), whole(seq, width), whole(width, seq), whole(width, width), whole(1, width)]
        + [columns, columns, rows]
        + (grad_specs if prev is not None else []),
        out_specs=[whole(band_rows, width)] * bands + [whole(seq, width), whole(width, seq)] + grad_specs,
        scratch_shapes=[
            pltpu.VMEM((seq, width), LOW),
            pltpu.VMEM((seq, width), F32),
            pltpu.VMEM((seq, width), LOW),
            pltpu.VMEM((width, seq), LOW),
            pltpu.VMEM((seq, width), F32),
            pltpu.VMEM((seq, width), F32),
        ],
        compiler_params=params(60),
        cost_estimate=pl.CostEstimate(
            flops=18 * seq * width * ff + 6 * seq * width * width, bytes_accessed=12 * width * ff, transcendentals=0
        ),
    )(scalars, *chunks, x, attended, attended_t, w_out, gain, w_gate, w_up, w_down, *(prev or ()))


def back_kernel(bands, follows, scalars, *refs):
    x, grad_resid, grad_attended, attended, query, key, value, log_total, w_query, w_key, w_value = refs[:11]
    gain, cos, sin = refs[11:14]
    refs = refs[14:]
    prev = None
    if follows:
        prev, refs = refs[:2], refs[2:]
    outs, refs = refs[:bands], refs[bands:]
    g_weights, g_norm, grads, normed_t, back = refs
    seq, width = x.shape
    band_rows = seq // bands
    band, length = scalars[0], scalars[1]
    blocks = query_blocks(seq)

    def head(at, _):
        for which in range(2):
            number = at * 2 + which
            rows = pl.ds(pl.multiple_of(number * HEAD_DIM, HEAD_DIM), HEAD_DIM)
            keys, values = key[rows, :], value[rows, :]
            delta_all = jnp.sum(grad_attended[rows, :].astype(F32) * attended[rows, :].astype(F32), 0, keepdims=True)
            key_grads = [0.0] * len(blocks)
            value_grads = [0.0] * len(blocks)
            for start, stop in blocks:
                queries, incoming = query[rows, start:stop], grad_attended[rows, start:stop]
                total = log_total[number, :, start:stop]
                delta = delta_all[:, start:stop]
                query_grad = 0.0
                for first, last, scores in score_parts(keys, queries, start, stop, length):
                    prob = jnp.exp2(scores - total)
                    grad_prob = dot_tn(values[:, first:last], incoming)
                    grad_score = (prob * (grad_prob - delta)).astype(LOW)
                    query_grad += dot_nn(keys[:, first:last], grad_score)
                    key_grad = dot_nt(queries, grad_score)
                    value_grad = dot_nt(incoming, prob.astype(LOW))
                    for piece, (low, high) in enumerate(blocks):
                        if first <= low and high <= last:
                            key_grads[piece] += key_grad[:, low - first : high - first]
                            value_grads[piece] += value_grad[:, low - first : high - first]
                grads[rows, start:stop] = (
                    rope(query_grad, cos[:, start:stop], -sin[:, start:stop]) * SCALE
                ).astype(LOW)
            for (start, stop), key_grad, value_grad in zip(blocks, key_grads, value_grads):
                at_key = pl.ds(pl.multiple_of(width + number * HEAD_DIM, HEAD_DIM), HEAD_DIM)
                at_value = pl.ds(pl.multiple_of(2 * width + number * HEAD_DIM, HEAD_DIM), HEAD_DIM)
                grads[at_key, start:stop] = (
                    rope(key_grad, cos[:, start:stop], -sin[:, start:stop]) * (1.0 / LOG2E)
                ).astype(LOW)
                grads[at_value, start:stop] = value_grad.astype(LOW)
        return 0

    lax.fori_loop(0, width // HEAD_DIM // 2, head, 0)

    tile = 128
    for at in range(0, seq, tile):
        inputs = x[at : at + tile, :].astype(F32)
        normed_t[:, at : at + tile] = (inputs * norm_rows(inputs) * gain[...]).astype(LOW).T
    project = 256
    for at in range(0, width, project):
        rows = slice(at, at + project)
        total = dot_nn(w_query[rows, :], grads[:width, :])
        total += dot_nn(w_key[rows, :], grads[width : 2 * width, :])
        total += dot_nn(w_value[rows, :], grads[2 * width :, :])
        back[:, rows] = total.T
        for part in range(3):
            grad = dot_nt(normed_t[rows, :], grads[part * width : (part + 1) * width, :])
            columns = slice(part * width, (part + 1) * width)
            if follows:
                grad += prev[0][rows, columns].astype(F32)
            g_weights[rows, columns] = grad.astype(LOW)
    norm_sum = jnp.zeros((1, width), F32)
    for at in range(0, seq, tile):
        rows = slice(at, at + tile)
        inputs, incoming = x[rows, :].astype(F32), back[rows, :]
        inv = norm_rows(inputs)
        scaled = inputs * inv
        norm_sum += jnp.sum(incoming * scaled, 0, keepdims=True)
        weighted = incoming * gain[...]
        back[rows, :] = grad_resid[rows, :].astype(F32) + inv * (
            weighted - scaled * jnp.mean(weighted * scaled, -1, keepdims=True)
        )
    if follows:
        norm_sum += prev[1][...]
    g_norm[...] = norm_sum
    for shift, out in enumerate(outs):
        out[...] = back[pl.ds(band_start(band, shift, bands, band_rows), band_rows), :].astype(LOW)


def back_attend(bands, scalars, x, grad_resid, grad_attended_t, attended_t, query, key, value, log_total, weights, gain, cos, sin, prev):
    seq, width = x.shape
    band_rows = seq // bands
    pairs = seq * seq * width
    args = [x, grad_resid, grad_attended_t, attended_t, query, key, value, log_total, *weights, gain, cos, sin, *(prev or ())]
    return pl.pallas_call(
        functools.partial(back_kernel, bands, prev is not None),
        name="back_attend",
        out_shape=[jax.ShapeDtypeStruct((band_rows, width), LOW)] * bands
        + [jax.ShapeDtypeStruct((width, 3 * width), LOW), jax.ShapeDtypeStruct((1, width), F32)],
        in_specs=[smem()] + vmem(len(args)),
        out_specs=vmem(bands + 2),
        scratch_shapes=[
            pltpu.VMEM((3 * width, seq), LOW),
            pltpu.VMEM((width, seq), LOW),
            pltpu.VMEM((seq, width), F32),
        ],
        compiler_params=params(48),
        cost_estimate=pl.CostEstimate(
            flops=12 * seq * width * width + 30 * pairs, bytes_accessed=24 * seq * width, transcendentals=0
        ),
    )(scalars, *args)


def rope_tables(seq):
    frequency = jnp.exp(-jnp.log(ROPE_BASE) * (2.0 * jnp.arange(HALF, dtype=F32) / HEAD_DIM))
    angles = frequency[:, None] * jnp.arange(seq, dtype=jnp.int32).astype(F32)[None, :]
    return jnp.cos(angles), jnp.sin(angles)


def per_device(
    bands,
    tokens,
    lengths,
    norm_attn,
    w_query,
    w_key,
    w_value,
    w_out,
    norm_ffn,
    w_gate,
    w_up,
    w_down,
    cotangent,
):
    band_rows, items, width = tokens.shape
    per = items // bands
    seq = bands * band_rows
    band = lax.axis_index("band")
    token_parts = split_items(tokens, band, bands)
    x_chunks = [exchange(token_parts, bands, per, item) for item in range(per)]
    cot_parts = split_items(cotangent, band, bands)
    cot_chunks = [exchange(cot_parts, bands, per, item) for item in range(per)]
    cos, sin = rope_tables(seq)
    gain_attn, gain_ffn = norm_attn.reshape(1, width), norm_ffn.reshape(1, width)
    weights_t = jnp.concatenate([w_query.T, w_key.T, w_value.T], 0)
    scalars = [
        jnp.stack([band, lax.dynamic_index_in_dim(lengths, band * per + item, keepdims=False)]).astype(jnp.int32)
        for item in range(per)
    ]
    fronts = [attend(x_chunks[i], scalars[i], weights_t, gain_attn, cos, sin) for i in range(per)]
    feeds, prev = [], None
    for i in range(per):
        x, _, _, _, attended_t, attended, _ = fronts[i]
        feeds.append(
            feed(cot_chunks[i], scalars[i], x, attended, attended_t, w_out, gain_ffn, w_gate, w_up, w_down, prev)
        )
        prev = feeds[-1][bands + 2 :]
    out_parts = [f[:bands] for f in feeds]
    g_gate, g_up, g_down, g_out, g_norm_ffn = prev
    backs, prev = [], None
    for i in range(per):
        x, query, key, value, attended_t, _, log_total = fronts[i]
        grad_resid, grad_attended_t = feeds[i][bands : bands + 2]
        backs.append(
            back_attend(
                bands, scalars[i], x, grad_resid, grad_attended_t, attended_t, query, key, value, log_total,
                (w_query, w_key, w_value), gain_attn, cos, sin, prev,
            )
        )
        prev = backs[-1][bands:]
    g_weights, g_norm_attn = prev

    def home(parts):
        came = [exchange([parts[i][k] for k in range(bands)], bands, 1, 0) for i in range(per)]
        return merge_items([came[j][k] for k in range(bands) for j in range(per)], band, bands)

    output = home(out_parts)
    grad_tokens = home([b[:bands] for b in backs])
    axes = ("items", "band")
    gains = jnp.concatenate([g_norm_attn.T, g_norm_ffn.T], 1)
    feed_sum = lax.psum_scatter(jnp.concatenate([g_gate, g_up], 1), axes, scatter_dimension=0, tiled=True).astype(F32)
    down_sum = lax.psum_scatter(g_down, axes, scatter_dimension=0, tiled=True).astype(F32)
    rest = jnp.concatenate([g_weights, g_out, gains.astype(LOW)], 1)
    rest_sum = lax.psum_scatter(rest, axes, scatter_dimension=0, tiled=True).astype(F32)
    ff = w_gate.shape[1]
    return (
        output,
        grad_tokens,
        rest_sum[:, 4 * width],
        rest_sum[:, :width],
        rest_sum[:, width : 2 * width],
        rest_sum[:, 2 * width : 3 * width],
        rest_sum[:, 3 * width : 4 * width],
        rest_sum[:, 4 * width + 1],
        feed_sum[:, :ff],
        feed_sum[:, ff:],
        down_sum,
    )


def solution(mesh):
    split = P("band", "items", None)
    rows = P(("items", "band"), None)
    flat = P(("items", "band"))
    return jax.shard_map(
        functools.partial(per_device, mesh.shape["band"]),
        mesh=mesh,
        in_specs=(split, P("items")) + (P(),) * 9 + (split,),
        out_specs=(split, split, flat, rows, rows, rows, rows, flat, rows, rows, rows),
        check_vma=False,
    )
```

time: 1900 us -> 535 us (0.28)
  waiting for transfers between devices: 1310 us -> 207 us
  matrix products: 254 us -> 0 us
  Pallas kernels: 0 us -> 155 us
  local copies, waits for them, and re-layouts: 171 us -> 40.7 us
  starting transfers between devices: 1.63 us -> 98.3 us
  other arithmetic: 99.6 us -> 14.3 us
  blocking collectives: 41.3 us -> 0 us
    reduce_scatter x8 -> x2, waiting for transfers between devices: 849 us -> 117 us  [the longest x1 117 us: per_device(): lax.psum_scatter(jnp.concatenate([g_gate, g_up], 1), axes, scatter_dimens...]
    all_gather x2 -> x0, waiting for transfers between devices: 459 us -> none  [the longest x1 251 us: per_device(): key_piece = lax.all_gather(key_rows, 'band', axis=0, tiled=True)]
    dot_general x27 -> x0, matrix products: 254 us -> none  [the longest x7 36.4 us: product(): return jnp.dot(left, right, preferred_element_type=jnp.float32)]
    pallas_call x0 -> x10, Pallas kernels: none -> 155 us  [the longest x2 63.7 us: feed(): pl.pallas_call(functools.partial(feed_kernel, bands, prev is not None), n...]
    ppermute x0 -> x24, starting transfers between devices: none -> 98 us  [exchange(): lax.ppermute(parts[shift * per + item], 'band', [(i, (i + shift) % bands)...]
    unnamed x10 -> x4, waiting for transfers between devices: 0.16 us -> 63.5 us
    reshape x7 -> x2, local copies, waits for them, and re-layouts: 59.8 us -> 0.58 us  [the longest x1 0.58 us: per_device(): norm_ffn.reshape(1, width)]
    unnamed x1 -> x0, blocking collectives: 41.3 us -> none
  transfers between devices with their start and end apart: 10 -> 27, of which waited for: 9 -> 6; matrix products, arithmetic and copies ran while one was open for 12% -> 6% of each run, Pallas kernels for 0% -> 23%
where the time goes in v1:
time: 535 us; the launch traced here: 529 us
  waiting for transfers between devices  207 us (39%)
  Pallas kernels  155 us (29%)
  starting transfers between devices  98.3 us (18%)
  local copies, waits for them, and re-layouts  40.7 us (8%)
  between operations  14.5 us (3%)
  other arithmetic  14.3 us (3%)
    reduce_scatter x1, waiting for transfers between devices, per_device(): lax.psum_scatter(jnp.concatenate([g_gate, g_up], 1), axes, scatter_dimens...  117 us
    ppermute x24, starting transfers between devices, exchange(): lax.ppermute(parts[shift * per + item], 'band', [(i, (i + shift) % bands)...  98 us
    pallas_call x2, Pallas kernels, feed(): pl.pallas_call(functools.partial(feed_kernel, bands, prev is not None), n...  63.7 us
    unnamed x4, waiting for transfers between devices  63.5 us
    pallas_call x2, Pallas kernels, back_attend(): pl.pallas_call(functools.partial(back_kernel, bands, prev is not None), n...  49.6 us
    pallas_call x2, Pallas kernels, attend(): pl.pallas_call(functools.partial(attend_kernel, bands), name='attend', ou...  35.3 us
    unnamed x87, local copies, waits for them, and re-layouts  26.9 us
    ppermute x24, waiting for transfers between devices, exchange(): lax.ppermute(parts[shift * per + item], 'band', [(i, (i + shift) % bands)...  25.9 us
  transfers between devices with their start and end apart: 27, of which 6 were waited for; matrix products, arithmetic and copies ran while one was open for 6% of the time, Pallas kernels for 23%

profile of v1, /device:TPU:0, one launch (start us, length us, event | category | flops | bytes accessed | tf_op | source)
XLA Modules:
  0.0 528.8 jit_solution(11608015342170207190)
XLA Ops:
  10.1 3.0 collective-permute-start.3
  13.1 2.6 collective-permute-start.4
  18.1 2.4 copy.31
  20.5 2.4 copy.32
  22.9 2.4 copy.33
  26.6 3.6 pad_maximum_fusion.1.refs_4_
  34.0 3.4 collective-permute-start
  37.4 7.8 %collective-permute-start.2 = (bf16[160,768]{1,0:T(8,128)(2,1)S(1)}, bf16[160,768]{1,0:T(8,128)(2,1)S(1)}, u32[]{:S(2)}, u32[]{:S(2)}) collective-permute-start(bf16[160,768]{1,0:T(8,128)(2,1)S(1)} %get-tuple-element.78), channel_id=1, source_target_pairs={{0,3},{1,0},{2,1},{3,2},{4,7},{5,4},{6,5},{7,6},{8,11},{9,8},{10,9... | collective-permute-start | bytes 737288 | tf_op jit(solution)/shard_map/ppermute | solution.py:114
  45.2 17.6 %attend.2 = (bf16[640,768]{1,0:T(8,128)(2,1)S(1)}, bf16[768,640]{1,0:T(8,128)(2,1)S(1)}, bf16[768,640]{1,0:T(8,128)(2,1)S(1)}, bf16[768,640]{1,0:T(8,128)(2,1)S(...) custom-call(s32[2]{0:T(128)S(1)} %pad_add_fusion.scalars, ...), custom_call_target="tpu_custom_call" | custom-call | flops 6039797760 | bytes 9830400 | tf_op jit(solution)/shard_map/attend/pallas_call | solution.py:210
  67.7 14.1 %collective-permute-start.11 = (bf16[160,768]{1,0:T(8,128)(2,1)S(1)}, bf16[160,768]{1,0:T(8,128)(2,1)S(1)}, u32[]{:S(2)}, u32[]{:S(2)}) collective-permute-start(bf16[160,768]{1,0:T(8,128)(2,1)S(1)} %get-tuple-element.94), channel_id=1, source_target_pairs={{0,3},{1,0},{2,1},{3,2},{4,7},{5,4},{6,5},{7,6},{8,11},{9,8},{10,9... | collective-permute-start | bytes 737288 | tf_op jit(solution)/shard_map/ppermute | solution.py:114
  82.3 3.0 collective-permute-start.7
  85.3 31.2 %feed.2 = (bf16[160,768]{1,0:T(8,128)(2,1)}, bf16[160,768]{1,0:T(8,128)(2,1)}, bf16[160,768]{1,0:T(8,128)(2,1)}, bf16[160,768]{1,0:T(8,128)(2,1)}, bf16[640,768]...) custom-call(s32[2]{0:T(128)} %copy-done.8, ...), custom_call_target="tpu_custom_call" | custom-call | flops 20384317440 | bytes 18874368 | tf_op jit(solution)/shard_map/feed/pallas_call | solution.py:307
  118.2 17.7 %attend.3 = (bf16[640,768]{1,0:T(8,128)(2,1)S(1)}, bf16[768,640]{1,0:T(8,128)(2,1)S(1)}, bf16[768,640]{1,0:T(8,128)(2,1)S(1)}, bf16[768,640]{1,0:T(8,128)(2,1)S(...) custom-call(s32[2]{0:T(128)S(1)} %pad_add_fusion.1.scalars, ...), custom_call_target="tpu_custom_call" | custom-call | flops 6039797760 | bytes 9830400 | tf_op jit(solution)/shard_map/attend/pallas_call | solution.py:210
  141.4 32.5 %feed.3 = (bf16[160,768]{1,0:T(8,128)(2,1)}, bf16[160,768]{1,0:T(8,128)(2,1)}, bf16[160,768]{1,0:T(8,128)(2,1)}, bf16[160,768]{1,0:T(8,128)(2,1)}, bf16[640,768]...) custom-call(s32[2]{0:T(128)} %copy-done.6, ...), custom_call_target="tpu_custom_call" | custom-call | flops 20384317440 | bytes 18874368 | tf_op jit(solution)/shard_map/feed/pallas_call | solution.py:307
  180.1 24.2 %back_attend.2 = (bf16[160,768]{1,0:T(8,128)(2,1)S(1)}, bf16[160,768]{1,0:T(8,128)(2,1)S(1)}, bf16[160,768]{1,0:T(8,128)(2,1)S(1)}, bf16[160,768]{1,0:T(8,128)(2...) custom-call(s32[2]{0:T(128)S(1)} %copy-done.9, bf16[640,768]{1,0:T(8,128)(2,1)S(1)} %copy-done.11, ...), custom_call_target="tpu_custom_call" | custom-call | flops 13967032320 | bytes 11796480 | tf_op jit(solution)/shard_map/back_attend/pallas_call | solution.py:434
  204.3 25.4 %back_attend.3 = (bf16[160,768]{1,0:T(8,128)(2,1)S(1)}, bf16[160,768]{1,0:T(8,128)(2,1)S(1)}, bf16[160,768]{1,0:T(8,128)(2,1)S(1)}, bf16[160,768]{1,0:T(8,128)(2...) custom-call(s32[2]{0:T(128)S(1)} %copy-done.7, bf16[640,768]{1,0:T(8,128)(2,1)S(1)} %copy-done.19, ...), custom_call_target="tpu_custom_call" | custom-call | flops 13967032320 | bytes 11796480 | tf_op jit(solution)/shard_map/back_attend/pallas_call | solution.py:434
  230.6 7.7 %concatenate.13 = bf16[768,3074]{1,0:T(8,128)(2,1)} concatenate(bf16[768,2304]{1,0:T(8,128)(2,1)} %get-tuple-element.132, bf16[768,768]{1,0:T(8,128)(2,1)S(1)} %copy-done.30, bf16[768,1]{1,0:T(8,128)(2,1)} %copy.34, bf16[768,1]{1,0:T(8,128)(2,1)S(1)} %copy.35), dimensions={1} | concatenate | bytes 9443328 | tf_op jit(solution)/shard_map/concatenate | solution.py:522
  238.3 6.3 %pad_maximum_fusion = bf16[768,4096]{1,0:T(8,128)(2,1)} fusion(bf16[768,2048]{1,0:T(8,128)(2,1)} %get-tuple-element.137, bf16[768,2048]{1,0:T(8,128)(2,1)} %get-tuple-element.136), kind=kLoop, calls=%fused_computation | loop fusion | flops 12582912 | bytes 12582912 | tf_op jit(solution)/shard_map/concatenate | solution.py:520
  247.1 2.8 collective-permute-start.16
  250.0 2.0 collective-permute-start.13
  252.0 6.9 %collective-permute-done.12.refs_2_ = bf16[160,768]{1,0:T(8,128)(2,1)S(1)} collective-permute-done((bf16[160,768]{1,0:T(8,128)(2,1)S(1)}, bf16[160,768]{1,0:T(8,128)(2,1)S(1)}, u32[]{:S(2)}, u32[]{:S(2)}) %collective-permute-start.12) | collective-permute-done | bytes 245792 | tf_op jit(solution)/shard_map/ppermute | solution.py:114
  258.9 10.0 %collective-permute-start.15 = (bf16[160,768]{1,0:T(8,128)(2,1)}, bf16[160,768]{1,0:T(8,128)(2,1)S(1)}, u32[]{:S(2)}, u32[]{:S(2)}) collective-permute-start(bf16[160,768]{1,0:T(8,128)(2,1)} %get-tuple-element.107), channel_id=1, source_target_pairs={{0,2},{1,3},{2,0},{3,1},{4,6},{5,7},{6,4},{7,5},{8,10},{9,11},{10,... | collective-permute-start | bytes 737288 | tf_op jit(solution)/shard_map/ppermute | solution.py:114
  268.9 5.1 collective-permute-done.14.refs_4_
  275.9 14.4 %collective-permute-start.20 = (bf16[160,768]{1,0:T(8,128)(2,1)S(1)}, bf16[160,768]{1,0:T(8,128)(2,1)S(1)}, u32[]{:S(2)}, u32[]{:S(2)}) collective-permute-start(bf16[160,768]{1,0:T(8,128)(2,1)S(1)} %get-tuple-element.128), channel_id=1, source_target_pairs={{0,2},{1,3},{2,0},{3,1},{4,6},{5,7},{6,4},{7,5},{8,10},{9,11},{10,... | collective-permute-start | bytes 737288 | tf_op jit(solution)/shard_map/ppermute | solution.py:114
  290.3 3.4 collective-permute-start.22
  293.7 15.1 %collective-permute-start.19 = (bf16[160,768]{1,0:T(8,128)(2,1)S(1)}, bf16[160,768]{1,0:T(8,128)(2,1)S(1)}, u32[]{:S(2)}, u32[]{:S(2)}) collective-permute-start(bf16[160,768]{1,0:T(8,128)(2,1)S(1)} %get-tuple-element.127), channel_id=1, source_target_pairs={{0,1},{1,2},{2,3},{3,0},{4,5},{5,6},{6,7},{7,4},{8,9},{9,10},{10,1... | collective-permute-start | bytes 737288 | tf_op jit(solution)/shard_map/ppermute | solution.py:114
  310.6 6.5 %collective-permute-start.23 = (bf16[160,768]{1,0:T(8,128)(2,1)S(1)}, bf16[160,768]{1,0:T(8,128)(2,1)S(1)}, u32[]{:S(2)}, u32[]{:S(2)}) collective-permute-start(bf16[160,768]{1,0:T(8,128)(2,1)S(1)} %get-tuple-element.131), channel_id=1, source_target_pairs={{0,3},{1,0},{2,1},{3,2},{4,7},{5,4},{6,5},{7,6},{8,11},{9,8},{10,9... | collective-permute-start | bytes 737288 | tf_op jit(solution)/shard_map/ppermute | solution.py:114
  317.1 2.0 merge_items.2
  319.1 3.3 collective-permute-done.20.refs_4_
  322.4 10.5 %collective-permute-done.21.refs_5_ = bf16[160,768]{1,0:T(8,128)(2,1)S(1)} collective-permute-done((bf16[160,768]{1,0:T(8,128)(2,1)S(1)}, bf16[160,768]{1,0:T(8,128)(2,1)S(1)}, u32[]{:S(2)}, u32[]{:S(2)}) %collective-permute-start.21) | collective-permute-done | bytes 245792 | tf_op jit(solution)/shard_map/ppermute | solution.py:114
  336.5 63.5 %reduce-scatter.10.cloned.1.call-done = bf16[24,3074]{1,0:T(8,128)(2,1)} async-done(((bf16[768,3074]{1,0:T(8,128)(2,1)}), bf16[24,3074]{1,0:T(8,128)(2,1)}) %reduce-scatter.10.cloned.1.call-update) | async-done | bytes 147568
  403.1 117.0 %reduce-scatter.6.cloned.1.call-done = bf16[24,4096]{1,0:T(8,128)(2,1)} async-done(((bf16[768,4096]{1,0:T(8,128)(2,1)}), bf16[24,4096]{1,0:T(8,128)(2,1)}) %reduce-scatter.6.cloned.1.call-update) | async-done | bytes 196624 | tf_op jit(solution)/shard_map/reduce_scatter | solution.py:520
  (142 shorter events, 44.5 us)
Async XLA Ops:
  7.2 327.7 %reduce-scatter.8.cloned.1.call-start = ((), (), s32[]{:S(2)}) async-start(), calls=%async_computation.4 | async-start | bytes 3244032 | tf_op jit(solution)/shard_map/reduce_scatter | solution.py:521
  10.1 23.9 %collective-permute-start.3 = (bf16[160,768]{1,0:T(8,128)(2,1)}, bf16[160,768]{1,0:T(8,128)(2,1)S(1)}, u32[]{:S(2)}, u32[]{:S(2)}) collective-permute-start(bf16[160,768]{1,0:T(8,128)(2,1)} %get-tuple-element.80), channel_id=1, source_target_pairs={{0,1},{1,2},{2,3},{3,0},{4,5},{5,6},{6,7},{7,4},{8,9},{9,10},{10,1... | collective-permute-start | bytes 737288 | tf_op jit(solution)/shard_map/ppermute | solution.py:114
  13.1 24.3 %collective-permute-start.4 = (bf16[160,768]{1,0:T(8,128)(2,1)S(1)}, bf16[160,768]{1,0:T(8,128)(2,1)S(1)}, u32[]{:S(2)}, u32[]{:S(2)}) collective-permute-start(bf16[160,768]{1,0:T(8,128)(2,1)S(1)} %get-tuple-element.81), channel_id=1, source_target_pairs={{0,2},{1,3},{2,0},{3,1},{4,6},{5,7},{6,4},{7,5},{8,10},{9,11},{10,... | collective-permute-start | bytes 737288 | tf_op jit(solution)/shard_map/ppermute | solution.py:114
  15.7 21.7 %collective-permute-start.5 = (bf16[160,768]{1,0:T(8,128)(2,1)S(1)}, bf16[160,768]{1,0:T(8,128)(2,1)S(1)}, u32[]{:S(2)}, u32[]{:S(2)}) collective-permute-start(bf16[160,768]{1,0:T(8,128)(2,1)S(1)} %get-tuple-element.82), channel_id=1, source_target_pairs={{0,3},{1,0},{2,1},{3,2},{4,7},{5,4},{6,5},{7,6},{8,11},{9,8},{10,9... | collective-permute-start | bytes 737288 | tf_op jit(solution)/shard_map/ppermute | solution.py:114
  17.1 99.5 %collective-permute-start.9 = (bf16[160,768]{1,0:T(8,128)(2,1)S(1)}, bf16[160,768]{1,0:T(8,128)(2,1)S(1)}, u32[]{:S(2)}, u32[]{:S(2)}) collective-permute-start(bf16[160,768]{1,0:T(8,128)(2,1)S(1)} %get-tuple-element.92), channel_id=1, source_target_pairs={{0,1},{1,2},{2,3},{3,0},{4,5},{5,6},{6,7},{7,4},{8,9},{9,10},{10,1... | collective-permute-start | bytes 737288 | tf_op jit(solution)/shard_map/ppermute | solution.py:114
  17.8 100.5 %collective-permute-start.10 = (bf16[160,768]{1,0:T(8,128)(2,1)S(1)}, bf16[160,768]{1,0:T(8,128)(2,1)S(1)}, u32[]{:S(2)}, u32[]{:S(2)}) collective-permute-start(bf16[160,768]{1,0:T(8,128)(2,1)S(1)} %get-tuple-element.93), channel_id=1, source_target_pairs={{0,2},{1,3},{2,0},{3,1},{4,6},{5,7},{6,4},{7,5},{8,10},{9,11},{10,... | collective-permute-start | bytes 737288 | tf_op jit(solution)/shard_map/ppermute | solution.py:114
  26.6 91.7 %copy-start.6 = (s32[2]{0:T(128)}, s32[2]{0:T(128)S(1)}, u32[]{:S(2)}) copy-start(s32[2]{0:T(128)S(1)} %pad_add_fusion.1.scalars) | copy-start | bytes 28
  30.9 31.9 %copy-start.8 = (s32[2]{0:T(128)}, s32[2]{0:T(128)S(1)}, u32[]{:S(2)}) copy-start(s32[2]{0:T(128)S(1)} %pad_add_fusion.scalars) | copy-start | bytes 28
  34.0 33.7 %collective-permute-start = (bf16[160,768]{1,0:T(8,128)(2,1)S(1)}, bf16[160,768]{1,0:T(8,128)(2,1)S(1)}, u32[]{:S(2)}, u32[]{:S(2)}) collective-permute-start(bf16[160,768]{1,0:T(8,128)(2,1)S(1)} %get-tuple-element.76), channel_id=1, source_target_pairs={{0,1},{1,2},{2,3},{3,0},{4,5},{5,6},{6,7},{7,4},{8,9},{9,10},{10,1... | collective-permute-start | bytes 737288 | tf_op jit(solution)/shard_map/ppermute | solution.py:114
  37.4 44.3 %collective-permute-start.1 = (bf16[160,768]{1,0:T(8,128)(2,1)S(1)}, bf16[160,768]{1,0:T(8,128)(2,1)S(1)}, u32[]{:S(2)}, u32[]{:S(2)}) collective-permute-start(bf16[160,768]{1,0:T(8,128)(2,1)S(1)} %get-tuple-element.77), channel_id=1, source_target_pairs={{0,2},{1,3},{2,0},{3,1},{4,6},{5,7},{6,4},{7,5},{8,10},{9,11},{10,... | collective-permute-start | bytes 737288 | tf_op jit(solution)/shard_map/ppermute | solution.py:114
  37.4 44.9 %collective-permute-start.2 = (bf16[160,768]{1,0:T(8,128)(2,1)S(1)}, bf16[160,768]{1,0:T(8,128)(2,1)S(1)}, u32[]{:S(2)}, u32[]{:S(2)}) collective-permute-start(bf16[160,768]{1,0:T(8,128)(2,1)S(1)} %get-tuple-element.78), channel_id=1, source_target_pairs={{0,3},{1,0},{2,1},{3,2},{4,7},{5,4},{6,5},{7,6},{8,11},{9,8},{10,9... | collective-permute-start | bytes 737288 | tf_op jit(solution)/shard_map/ppermute | solution.py:114
  67.7 50.6 %collective-permute-start.11 = (bf16[160,768]{1,0:T(8,128)(2,1)S(1)}, bf16[160,768]{1,0:T(8,128)(2,1)S(1)}, u32[]{:S(2)}, u32[]{:S(2)}) collective-permute-start(bf16[160,768]{1,0:T(8,128)(2,1)S(1)} %get-tuple-element.94), channel_id=1, source_target_pairs={{0,3},{1,0},{2,1},{3,2},{4,7},{5,4},{6,5},{7,6},{8,11},{9,8},{10,9... | collective-permute-start | bytes 737288 | tf_op jit(solution)/shard_map/ppermute | solution.py:114
  81.8 58.9 %collective-permute-start.6 = (bf16[160,768]{1,0:T(8,128)(2,1)S(1)}, bf16[160,768]{1,0:T(8,128)(2,1)}, u32[]{:S(2)}, u32[]{:S(2)}) collective-permute-start(bf16[160,768]{1,0:T(8,128)(2,1)S(1)} %get-tuple-element.88), channel_id=1, source_target_pairs={{0,1},{1,2},{2,3},{3,0},{4,5},{5,6},{6,7},{7,4},{8,9},{9,10},{10,1... | collective-permute-start | bytes 737288 | tf_op jit(solution)/shard_map/ppermute | solution.py:114
  82.3 58.4 %collective-permute-start.7 = (bf16[160,768]{1,0:T(8,128)(2,1)S(1)}, bf16[160,768]{1,0:T(8,128)(2,1)}, u32[]{:S(2)}, u32[]{:S(2)}) collective-permute-start(bf16[160,768]{1,0:T(8,128)(2,1)S(1)} %get-tuple-element.89), channel_id=1, source_target_pairs={{0,2},{1,3},{2,0},{3,1},{4,6},{5,7},{6,4},{7,5},{8,10},{9,11},{10,... | collective-permute-start | bytes 737288 | tf_op jit(solution)/shard_map/ppermute | solution.py:114
  116.6 24.2 %collective-permute-start.8 = (bf16[160,768]{1,0:T(8,128)(2,1)S(1)}, bf16[160,768]{1,0:T(8,128)(2,1)S(1)}, u32[]{:S(2)}, u32[]{:S(2)}) collective-permute-start(bf16[160,768]{1,0:T(8,128)(2,1)S(1)} %get-tuple-element.90), channel_id=1, source_target_pairs={{0,3},{1,0},{2,1},{3,2},{4,7},{5,4},{6,5},{7,6},{8,11},{9,8},{10,9... | collective-permute-start | bytes 737288 | tf_op jit(solution)/shard_map/ppermute | solution.py:114
  174.0 225.9 %reduce-scatter.10.cloned.1.call-start = ((), (), s32[]{:S(2)}) async-start(), calls=%async_computation.5 | async-start | bytes 5068800
  204.3 26.3 %copy-start.30 = (bf16[768,768]{1,0:T(8,128)(2,1)S(1)}, bf16[768,768]{1,0:T(8,128)(2,1)}, u32[]{:S(2)}) copy-start(bf16[768,768]{1,0:T(8,128)(2,1)} %get-tuple-element.133) | copy-start | bytes 3538948
  238.3 281.9 %reduce-scatter.6.cloned.1.call-start = ((), (), s32[]{:S(2)}) async-start(), calls=%async_computation.3 | async-start | bytes 6488064 | tf_op jit(solution)/shard_map/reduce_scatter | solution.py:520
  244.6 72.5 %copy-start.2 = (bf16[160,768]{1,0:T(8,128)(2,1)S(1)}, bf16[160,768]{1,0:T(8,128)(2,1)}, u32[]{:S(2)}) copy-start(bf16[160,768]{1,0:T(8,128)(2,1)} %get-tuple-element.86.refs_0_) | copy-start | bytes 737284
  244.7 72.5 %copy-start.3 = (bf16[160,768]{1,0:T(8,128)(2,1)S(1)}, bf16[160,768]{1,0:T(8,128)(2,1)}, u32[]{:S(2)}) copy-start(bf16[160,768]{1,0:T(8,128)(2,1)} %get-tuple-element.103.refs_1_) | copy-start | bytes 737284
  245.6 13.3 %collective-permute-start.12 = (bf16[160,768]{1,0:T(8,128)(2,1)S(1)}, bf16[160,768]{1,0:T(8,128)(2,1)S(1)}, u32[]{:S(2)}, u32[]{:S(2)}) collective-permute-start(bf16[160,768]{1,0:T(8,128)(2,1)S(1)} %copy-done.37), channel_id=1, source_target_pairs={{0,1},{1,2},{2,3},{3,0},{4,5},{5,6},{6,7},{7,4},{8,9},{9,10},{10,1... | collective-permute-start | bytes 737288 | tf_op jit(solution)/shard_map/ppermute | solution.py:114
  246.2 27.9 %collective-permute-start.14 = (bf16[160,768]{1,0:T(8,128)(2,1)S(1)}, bf16[160,768]{1,0:T(8,128)(2,1)S(1)}, u32[]{:S(2)}, u32[]{:S(2)}) collective-permute-start(bf16[160,768]{1,0:T(8,128)(2,1)S(1)} %copy-done.36), channel_id=1, source_target_pairs={{0,2},{1,3},{2,0},{3,1},{4,6},{5,7},{6,4},{7,5},{8,10},{9,11},{10,... | collective-permute-start | bytes 737288 | tf_op jit(solution)/shard_map/ppermute | solution.py:114
  247.1 28.8 %collective-permute-start.16 = (bf16[160,768]{1,0:T(8,128)(2,1)S(1)}, bf16[160,768]{1,0:T(8,128)(2,1)S(1)}, u32[]{:S(2)}, u32[]{:S(2)}) collective-permute-start(bf16[160,768]{1,0:T(8,128)(2,1)S(1)} %copy-done.35), channel_id=1, source_target_pairs={{0,3},{1,0},{2,1},{3,2},{4,7},{5,4},{6,5},{7,6},{8,11},{9,8},{10,9... | collective-permute-start | bytes 737288 | tf_op jit(solution)/shard_map/ppermute | solution.py:114
  249.9 40.4 %collective-permute-start.18 = (bf16[160,768]{1,0:T(8,128)(2,1)S(1)}, bf16[160,768]{1,0:T(8,128)(2,1)S(1)}, u32[]{:S(2)}, u32[]{:S(2)}) collective-permute-start(bf16[160,768]{1,0:T(8,128)(2,1)S(1)} %get-tuple-element.126), channel_id=1, source_target_pairs={{0,1},{1,2},{2,3},{3,0},{4,5},{5,6},{6,7},{7,4},{8,9},{9,10},{10,1... | collective-permute-start | bytes 737288 | tf_op jit(solution)/shard_map/ppermute | solution.py:114
  250.0 43.7 %collective-permute-start.13 = (bf16[160,768]{1,0:T(8,128)(2,1)}, bf16[160,768]{1,0:T(8,128)(2,1)S(1)}, u32[]{:S(2)}, u32[]{:S(2)}) collective-permute-start(bf16[160,768]{1,0:T(8,128)(2,1)} %get-tuple-element.105), channel_id=1, source_target_pairs={{0,1},{1,2},{2,3},{3,0},{4,5},{5,6},{6,7},{7,4},{8,9},{9,10},{10,1... | collective-permute-start | bytes 737288 | tf_op jit(solution)/shard_map/ppermute | solution.py:114
  258.9 49.9 %collective-permute-start.15 = (bf16[160,768]{1,0:T(8,128)(2,1)}, bf16[160,768]{1,0:T(8,128)(2,1)S(1)}, u32[]{:S(2)}, u32[]{:S(2)}) collective-permute-start(bf16[160,768]{1,0:T(8,128)(2,1)} %get-tuple-element.107), channel_id=1, source_target_pairs={{0,2},{1,3},{2,0},{3,1},{4,6},{5,7},{6,4},{7,5},{8,10},{9,11},{10,... | collective-permute-start | bytes 737288 | tf_op jit(solution)/shard_map/ppermute | solution.py:114
  274.0 36.6 %collective-permute-start.17 = (bf16[160,768]{1,0:T(8,128)(2,1)}, bf16[160,768]{1,0:T(8,128)(2,1)S(1)}, u32[]{:S(2)}, u32[]{:S(2)}) collective-permute-start(bf16[160,768]{1,0:T(8,128)(2,1)} %get-tuple-element.109), channel_id=1, source_target_pairs={{0,3},{1,0},{2,1},{3,2},{4,7},{5,4},{6,5},{7,6},{8,11},{9,8},{10,9... | collective-permute-start | bytes 737288 | tf_op jit(solution)/shard_map/ppermute | solution.py:114
  275.9 46.5 %collective-permute-start.20 = (bf16[160,768]{1,0:T(8,128)(2,1)S(1)}, bf16[160,768]{1,0:T(8,128)(2,1)S(1)}, u32[]{:S(2)}, u32[]{:S(2)}) collective-permute-start(bf16[160,768]{1,0:T(8,128)(2,1)S(1)} %get-tuple-element.128), channel_id=1, source_target_pairs={{0,2},{1,3},{2,0},{3,1},{4,6},{5,7},{6,4},{7,5},{8,10},{9,11},{10,... | collective-permute-start | bytes 737288 | tf_op jit(solution)/shard_map/ppermute | solution.py:114
  290.3 32.1 %collective-permute-start.22 = (bf16[160,768]{1,0:T(8,128)(2,1)S(1)}, bf16[160,768]{1,0:T(8,128)(2,1)S(1)}, u32[]{:S(2)}, u32[]{:S(2)}) collective-permute-start(bf16[160,768]{1,0:T(8,128)(2,1)S(1)} %get-tuple-element.130), channel_id=1, source_target_pairs={{0,3},{1,0},{2,1},{3,2},{4,7},{5,4},{6,5},{7,6},{8,11},{9,8},{10,9... | collective-permute-start | bytes 737288 | tf_op jit(solution)/shard_map/ppermute | solution.py:114
  293.7 28.7 %collective-permute-start.19 = (bf16[160,768]{1,0:T(8,128)(2,1)S(1)}, bf16[160,768]{1,0:T(8,128)(2,1)S(1)}, u32[]{:S(2)}, u32[]{:S(2)}) collective-permute-start(bf16[160,768]{1,0:T(8,128)(2,1)S(1)} %get-tuple-element.127), channel_id=1, source_target_pairs={{0,1},{1,2},{2,3},{3,0},{4,5},{5,6},{6,7},{7,4},{8,9},{9,10},{10,1... | collective-permute-start | bytes 737288 | tf_op jit(solution)/shard_map/ppermute | solution.py:114
  308.8 24.1 %collective-permute-start.21 = (bf16[160,768]{1,0:T(8,128)(2,1)S(1)}, bf16[160,768]{1,0:T(8,128)(2,1)S(1)}, u32[]{:S(2)}, u32[]{:S(2)}) collective-permute-start(bf16[160,768]{1,0:T(8,128)(2,1)S(1)} %get-tuple-element.129), channel_id=1, source_target_pairs={{0,2},{1,3},{2,0},{3,1},{4,6},{5,7},{6,4},{7,5},{8,10},{9,11},{10,... | collective-permute-start | bytes 737288 | tf_op jit(solution)/shard_map/ppermute | solution.py:114
  310.6 22.3 %collective-permute-start.23 = (bf16[160,768]{1,0:T(8,128)(2,1)S(1)}, bf16[160,768]{1,0:T(8,128)(2,1)S(1)}, u32[]{:S(2)}, u32[]{:S(2)}) collective-permute-start(bf16[160,768]{1,0:T(8,128)(2,1)S(1)} %get-tuple-element.131), channel_id=1, source_target_pairs={{0,3},{1,0},{2,1},{3,2},{4,7},{5,4},{6,5},{7,6},{8,11},{9,8},{10,9... | collective-permute-start | bytes 737288 | tf_op jit(solution)/shard_map/ppermute | solution.py:114
  (37 other events, 216.3 us)
Sparse Core Ops, SparseCore 0:
  174.1 115.1 reduce-scatter.7
  295.1 104.8 reduce-scatter.9
  406.5 113.5 reduce-scatter.5

commit v2 on v1

--- a/solution.py
+++ b/solution.py
@@ -2,6 +2,7 @@
 
 import jax
 import jax.numpy as jnp
+import numpy as np
 from jax import lax
 from jax.experimental import pallas as pl
 from jax.experimental.pallas import tpu as pltpu
@@ -17,6 +18,7 @@
 BLOCK = 256
 F32 = jnp.float32
 LOW = jnp.bfloat16
+MESH = pl.DeviceIdType.MESH
 
 
 def dot_nn(left, right):
@@ -47,31 +49,13 @@
     return number.bit_length() - 1
 
 
-def split_kernel(items, chunk, band_items_ref, rows_ref, *outs):
+def split_order(items, chunk, first):
     size = items * chunk
     row = lax.broadcasted_iota(jnp.int32, (size, size), 0)
     col = lax.broadcasted_iota(jnp.int32, (size, size), 1)
-    item = (row >> log2_of(chunk)) + band_items_ref[0]
+    item = (row >> log2_of(chunk)) + first
     item = jnp.where(item >= items, item - items, item)
-    order = jnp.where(col == (row & (chunk - 1)) * items + item, 1.0, 0.0).astype(LOW)
-    for block in range(rows_ref.shape[0] // size):
-        moved = dot_nn(order, rows_ref[block * size : (block + 1) * size, :]).astype(LOW)
-        for at, out in enumerate(outs):
-            out[block * chunk : (block + 1) * chunk, :] = moved[at * chunk : (at + 1) * chunk]
-
-
-def split_items(array, band, bands):
-    band_rows, items, width = array.shape
-    chunk = 32 if band_rows % 32 == 0 else 16
-    per = items // bands
-    return pl.pallas_call(
-        functools.partial(split_kernel, items, chunk),
-        name="split_items",
-        out_shape=[jax.ShapeDtypeStruct((band_rows, width), LOW)] * items,
-        in_specs=[smem()] + vmem(1),
-        out_specs=vmem(items),
-        compiler_params=params(32),
-    )(jnp.reshape(band * per, (1,)), array.reshape(band_rows * items, width))
+    return jnp.where(col == (row & (chunk - 1)) * items + item, 1.0, 0.0).astype(LOW)
 
 
 def merge_kernel(items, per, chunk, band_ref, *refs):
@@ -151,14 +135,8 @@
     return lax.rsqrt(jnp.mean(inputs * inputs, -1, keepdims=True) + EPS)
 
 
-def attend_kernel(bands, scalars, *refs):
-    chunks, refs = refs[:bands], refs[bands:]
-    weights, gain, cos, sin, x, query, key, value, attended_t, attended, log_total, normed = refs
+def attend_item(length, x, weights, gain, cos, sin, query, key, value, attended_t, attended, log_total, normed, ready):
     seq, width = x.shape
-    band_rows = seq // bands
-    band, length = scalars[0], scalars[1]
-    for shift, chunk in enumerate(chunks):
-        x[pl.ds(band_start(band, -shift, bands, band_rows), band_rows), :] = chunk[...]
     tile = 128
     for at in range(0, seq, tile):
         inputs = x[at : at + tile, :].astype(F32)
@@ -176,6 +154,7 @@
         return 0
 
     lax.fori_loop(0, width // project, project_tile, 0)
+    ready()
 
     def head(at, _):
         for which in range(2):
@@ -200,143 +179,250 @@
         attended[:, at : at + project] = attended_t[at : at + project, :].T
 
 
-def attend(chunks, scalars, weights_t, gain, cos, sin):
-    bands = len(chunks)
-    band_rows, width = chunks[0].shape
-    seq = bands * band_rows
-    low_t = jax.ShapeDtypeStruct((width, seq), LOW)
-    low = jax.ShapeDtypeStruct((seq, width), LOW)
-    pairs = seq * seq * width
+def feed_item(follows, x, attended, attended_t, cot, weights, gain, grads, g_norm, out, grad_attended_t, scratch):
+    w_out, w_gate, w_up, w_down = weights
+    g_out, g_gate, g_up, g_down = grads
+    normed, normed_t, resid, out_acc, back_acc = scratch
+    seq, width = x.shape
+    tile, wide = 128, 512
+
+    def put(ref, at, grad):
+        if follows:
+            grad += ref[at].astype(F32)
+        ref[at] = grad.astype(LOW)
+
+    for at in range(0, seq, tile):
+        rows = slice(at, at + tile)
+        total = x[rows, :].astype(F32) + dot_nn(attended[rows, :], w_out[...])
+        resid[rows, :] = total
+        out_acc[rows, :] = total
+        low = (total * norm_rows(total) * gain[...]).astype(LOW)
+        normed[rows, :] = low
+        normed_t[:, rows] = low.T
+    back_acc[...] = jnp.zeros_like(back_acc)
+
+    def chunk(step, _):
+        span = pl.ds(pl.multiple_of(step * wide, wide), wide)
+        gate = dot_nn(normed[...], w_gate[:, span])
+        upward = dot_nn(normed[...], w_up[:, span])
+        grad_hidden = dot_nt(cot[...], w_down[span, :])
+        sig = 0.5 * jnp.tanh(0.5 * gate) + 0.5
+        silu = gate * sig
+        hidden = (silu * upward).astype(LOW)
+        grad_gate = (grad_hidden * upward * (sig + silu * (1.0 - sig))).astype(LOW)
+        grad_upward = (grad_hidden * silu).astype(LOW)
+        out_acc[...] += dot_nn(hidden, w_down[span, :])
+        back_acc[...] += dot_nt(grad_gate, w_gate[:, span]) + dot_nt(grad_upward, w_up[:, span])
+        put(g_down, (span, slice(None)), dot_nn(hidden.T, cot[...]))
+        put(g_gate, (slice(None), span), dot_nn(normed_t[...], grad_gate))
+        put(g_up, (slice(None), span), dot_nn(normed_t[...], grad_upward))
+        return 0
+
+    lax.fori_loop(0, w_gate.shape[1] // wide, chunk, 0)
+    norm_sum = jnp.zeros((1, width), F32)
+    for at in range(0, seq, tile):
+        rows = slice(at, at + tile)
+        out[rows, :] = out_acc[rows, :].astype(LOW)
+        total, incoming = resid[rows, :], back_acc[rows, :]
+        inv = norm_rows(total)
+        scaled = total * inv
+        norm_sum += jnp.sum(incoming * scaled, 0, keepdims=True)
+        weighted = incoming * gain[...]
+        grad = cot[rows, :].astype(F32) + inv * (weighted - scaled * jnp.mean(weighted * scaled, -1, keepdims=True))
+        cot[rows, :] = grad.astype(LOW)
+    g_norm[...] = g_norm[...] + norm_sum if follows else norm_sum
+    grad_attended_t[...] = dot_nt(w_out[...], cot[...]).astype(LOW)
+    put(g_out, (slice(None), slice(None)), dot_nn(attended_t[...], cot[...]))
+
+
+class Copies:
+    def __init__(self, local, send, receive, bands):
+        self.local, self.send, self.receive = local, send, receive
+        self.at, self.link, self.bands = 0, 0, bands
+        self.band, self.items = lax.axis_index("band"), lax.axis_index("items")
+
+    def start(self, source, target):
+        copy = pltpu.make_async_copy(source, target, self.local.at[self.at])
+        self.at += 1
+        copy.start()
+        return copy
+
+    def other(self, shift):
+        return lax.rem(self.band + shift + self.bands, self.bands)
+
+    def greet(self):
+        barrier = pltpu.get_barrier_semaphore()
+        for shift in range(1, self.bands):
+            pl.semaphore_signal(barrier, inc=1, device_id=(self.items, self.other(shift)), device_id_type=MESH)
+        pl.semaphore_wait(barrier, self.bands - 1)
+
+    def remote(self, source, target, arrival, device):
+        ends = []
+        for place in (target, arrival):
+            ends.append(
+                pltpu.make_async_remote_copy(
+                    src_ref=source,
+                    dst_ref=place,
+                    send_sem=self.send.at[self.link],
+                    recv_sem=self.receive.at[self.link],
+                    device_id=device,
+                    device_id_type=MESH,
+                )
+            )
+        self.link += 1
+        ends[0].start()
+        return ends
+
+
+def front_kernel(
+    bands, per, lengths, tokens, cotangent, gain_attn, gain_ffn, cos, sin,
+    w_query, w_key, w_value, w_out, w_gate, w_up, w_down,
+    x_to, query_to, key_to, value_to, attended_t_to, log_total, grad_resid_to, grad_attended_t_to, out_to, home,
+    g_gate_to, g_up_to, g_down_to, g_out_to, g_norm,
+    weights_t, out_s, gate_s, up_s, down_s, g_gate, g_up, g_down, g_out,
+    x, attended, attended_t, cot, query, key, value, grad_attended_t, normed, normed_t, resid, out_acc, back_acc,
+    token_send, cot_send, local, send, receive,
+):
+    seq, width = x.shape[1:]
+    band_rows, items = seq // bands, bands * per
+    copies = Copies(local, send, receive, bands)
+    band = copies.band
+    loads = [copies.start(w_query, g_down.at[pl.ds(0, width)]), copies.start(w_key, g_down.at[pl.ds(width, width)])]
+    loads.append(copies.start(w_value, g_out))
+    late = [copies.start(a, b) for a, b in ((w_out, out_s), (w_gate, gate_s), (w_up, up_s), (w_down, down_s))]
+    copies.greet()
+
+    def own_rows(shift):
+        return pl.ds(pl.multiple_of(copies.other(shift) * band_rows, band_rows), band_rows)
+
+    chunk = 32 if band_rows % 32 == 0 else 16
+    size = items * chunk
+    order = split_order(items, chunk, band * per)
+
+    def split(source, kept, sent):
+        for block in range(band_rows // chunk):
+            moved = dot_nn(order, source[block * size : (block + 1) * size, :]).astype(LOW)
+            rows = pl.ds(pl.multiple_of(band * band_rows + block * chunk, 16), chunk)
+            for at in range(items):
+                part = moved[at * chunk : (at + 1) * chunk]
+                if at < per:
+                    kept[at, rows, :] = part
+                else:
+                    sent[at - per, block * chunk : (block + 1) * chunk, :] = part
+
+    def scatter(sent, kept, item):
+        return [
+            copies.remote(
+                sent.at[(shift - 1) * per + item],
+                kept.at[item, own_rows(0)],
+                kept.at[item, own_rows(-shift)],
+                (copies.items, copies.other(shift)),
+            )
+            for shift in range(1, bands)
+        ]
+
+    split(tokens, x, token_send)
+    token_links = [scatter(token_send, x, item) for item in range(per)]
+    for part, source in enumerate((g_down.at[pl.ds(0, width)], g_down.at[pl.ds(width, width)], g_out)):
+        loads[part].wait()
+        for at in range(0, width, 256):
+            weights_t[part * width + at : part * width + at + 256, :] = source[:, at : at + 256].T
+    split(cotangent, cot, cot_send)
+    cot_links, saves, home_links = [], [], []
+
+    for item in range(per):
+        for _, arrival in token_links[item]:
+            arrival.wait_recv()
+        cot_links.append(scatter(cot_send, cot, item))
+        saved = [copies.start(x.at[item], x_to.at[item])]
+        if item:
+            for save in saves[-1][1:]:
+                save.wait()
+
+        def ready():
+            for source, target in ((query, query_to), (key, key_to), (value, value_to)):
+                saved.append(copies.start(source, target.at[item]))
+
+        attend_item(
+            lengths[band * per + item], x.at[item], weights_t, gain_attn, cos, sin, query, key, value,
+            attended_t.at[item], attended.at[item], log_total.at[item], normed, ready,
+        )
+        saves.append(saved)
+    waits = [save for save in saves[-1][1:]] + [saved[0] for saved in saves]
+    for load in late:
+        load.wait()
+    grads = (g_out, g_gate, g_up, g_down)
+    for item in range(per):
+        for _, arrival in cot_links[item]:
+            arrival.wait_recv()
+        if item:
+            dependent.wait()
+        feed_item(
+            item > 0, x.at[item], attended.at[item], attended_t.at[item], cot.at[item],
+            (out_s, gate_s, up_s, down_s), gain_ffn, grads, g_norm, attended.at[item], grad_attended_t,
+            (normed, normed_t, resid, out_acc, back_acc),
+        )
+        dependent = copies.start(grad_attended_t, grad_attended_t_to.at[item])
+        waits.append(copies.start(attended_t.at[item], attended_t_to.at[item]))
+        waits.append(copies.start(cot.at[item], grad_resid_to.at[item]))
+        if item < per - 1:
+            waits.append(copies.start(attended.at[item, own_rows(0)], home.at[item]))
+            for shift in range(1, bands):
+                slot = home.at[shift * (per - 1) + item]
+                home_links.append(
+                    copies.remote(attended.at[item, own_rows(shift)], slot, slot, (copies.items, copies.other(shift)))
+                )
+        else:
+            waits.append(copies.start(attended.at[item], out_to))
+    waits.append(dependent)
+    waits += [copies.start(a, b) for a, b in ((g_gate, g_gate_to), (g_up, g_up_to), (g_down, g_down_to), (g_out, g_out_to))]
+    for wait in waits:
+        wait.wait()
+    for links in token_links + cot_links + [home_links]:
+        for started, _ in links:
+            started.wait_send()
+    for _, arrival in home_links:
+        arrival.wait_recv()
+
+
+def front(bands, lengths, tokens, cotangent, gains, tables, weights):
+    band_rows, items, width = tokens.shape
+    per, seq, ff = items // bands, bands * band_rows, weights[4].shape[1]
+    rows, columns = (seq, width), (width, seq)
+    many = lambda shape: jax.ShapeDtypeStruct((per,) + shape, LOW)
+    low = lambda shape: jax.ShapeDtypeStruct(shape, LOW)
+    scratch = lambda *shape: pltpu.VMEM(shape, LOW)
+    full = lambda *shape: pltpu.VMEM(shape, F32)
+    outside = pl.BlockSpec(memory_space=pl.ANY)
+    inside = pl.BlockSpec(memory_space=pltpu.VMEM)
+    home = max(bands * (per - 1), 1)
+    local = 7 + per * 8 + bands + 8
+    links = (bands - 1) * per * 3
     return pl.pallas_call(
-        functools.partial(attend_kernel, bands),
-        name="attend",
-        out_shape=[low, low_t, low_t, low_t, low_t, low, jax.ShapeDtypeStruct((width // HEAD_DIM, 1, seq), F32)],
-        in_specs=[smem()] + vmem(bands + 4),
-        out_specs=vmem(7),
-        scratch_shapes=[pltpu.VMEM((seq, width), LOW)],
-        compiler_params=params(48),
-        cost_estimate=pl.CostEstimate(
-            flops=6 * seq * width * width + 12 * pairs, bytes_accessed=20 * seq * width, transcendentals=0
+        functools.partial(front_kernel, bands, per),
+        name="front",
+        out_shape=[many(rows)] + [many(columns)] * 4
+        + [jax.ShapeDtypeStruct((per, width // HEAD_DIM, 1, seq), F32), many(rows), many(columns), low(rows)]
+        + [low((home, band_rows, width)), low((width, ff)), low((width, ff)), low((ff, width)), low((width, width))]
+        + [jax.ShapeDtypeStruct((1, width), F32)],
+        in_specs=[smem()] + [inside] * 6 + [outside] * 7,
+        out_specs=[outside] * 5 + [inside] + [outside] * 8 + [inside],
+        scratch_shapes=[
+            scratch(3 * width, width), scratch(width, width), scratch(width, ff), scratch(width, ff), scratch(ff, width),
+            scratch(width, ff), scratch(width, ff), scratch(ff, width), scratch(width, width),
+            scratch(per, seq, width), scratch(per, seq, width), scratch(per, width, seq), scratch(per, seq, width),
+            scratch(width, seq), scratch(width, seq), scratch(width, seq), scratch(width, seq),
+            scratch(seq, width), scratch(width, seq), full(seq, width), full(seq, width), full(seq, width),
+            scratch(items - per, band_rows, width), scratch(items - per, band_rows, width),
+            pltpu.SemaphoreType.DMA((local,)), pltpu.SemaphoreType.DMA((links,)), pltpu.SemaphoreType.DMA((links,)),
+        ],
+        compiler_params=pltpu.CompilerParams(
+            vmem_limit_bytes=62 * 2**20, collective_id=0, has_side_effects=True
         ),
-    )(scalars, *chunks, weights_t, gain, cos, sin)
-
-
-def feed_kernel(bands, follows, scalars, *refs):
-    chunks, refs = refs[:bands], refs[bands:]
-    x, attended, attended_t, w_out, gain, w_gate, w_up, w_down = refs[:8]
-    refs = refs[8:]
-    prev = None
-    if follows:
-        prev, refs = refs[:5], refs[5:]
-    outs, refs = refs[:bands], refs[bands:]
-    grad_resid_low, grad_attended_t, g_gate, g_up, g_down, g_out, g_norm = refs[:7]
-    cot, resid, normed, normed_t, out_acc, back_acc = refs[7:]
-    seq, width = x.shape
-    band_rows = seq // bands
-    band = scalars[0]
-    step = pl.program_id(0)
-    tile = 128
-
-    @pl.when(step == 0)
-    def _():
-        for shift, chunk in enumerate(chunks):
-            cot[pl.ds(band_start(band, -shift, bands, band_rows), band_rows), :] = chunk[...]
-        for at in range(0, seq, tile):
-            rows = slice(at, at + tile)
-            total = x[rows, :].astype(F32) + dot_nn(attended[rows, :], w_out[...])
-            resid[rows, :] = total
-            out_acc[rows, :] = total
-            low = (total * norm_rows(total) * gain[...]).astype(LOW)
-            normed[rows, :] = low
-            normed_t[:, rows] = low.T
-        back_acc[...] = jnp.zeros_like(back_acc)
-
-    gate = dot_nn(normed[...], w_gate[...])
-    upward = dot_nn(normed[...], w_up[...])
-    grad_hidden = dot_nt(cot[...], w_down[...])
-    sig = 0.5 * jnp.tanh(0.5 * gate) + 0.5
-    silu = gate * sig
-    hidden = (silu * upward).astype(LOW)
-    grad_gate = (grad_hidden * upward * (sig + silu * (1.0 - sig))).astype(LOW)
-    grad_upward = (grad_hidden * silu).astype(LOW)
-    out_acc[...] += dot_nn(hidden, w_down[...])
-    back_acc[...] += dot_nt(grad_gate, w_gate[...]) + dot_nt(grad_upward, w_up[...])
-
-    def put(out, at, grad):
-        if follows:
-            grad += prev[at][...].astype(F32)
-        out[...] = grad.astype(LOW)
-
-    put(g_down, 2, dot_nn(hidden.T, cot[...]))
-    put(g_gate, 0, dot_nn(normed_t[...], grad_gate))
-    put(g_up, 1, dot_nn(normed_t[...], grad_upward))
-
-    @pl.when(step == pl.num_programs(0) - 1)
-    def _():
-        norm_sum = jnp.zeros((1, width), F32)
-        for at in range(0, seq, tile):
-            rows = slice(at, at + tile)
-            total, incoming = resid[rows, :], back_acc[rows, :]
-            inv = norm_rows(total)
-            scaled = total * inv
-            norm_sum += jnp.sum(incoming * scaled, 0, keepdims=True)
-            weighted = incoming * gain[...]
-            grad = cot[rows, :].astype(F32) + inv * (
-                weighted - scaled * jnp.mean(weighted * scaled, -1, keepdims=True)
-            )
-            grad_resid_low[rows, :] = grad.astype(LOW)
-        if follows:
-            norm_sum += prev[4][...]
-        g_norm[...] = norm_sum
-        grad_attended_t[...] = dot_nt(w_out[...], grad_resid_low[...]).astype(LOW)
-        put(g_out, 3, dot_nn(attended_t[...], grad_resid_low[...]))
-        for shift, out in enumerate(outs):
-            out[...] = out_acc[pl.ds(band_start(band, shift, bands, band_rows), band_rows), :].astype(LOW)
-
-
-def feed(chunks, scalars, x, attended, attended_t, w_out, gain, w_gate, w_up, w_down, prev):
-    bands = len(chunks)
-    seq, width = x.shape
-    ff = w_gate.shape[1]
-    wide = 512
-    whole = lambda *shape: pl.BlockSpec(shape, lambda i: (0,) * len(shape))
-    columns = pl.BlockSpec((width, wide), lambda i: (0, i))
-    rows = pl.BlockSpec((wide, width), lambda i: (i, 0))
-    grad_specs = [columns, columns, rows, whole(width, width), whole(1, width)]
-    band_rows = seq // bands
-    return pl.pallas_call(
-        functools.partial(feed_kernel, bands, prev is not None),
-        name="feed",
-        grid=(ff // wide,),
-        out_shape=[jax.ShapeDtypeStruct((band_rows, width), LOW)] * bands
-        + [
-            jax.ShapeDtypeStruct((seq, width), LOW),
-            jax.ShapeDtypeStruct((width, seq), LOW),
-            jax.ShapeDtypeStruct((width, ff), LOW),
-            jax.ShapeDtypeStruct((width, ff), LOW),
-            jax.ShapeDtypeStruct((ff, width), LOW),
-            jax.ShapeDtypeStruct((width, width), LOW),
-            jax.ShapeDtypeStruct((1, width), F32),
-        ],
-        in_specs=[smem()]
-        + [whole(band_rows, width)] * bands
-        + [whole(seq, width), whole(seq, width), whole(width, seq), whole(width, width), whole(1, width)]
-        + [columns, columns, rows]
-        + (grad_specs if prev is not None else []),
-        out_specs=[whole(band_rows, width)] * bands + [whole(seq, width), whole(width, seq)] + grad_specs,
-        scratch_shapes=[
-            pltpu.VMEM((seq, width), LOW),
-            pltpu.VMEM((seq, width), F32),
-            pltpu.VMEM((seq, width), LOW),
-            pltpu.VMEM((width, seq), LOW),
-            pltpu.VMEM((seq, width), F32),
-            pltpu.VMEM((seq, width), F32),
-        ],
-        compiler_params=params(60),
-        cost_estimate=pl.CostEstimate(
-            flops=18 * seq * width * ff + 6 * seq * width * width, bytes_accessed=12 * width * ff, transcendentals=0
-        ),
-    )(scalars, *chunks, x, attended, attended_t, w_out, gain, w_gate, w_up, w_down, *(prev or ()))
+    )(
+        lengths, tokens.reshape(band_rows * items, width), cotangent.reshape(band_rows * items, width),
+        *gains, *tables, *weights,
+    )
 
 
 def back_kernel(bands, follows, scalars, *refs):
@@ -451,9 +537,9 @@
 
 
 def rope_tables(seq):
-    frequency = jnp.exp(-jnp.log(ROPE_BASE) * (2.0 * jnp.arange(HALF, dtype=F32) / HEAD_DIM))
-    angles = frequency[:, None] * jnp.arange(seq, dtype=jnp.int32).astype(F32)[None, :]
-    return jnp.cos(angles), jnp.sin(angles)
+    frequency = np.exp(-np.log(ROPE_BASE) * (2.0 * np.arange(HALF) / HEAD_DIM))
+    angles = frequency[:, None] * np.arange(seq)[None, :]
+    return jnp.asarray(np.cos(angles), F32), jnp.asarray(np.sin(angles), F32)
 
 
 def per_device(
@@ -475,34 +561,24 @@
     per = items // bands
     seq = bands * band_rows
     band = lax.axis_index("band")
-    token_parts = split_items(tokens, band, bands)
-    x_chunks = [exchange(token_parts, bands, per, item) for item in range(per)]
-    cot_parts = split_items(cotangent, band, bands)
-    cot_chunks = [exchange(cot_parts, bands, per, item) for item in range(per)]
     cos, sin = rope_tables(seq)
     gain_attn, gain_ffn = norm_attn.reshape(1, width), norm_ffn.reshape(1, width)
-    weights_t = jnp.concatenate([w_query.T, w_key.T, w_value.T], 0)
     scalars = [
         jnp.stack([band, lax.dynamic_index_in_dim(lengths, band * per + item, keepdims=False)]).astype(jnp.int32)
         for item in range(per)
     ]
-    fronts = [attend(x_chunks[i], scalars[i], weights_t, gain_attn, cos, sin) for i in range(per)]
-    feeds, prev = [], None
-    for i in range(per):
-        x, _, _, _, attended_t, attended, _ = fronts[i]
-        feeds.append(
-            feed(cot_chunks[i], scalars[i], x, attended, attended_t, w_out, gain_ffn, w_gate, w_up, w_down, prev)
-        )
-        prev = feeds[-1][bands + 2 :]
-    out_parts = [f[:bands] for f in feeds]
-    g_gate, g_up, g_down, g_out, g_norm_ffn = prev
+    (
+        x, query, key, value, attended_t, log_total, grad_resid, grad_attended_t, out_last, home_early,
+        g_gate, g_up, g_down, g_out, g_norm_ffn,
+    ) = front(
+        bands, lengths, tokens, cotangent, (gain_attn, gain_ffn), (cos, sin),
+        (w_query, w_key, w_value, w_out, w_gate, w_up, w_down),
+    )
     backs, prev = [], None
     for i in range(per):
-        x, query, key, value, attended_t, _, log_total = fronts[i]
-        grad_resid, grad_attended_t = feeds[i][bands : bands + 2]
         backs.append(
             back_attend(
-                bands, scalars[i], x, grad_resid, grad_attended_t, attended_t, query, key, value, log_total,
+                bands, scalars[i], x[i], grad_resid[i], grad_attended_t[i], attended_t[i], query[i], key[i], value[i], log_total[i],
                 (w_query, w_key, w_value), gain_attn, cos, sin, prev,
             )
         )
@@ -513,7 +589,12 @@
         came = [exchange([parts[i][k] for k in range(bands)], bands, 1, 0) for i in range(per)]
         return merge_items([came[j][k] for k in range(bands) for j in range(per)], band, bands)
 
-    output = home(out_parts)
+    def last_part(shift):
+        return lax.dynamic_slice_in_dim(out_last, band_start(band, shift, bands, band_rows), band_rows, 0)
+
+    came = exchange([last_part(k) for k in range(bands)], bands, 1, 0)
+    early = [[home_early[k * (per - 1) + j] for j in range(per - 1)] for k in range(bands)]
+    output = merge_items([part for k in range(bands) for part in early[k] + [came[k]]], band, bands)
     grad_tokens = home([b[:bands] for b in backs])
     axes = ("items", "band")
     gains = jnp.concatenate([g_norm_attn.T, g_norm_ffn.T], 1)

time: 535 us -> 512 us (0.957)
  starting transfers between devices: 98.3 us -> 21.8 us
  waiting for transfers between devices: 207 us -> 249 us
  Pallas kernels: 155 us -> 187 us
  local copies, waits for them, and re-layouts: 40.7 us -> 26.9 us
    ppermute x24 -> x9, starting transfers between devices: 98 us -> 21.5 us  [exchange(): lax.ppermute(parts[shift * per + item], 'band', [(i, (i + shift) % bands)...]
    pallas_call x6 -> x1, Pallas kernels: 101 us -> 133 us  [front(): pl.pallas_call(functools.partial(front_kernel, bands, per), name='front',...]
    unnamed x87 -> x26, local copies, waits for them, and re-layouts: 26.9 us -> 4.14 us
    unnamed x4, waiting for transfers between devices: 63.5 us -> 85.5 us
    ppermute x24 -> x9, waiting for transfers between devices: 25.9 us -> 46.8 us  [exchange(): lax.ppermute(parts[shift * per + item], 'band', [(i, (i + shift) % bands)...]
    squeeze x0 -> x6, local copies, waits for them, and re-layouts: none -> 6.62 us  [the longest x1 2.5 us: per_device(): grad_resid[i]]
  transfers between devices with their start and end apart: 27 -> 12, of which waited for: 6 -> 6; matrix products, arithmetic and copies ran while one was open for 6% -> 6% of each run, Pallas kernels for 23% -> 10%
where the time goes in v2:
time: 512 us; the launch traced here: 509 us
  waiting for transfers between devices  249 us (49%)
  Pallas kernels  187 us (37%)
  local copies, waits for them, and re-layouts  26.9 us (5%)
  starting transfers between devices  21.8 us (4%)
  between operations  14.2 us (3%)
  other arithmetic  10.2 us (2%)
    pallas_call x1, Pallas kernels, front(): pl.pallas_call(functools.partial(front_kernel, bands, per), name='front',...  133 us
    reduce_scatter x1, waiting for transfers between devices, per_device(): lax.psum_scatter(jnp.concatenate([g_gate, g_up], 1), axes, scatter_dimens...  117 us
    unnamed x4, waiting for transfers between devices  85.5 us
    pallas_call x2, Pallas kernels, back_attend(): pl.pallas_call(functools.partial(back_kernel, bands, prev is not None), n...  49.4 us
    ppermute x9, waiting for transfers between devices, exchange(): lax.ppermute(parts[shift * per + item], 'band', [(i, (i + shift) % bands)...  46.8 us
    ppermute x9, starting transfers between devices, exchange(): lax.ppermute(parts[shift * per + item], 'band', [(i, (i + shift) % bands)...  21.5 us
  transfers between devices with their start and end apart: 12, of which 6 were waited for; matrix products, arithmetic and copies ran while one was open for 6% of the time, Pallas kernels for 10%

profile of v2, /device:TPU:0, one launch (start us, length us, event | category | flops | bytes accessed | tf_op | source)
XLA Modules:
  0.0 508.8 jit_solution(16540025692517942911)
XLA Ops:
  7.2 1.3 reshape.47.gain_attn.refs_11_
  8.5 1.3 reshape.48.gain_ffn
  9.8 133.4 %front.1 = (bf16[2,640,768]{2,1,0:T(8,128)(2,1)}, bf16[2,768,640]{2,1,0:T(8,128)(2,1)}, bf16[2,768,640]{2,1,0:T(8,128)(2,1)}, bf16[2,768,640]{2,1,0:T(8,128)(2,1...) custom-call(s32[8]{0:T(128)} %lengths.1, ...), custom_call_target="tpu_custom_call" | custom-call | tf_op jit(solution)/shard_map/front/pallas_call | solution.py:401
  143.8 1.7 slice_bitcast_fusion.4
  146.1 1.4 pad_add_fusion
  147.5 0.8 copy.28
  148.4 2.5 slice_bitcast_fusion.5
  152.1 1.2 copy-done.3
  153.8 2.0 slice_bitcast_fusion
  155.9 24.1 %back_attend.2 = (bf16[160,768]{1,0:T(8,128)(2,1)S(1)}, bf16[160,768]{1,0:T(8,128)(2,1)S(1)}, bf16[160,768]{1,0:T(8,128)(2,1)S(1)}, bf16[160,768]{1,0:T(8,128)(2...) custom-call(s32[2]{0:T(128)S(1)} %get-tuple-element.99.scalars, ...), custom_call_target="tpu_custom_call" | custom-call | flops 13967032320 | bytes 11796480 | tf_op jit(solution)/shard_map/back_attend/pallas_call | solution.py:520
  179.9 25.3 %back_attend.3 = (bf16[160,768]{1,0:T(8,128)(2,1)S(1)}, bf16[160,768]{1,0:T(8,128)(2,1)}, bf16[160,768]{1,0:T(8,128)(2,1)S(1)}, bf16[160,768]{1,0:T(8,128)(2,1)S...) custom-call(s32[2]{0:T(128)S(1)} %get-tuple-element.100.scalars, bf16[640,768]{1,0:T(8,128)(2,1)S(1)} %get-tuple-element.106.refs_0_, ...), custom_call_target="tpu_custom_call" | custom-call | flops 13967032320 | bytes 11796480 | tf_op jit(solution)/shard_map/back_attend/pallas_call | solution.py:520
  205.5 7.9 %concatenate.9 = bf16[768,3074]{1,0:T(8,128)(2,1)} concatenate(bf16[768,2304]{1,0:T(8,128)(2,1)} %get-tuple-element.58, bf16[768,768]{1,0:T(8,128)(2,1)} %get-tuple-element.59, bf16[768,1]{1,0:T(8,128)(2,1)S(1)} %copy.27, bf16[768,1]{1,0:T(8,128)(2,1)S(1)} %copy-done.9), dimensions={1} | concatenate | bytes 9443328 | tf_op jit(solution)/shard_map/concatenate | solution.py:603
  213.5 6.3 %pad_maximum_fusion = bf16[768,4096]{1,0:T(8,128)(2,1)} fusion(bf16[768,2048]{1,0:T(8,128)(2,1)} %get-tuple-element.63, bf16[768,2048]{1,0:T(8,128)(2,1)} %get-tuple-element.62), kind=kLoop, calls=%fused_computation | loop fusion | flops 12582912 | bytes 12582912 | tf_op jit(solution)/shard_map/concatenate | solution.py:601
  219.9 1.1 copy-done.7
  221.1 8.9 %collective-permute-start.2 = (bf16[160,768]{1,0:T(8,128)(2,1)S(1)}, bf16[160,768]{1,0:T(8,128)(2,1)S(1)}, u32[]{:S(2)}, u32[]{:S(2)}) collective-permute-start(bf16[160,768]{1,0:T(8,128)(2,1)S(1)} %get-tuple-element.81), channel_id=1, source_target_pairs={{0,3},{1,0},{2,1},{3,2},{4,7},{5,4},{6,5},{7,6},{8,11},{9,8},{10,9... | collective-permute-start | bytes 737288 | tf_op jit(solution)/shard_map/ppermute | solution.py:98
  230.7 2.8 collective-permute-start.4
  233.5 0.9 collective-permute-start.6
  234.4 2.0 collective-permute-done.2.refs_7_
  236.4 4.3 collective-permute-start.8
  240.7 24.4 %collective-permute-done.1.refs_5_ = bf16[160,768]{1,0:T(8,128)(2,1)S(1)} collective-permute-done((bf16[160,768]{1,0:T(8,128)(2,1)S(1)}, bf16[160,768]{1,0:T(8,128)(2,1)S(1)}, u32[]{:S(2)}, u32[]{:S(2)}) %collective-permute-start.1) | collective-permute-done | bytes 245792 | tf_op jit(solution)/shard_map/ppermute | solution.py:98
  265.1 1.0 collective-permute-start.5
  266.1 2.9 collective-permute-start.7
  269.1 2.0 merge_items.2
  271.0 9.6 %collective-permute-done.6.refs_5_ = bf16[160,768]{1,0:T(8,128)(2,1)S(1)} collective-permute-done((bf16[160,768]{1,0:T(8,128)(2,1)S(1)}, bf16[160,768]{1,0:T(8,128)(2,1)S(1)}, u32[]{:S(2)}, u32[]{:S(2)}) %collective-permute-start.6) | collective-permute-done | bytes 245792 | tf_op jit(solution)/shard_map/ppermute | solution.py:98
  280.6 10.7 %collective-permute-done.5.refs_4_ = bf16[160,768]{1,0:T(8,128)(2,1)S(1)} collective-permute-done((bf16[160,768]{1,0:T(8,128)(2,1)S(1)}, bf16[160,768]{1,0:T(8,128)(2,1)S(1)}, u32[]{:S(2)}, u32[]{:S(2)}) %collective-permute-start.5) | collective-permute-done | bytes 245792 | tf_op jit(solution)/shard_map/ppermute | solution.py:98
  291.4 2.0 merge_items.3
  293.3 1.6 convert_element_type.12
  294.9 85.5 %reduce-scatter.10.cloned.1.call-done = bf16[24,3074]{1,0:T(8,128)(2,1)} async-done(((bf16[768,3074]{1,0:T(8,128)(2,1)}), bf16[24,3074]{1,0:T(8,128)(2,1)}) %reduce-scatter.10.cloned.1.call-update) | async-done | bytes 147568
  380.4 0.9 convert_element_type.10
  382.0 1.5 fusion.1
  383.6 116.7 %reduce-scatter.6.cloned.1.call-done = bf16[24,4096]{1,0:T(8,128)(2,1)} async-done(((bf16[768,4096]{1,0:T(8,128)(2,1)}), bf16[24,4096]{1,0:T(8,128)(2,1)}) %reduce-scatter.6.cloned.1.call-update) | async-done | bytes 196624 | tf_op jit(solution)/shard_map/reduce_scatter | solution.py:601
  500.3 1.7 fusion
  (48 shorter events, 4.8 us)
Async XLA Ops:
  7.2 286.2 %reduce-scatter.8.cloned.1.call-start = ((), (), s32[]{:S(2)}) async-start(), calls=%async_computation.4 | async-start | bytes 3244032 | tf_op jit(solution)/shard_map/reduce_scatter | solution.py:602
  143.1 0.7 copy-start.12
  143.2 237.2 %reduce-scatter.10.cloned.1.call-start = ((), (), s32[]{:S(2)}) async-start(), calls=%async_computation.5 | async-start | bytes 5068800
  143.8 1.7 copy-start.11
  143.8 4.5 copy-start.10
  148.4 2.7 copy-start.5
  148.4 3.3 copy-start.6
  151.7 1.5 copy-start.3
  151.7 2.1 copy-start.4
  153.8 2.0 copy-start
  153.8 2.0 copy-start.1
  153.8 2.0 copy-start.2
  179.9 25.5 %copy-start.9 = (bf16[768,1]{1,0:T(8,128)(2,1)S(1)}, bf16[768,1]{1,0:T(8,128)(2,1)}, u32[]{:S(2)}) copy-start(bf16[768,1]{1,0:T(8,128)(2,1)} %copy.28) | copy-start | bytes 4612
  213.4 286.9 %reduce-scatter.6.cloned.1.call-start = ((), (), s32[]{:S(2)}) async-start(), calls=%async_computation.3 | async-start | bytes 6488064 | tf_op jit(solution)/shard_map/reduce_scatter | solution.py:601
  219.8 1.2 copy-start.7
  219.9 49.1 %copy-start.8 = (bf16[4,160,768]{2,1,0:T(8,128)(2,1)S(1)}, bf16[4,160,768]{2,1,0:T(8,128)(2,1)}, u32[]{:S(2)}) copy-start(bf16[4,160,768]{2,1,0:T(8,128)(2,1)} %get-tuple-element.38) | copy-start | bytes 2949124
  221.1 15.4 %collective-permute-start.2 = (bf16[160,768]{1,0:T(8,128)(2,1)S(1)}, bf16[160,768]{1,0:T(8,128)(2,1)S(1)}, u32[]{:S(2)}, u32[]{:S(2)}) collective-permute-start(bf16[160,768]{1,0:T(8,128)(2,1)S(1)} %get-tuple-element.81), channel_id=1, source_target_pairs={{0,3},{1,0},{2,1},{3,2},{4,7},{5,4},{6,5},{7,6},{8,11},{9,8},{10,9... | collective-permute-start | bytes 737288 | tf_op jit(solution)/shard_map/ppermute | solution.py:98
  230.0 35.1 %collective-permute-start.1 = (bf16[160,768]{1,0:T(8,128)(2,1)S(1)}, bf16[160,768]{1,0:T(8,128)(2,1)S(1)}, u32[]{:S(2)}, u32[]{:S(2)}) collective-permute-start(bf16[160,768]{1,0:T(8,128)(2,1)S(1)} %get-tuple-element.82), channel_id=1, source_target_pairs={{0,2},{1,3},{2,0},{3,1},{4,6},{5,7},{6,4},{7,5},{8,10},{9,11},{10,... | collective-permute-start | bytes 737288 | tf_op jit(solution)/shard_map/ppermute | solution.py:98
  230.0 35.1 %collective-permute-start = (bf16[160,768]{1,0:T(8,128)(2,1)S(1)}, bf16[160,768]{1,0:T(8,128)(2,1)S(1)}, u32[]{:S(2)}, u32[]{:S(2)}) collective-permute-start(bf16[160,768]{1,0:T(8,128)(2,1)S(1)} %get-tuple-element.83), channel_id=1, source_target_pairs={{0,1},{1,2},{2,3},{3,0},{4,5},{5,6},{6,7},{7,4},{8,9},{9,10},{10,1... | collective-permute-start | bytes 737288 | tf_op jit(solution)/shard_map/ppermute | solution.py:98
  230.7 35.5 %collective-permute-start.4 = (bf16[160,768]{1,0:T(8,128)(2,1)}, bf16[160,768]{1,0:T(8,128)(2,1)S(1)}, u32[]{:S(2)}, u32[]{:S(2)}) collective-permute-start(bf16[160,768]{1,0:T(8,128)(2,1)} %get-tuple-element.53), channel_id=1, source_target_pairs={{0,1},{1,2},{2,3},{3,0},{4,5},{5,6},{6,7},{7,4},{8,9},{9,10},{10,1... | collective-permute-start | bytes 737288 | tf_op jit(solution)/shard_map/ppermute | solution.py:98
  233.5 47.1 %collective-permute-start.6 = (bf16[160,768]{1,0:T(8,128)(2,1)S(1)}, bf16[160,768]{1,0:T(8,128)(2,1)S(1)}, u32[]{:S(2)}, u32[]{:S(2)}) collective-permute-start(bf16[160,768]{1,0:T(8,128)(2,1)S(1)} %get-tuple-element.55), channel_id=1, source_target_pairs={{0,2},{1,3},{2,0},{3,1},{4,6},{5,7},{6,4},{7,5},{8,10},{9,11},{10,... | collective-permute-start | bytes 737288 | tf_op jit(solution)/shard_map/ppermute | solution.py:98
  236.4 44.2 %collective-permute-start.8 = (bf16[160,768]{1,0:T(8,128)(2,1)S(1)}, bf16[160,768]{1,0:T(8,128)(2,1)S(1)}, u32[]{:S(2)}, u32[]{:S(2)}) collective-permute-start(bf16[160,768]{1,0:T(8,128)(2,1)S(1)} %get-tuple-element.57), channel_id=1, source_target_pairs={{0,3},{1,0},{2,1},{3,2},{4,7},{5,4},{6,5},{7,6},{8,11},{9,8},{10,9... | collective-permute-start | bytes 737288 | tf_op jit(solution)/shard_map/ppermute | solution.py:98
  265.1 15.5 %collective-permute-start.3 = (bf16[160,768]{1,0:T(8,128)(2,1)S(1)}, bf16[160,768]{1,0:T(8,128)(2,1)S(1)}, u32[]{:S(2)}, u32[]{:S(2)}) collective-permute-start(bf16[160,768]{1,0:T(8,128)(2,1)S(1)} %get-tuple-element.52), channel_id=1, source_target_pairs={{0,1},{1,2},{2,3},{3,0},{4,5},{5,6},{6,7},{7,4},{8,9},{9,10},{10,1... | collective-permute-start | bytes 737288 | tf_op jit(solution)/shard_map/ppermute | solution.py:98
  265.1 26.3 %collective-permute-start.5 = (bf16[160,768]{1,0:T(8,128)(2,1)S(1)}, bf16[160,768]{1,0:T(8,128)(2,1)S(1)}, u32[]{:S(2)}, u32[]{:S(2)}) collective-permute-start(bf16[160,768]{1,0:T(8,128)(2,1)S(1)} %get-tuple-element.54), channel_id=1, source_target_pairs={{0,2},{1,3},{2,0},{3,1},{4,6},{5,7},{6,4},{7,5},{8,10},{9,11},{10,... | collective-permute-start | bytes 737288 | tf_op jit(solution)/shard_map/ppermute | solution.py:98
  266.1 25.3 %collective-permute-start.7 = (bf16[160,768]{1,0:T(8,128)(2,1)S(1)}, bf16[160,768]{1,0:T(8,128)(2,1)S(1)}, u32[]{:S(2)}, u32[]{:S(2)}) collective-permute-start(bf16[160,768]{1,0:T(8,128)(2,1)S(1)} %get-tuple-element.56), channel_id=1, source_target_pairs={{0,3},{1,0},{2,1},{3,2},{4,7},{5,4},{6,5},{7,6},{8,11},{9,8},{10,9... | collective-permute-start | bytes 737288 | tf_op jit(solution)/shard_map/ppermute | solution.py:98
Sparse Core Ops, SparseCore 0:
  143.3 130.1 reduce-scatter.7
  279.2 101.1 reduce-scatter.9
  387.0 113.2 reduce-scatter.5

commit v3 on v2

--- a/solution.py
+++ b/solution.py
@@ -85,21 +85,6 @@
         out_specs=vmem(1)[0],
         compiler_params=params(32),
     )(jnp.reshape(band, (1,)), *parts).reshape(band_rows, items, width)
-
-
-def band_start(band, shift, bands, band_rows):
-    return pl.multiple_of(lax.rem(band + shift + bands, bands) * band_rows, band_rows)
-
-
-def exchange(parts, bands, per, item):
-    kept = [parts[item]]
-    for shift in range(1, bands):
-        kept.append(
-            lax.ppermute(
-                parts[shift * per + item], "band", [(i, (i + shift) % bands) for i in range(bands)]
-            )
-        )
-    return kept
 
 
 def rope(vector, cos, sin):
@@ -250,11 +235,14 @@
     def other(self, shift):
         return lax.rem(self.band + shift + self.bands, self.bands)
 
-    def greet(self):
+    def greet(self, axis=0):
         barrier = pltpu.get_barrier_semaphore()
-        for shift in range(1, self.bands):
-            pl.semaphore_signal(barrier, inc=1, device_id=(self.items, self.other(shift)), device_id_type=MESH)
-        pl.semaphore_wait(barrier, self.bands - 1)
+        others = [(self.items, self.other(shift)) for shift in range(1, self.bands)]
+        if axis:
+            others += [(flipped(self.items, at), self.band) for at in range(log2_of(axis))]
+        for other in others:
+            pl.semaphore_signal(barrier, inc=1, device_id=other, device_id_type=MESH)
+        pl.semaphore_wait(barrier, len(others))
 
     def remote(self, source, target, arrival, device):
         ends = []
@@ -425,21 +413,16 @@
     )
 
 
-def back_kernel(bands, follows, scalars, *refs):
-    x, grad_resid, grad_attended, attended, query, key, value, log_total, w_query, w_key, w_value = refs[:11]
-    gain, cos, sin = refs[11:14]
-    refs = refs[14:]
-    prev = None
-    if follows:
-        prev, refs = refs[:2], refs[2:]
-    outs, refs = refs[:bands], refs[bands:]
-    g_weights, g_norm, grads, normed_t, back = refs
+def back_item(
+    follows, length, x, grad_resid, grad_attended, attended, query, key, value, log_total, weights, gain, cos, sin,
+    g_weights, g_norm, grads, normed_t, back, tick,
+):
+    w_query, w_key, w_value = weights
     seq, width = x.shape
-    band_rows = seq // bands
-    band, length = scalars[0], scalars[1]
     blocks = query_blocks(seq)
 
     def head(at, _):
+        tick(at)
         for which in range(2):
             number = at * 2 + which
             rows = pl.ds(pl.multiple_of(number * HEAD_DIM, HEAD_DIM), HEAD_DIM)
@@ -492,7 +475,7 @@
             grad = dot_nt(normed_t[rows, :], grads[part * width : (part + 1) * width, :])
             columns = slice(part * width, (part + 1) * width)
             if follows:
-                grad += prev[0][rows, columns].astype(F32)
+                grad += g_weights[rows, columns].astype(F32)
             g_weights[rows, columns] = grad.astype(LOW)
     norm_sum = jnp.zeros((1, width), F32)
     for at in range(0, seq, tile):
@@ -502,38 +485,311 @@
         scaled = inputs * inv
         norm_sum += jnp.sum(incoming * scaled, 0, keepdims=True)
         weighted = incoming * gain[...]
-        back[rows, :] = grad_resid[rows, :].astype(F32) + inv * (
+        grad = grad_resid[rows, :].astype(F32) + inv * (
             weighted - scaled * jnp.mean(weighted * scaled, -1, keepdims=True)
         )
-    if follows:
-        norm_sum += prev[1][...]
-    g_norm[...] = norm_sum
-    for shift, out in enumerate(outs):
-        out[...] = back[pl.ds(band_start(band, shift, bands, band_rows), band_rows), :].astype(LOW)
-
-
-def back_attend(bands, scalars, x, grad_resid, grad_attended_t, attended_t, query, key, value, log_total, weights, gain, cos, sin, prev):
-    seq, width = x.shape
-    band_rows = seq // bands
-    pairs = seq * seq * width
-    args = [x, grad_resid, grad_attended_t, attended_t, query, key, value, log_total, *weights, gain, cos, sin, *(prev or ())]
+        grad_resid[rows, :] = grad.astype(LOW)
+    g_norm[...] = g_norm[...] + norm_sum if follows else norm_sum
+
+
+def bit(number, at):
+    return lax.rem(lax.div(number, 2**at), 2)
+
+
+def flipped(number, at):
+    return number + (1 - 2 * bit(number, at)) * 2**at
+
+
+def replaced(number, bits, choice):
+    for order, at in enumerate(bits):
+        number = number + ((choice >> order & 1) - bit(number, at)) * 2**at
+    return number
+
+
+def sum_orders(axis):
+    later = list(range(1, log2_of(axis)))
+    return [0] + later, [0] + later[::-1]
+
+
+def sum_lanes(axis, stage, columns):
+    left, right = sum_orders(axis)
+    half = columns // 2
+    if stage == 0:
+        return [(left[0], left[1:], 0, columns)]
+    return [(left[stage], left[stage + 1 :], 0, half), (right[stage], right[stage + 1 :], half, half)]
+
+
+def band_shape(axis, bands, shape):
+    rows = shape[0] // axis // bands
+    return (rows, shape[1]) if rows % 16 == 0 else (2 * rows, shape[1] // 2)
+
+
+def sum_scratch(axis, bands, shape):
+    low = lambda *dims: pltpu.VMEM(dims, LOW)
+    out = []
+    for stage in range(log2_of(axis)):
+        for _, bits, _, columns in sum_lanes(axis, stage, shape[1]):
+            out.append(low(2 ** len(bits), shape[0] // axis, columns))
+    part = band_shape(axis, bands, shape)
+    out.append(low(bands, *part))
+    for stage in range(log2_of(bands)):
+        out.append(low(bands >> stage + 1, *part))
+    return out
+
+
+def sum_links(axis, bands):
+    return axis // 2 + 2 * (axis // 2 - 1) + bands - 1
+
+
+class Summing:
+    def __init__(self, copies, axis, arrays, scratch, outs):
+        self.copies, self.axis, self.arrays, self.outs = copies, axis, arrays, outs
+        self.count = log2_of(axis)
+        self.stages = self.count + log2_of(copies.bands)
+        each = len(scratch) // len(arrays)
+        self.scratch = [list(scratch[at * each : (at + 1) * each]) for at in range(len(arrays))]
+        self.flights = {}
+        self.sent = []
+
+    def buffers(self, at, stage):
+        taken = self.scratch[at]
+        if stage < self.count:
+            first = 0 if stage == 0 else 2 * stage - 1
+            return taken[first : first + (1 if stage == 0 else 2)]
+        return taken[2 * self.count + stage - self.count : 2 * self.count + stage - self.count + 1]
+
+    def piece(self, array, number, first, columns):
+        rows = array.shape[0] // self.axis
+        return array.at[pl.ds(pl.multiple_of(number * rows, rows), rows), pl.ds(first, columns)]
+
+    def begin(self, stage):
+        me, band = self.copies.items, self.copies.band
+        flights = []
+        for at, array in enumerate(self.arrays):
+            if stage < self.count:
+                lanes = sum_lanes(self.axis, stage, array.shape[1])
+                for (axis_bit, bits, first, columns), came in zip(lanes, self.buffers(at, stage)):
+                    other = flipped(me, axis_bit)
+                    for choice in range(2 ** len(bits)):
+                        sent = self.piece(array, replaced(other, bits, choice), first, columns)
+                        kept = self.piece(array, replaced(me, bits, choice), first, columns)
+                        links = self.copies.remote(sent, came.at[choice], came.at[choice], (other, band))
+                        flights.append((links, kept, came.at[choice]))
+            else:
+                band_bit = stage - self.count
+                bits = list(range(band_bit + 1, log2_of(self.copies.bands)))
+                parts, came = self.scratch[at][2 * self.count - 1], self.buffers(at, stage)[0]
+                other = flipped(band, band_bit)
+                for choice in range(2 ** len(bits)):
+                    sent, kept = parts.at[replaced(other, bits, choice)], parts.at[replaced(band, bits, choice)]
+                    links = self.copies.remote(sent, came.at[choice], came.at[choice], (me, other))
+                    flights.append((links, kept, came.at[choice]))
+        self.flights[stage] = flights
+        self.sent += [links[0] for links, _, _ in flights]
+
+    def end(self, stage):
+        for links, _, _ in self.flights[stage]:
+            links[1].wait_recv()
+        last = stage == self.stages - 1
+        for at, (_, kept, came) in enumerate(self.flights[stage]):
+            if last:
+                total = kept[...].astype(F32) + came[...].astype(F32)
+                out = self.outs[at]
+                rows, half = out.shape[0], total.shape[1]
+                if total.shape[0] == rows:
+                    out[...] = total
+                else:
+                    out[:, :half] = total[:rows]
+                    out[:, half:] = total[rows:]
+                continue
+            tile = 16
+
+            def add(step, _, kept=kept, came=came):
+                rows = pl.ds(pl.multiple_of(step * tile, tile), tile)
+                kept[rows, :] = (kept[rows, :].astype(F32) + came[rows, :].astype(F32)).astype(LOW)
+                return 0
+
+            lax.fori_loop(0, kept.shape[0] // tile, add, 0)
+        if stage == self.count - 1:
+            self.stack()
+
+    def stack(self):
+        bands = self.copies.bands
+        for at, array in enumerate(self.arrays):
+            parts = self.scratch[at][2 * self.count - 1]
+            whole = self.piece(array, self.copies.items, 0, array.shape[1])
+            rows = whole.shape[0] // bands
+            if parts.shape[1] == rows:
+                for number in range(bands):
+                    parts[number] = whole[number * rows : (number + 1) * rows, :]
+                continue
+            half = array.shape[1] // 2
+            left, right = whole[:, :half].astype(F32), whole[:, half:].astype(F32)
+            for number in range(bands):
+                span = slice(number * rows, (number + 1) * rows)
+                parts[number] = jnp.concatenate([left[span], right[span]], 0).astype(LOW)
+
+    def close(self):
+        for link in self.sent:
+            link.wait_send()
+
+
+def rear_kernel(
+    bands, per, axis, lengths, gain, cos, sin, log_total, g_norm_ffn, *refs
+):
+    fused = axis > 0
+    x_from, query_from, key_from, value_from, attended_t_from, grad_resid_from, grad_attended_t_from = refs[:7]
+    out_last, w_query_from, w_key_from, w_value_from, *g_feed_from = refs[7:15]
+    refs = refs[15:]
+    home_last, home_grad, *outs = refs[: 2 + (6 if fused else 2)]
+    refs = refs[2 + (6 if fused else 2) :]
+    x, query, key, value, attended_t, grad_resid, grad_attended_t, w_query, w_key, w_value = refs[:10]
+    g_weights, grads, normed_t, back, g_norm, local, send, receive = refs[10:18]
+    refs = refs[18:]
+    seq, width = x.shape[1:]
+    band_rows, items = seq // bands, bands * per
+    copies = Copies(local, send, receive, bands)
+    band = copies.band
+    loads = []
+    for item in range(per):
+        loads.append(
+            [
+                copies.start(source.at[item], target.at[item])
+                for source, target in (
+                    (query_from, query), (key_from, key), (value_from, value), (attended_t_from, attended_t),
+                    (grad_attended_t_from, grad_attended_t), (x_from, x), (grad_resid_from, grad_resid),
+                )
+            ]
+        )
+        if item == 0:
+            loads[0] += [
+                copies.start(w_query_from, w_query), copies.start(w_key_from, w_key), copies.start(w_value_from, w_value)
+            ]
+            if fused:
+                g_feed = refs[:4]
+                feed_loads = [copies.start(a, b) for a, b in zip(g_feed_from, g_feed)]
+    copies.greet(axis)
+    if fused:
+        each = len(sum_scratch(axis, bands, (axis * bands * 16, 256)))
+        feed_sum = Summing(copies, axis, g_feed, refs[4 : 4 + 4 * each], outs[:4])
+        rest_sum = Summing(copies, axis, [g_weights], refs[4 + 4 * each :], outs[4:5])
+
+    def own_rows(shift):
+        return pl.ds(pl.multiple_of(copies.other(shift) * band_rows, band_rows), band_rows)
+
+    def go_home(source, home, slots, item):
+        kept = copies.start(source.at[own_rows(0)], home.at[item])
+        links = []
+        for shift in range(1, bands):
+            slot = home.at[shift * slots + item]
+            links.append(
+                copies.remote(source.at[own_rows(shift)], slot, slot, (copies.items, copies.other(shift)))
+            )
+        return kept, links
+
+    flights = [go_home(out_last, home_last, 1, 0)]
+    if fused:
+        for load in feed_loads:
+            load.wait()
+        feed_sum.begin(0)
+    for item in range(per):
+        for load in loads[item]:
+            load.wait()
+
+        def tick(at, item=item):
+            if not fused:
+                return
+            for place, action in progress.get(item, {}).items():
+                pl.when(at == place)(action)
+
+        progress = {}
+        back_item(
+            item > 0, lengths[band * per + item], x.at[item], grad_resid.at[item], grad_attended_t.at[item],
+            attended_t.at[item], query.at[item], key.at[item], value.at[item], log_total.at[item],
+            (w_query, w_key, w_value), gain, cos, sin, g_weights, g_norm, grads, normed_t, back, tick,
+        )
+        flights.append(go_home(grad_resid.at[item], home_grad, per, item))
+        if fused and item < per - 1:
+            feed_sum.end(item)
+            feed_sum.begin(item + 1)
+    if fused:
+        lanes = 128
+        pad = jnp.zeros((lanes - 1, width), F32)
+        for at, sums in enumerate((g_norm, g_norm_ffn)):
+            spread = jnp.concatenate([sums[...], pad], 0).T
+            g_weights[:, 3 * width + at * lanes : 3 * width + (at + 1) * lanes] = spread.astype(LOW)
+        rest_sum.begin(0)
+        begun = per - 1
+        for stage in range(rest_sum.stages):
+            if begun < feed_sum.stages:
+                feed_sum.end(begun)
+                begun += 1
+                if begun < feed_sum.stages:
+                    feed_sum.begin(begun)
+            rest_sum.end(stage)
+            if stage + 1 < rest_sum.stages:
+                rest_sum.begin(stage + 1)
+        while begun < feed_sum.stages:
+            feed_sum.end(begun)
+            begun += 1
+            if begun < feed_sum.stages:
+                feed_sum.begin(begun)
+        feed_sum.close()
+        rest_sum.close()
+    else:
+        outs[0][...] = g_weights[...]
+        outs[1][...] = g_norm[...]
+    for kept, links in flights:
+        kept.wait()
+        for started, arrival in links:
+            started.wait_send()
+            arrival.wait_recv()
+
+
+def rear(bands, axis, lengths, gain, tables, kept, out_last, weights, g_feed, g_norm_ffn):
+    x, query, key, value, attended_t, log_total, grad_resid, grad_attended_t = kept
+    per, seq, width = x.shape
+    band_rows, items = seq // bands, bands * per
+    fused = axis > 0
+    low = lambda *shape: jax.ShapeDtypeStruct(shape, LOW)
+    scratch = lambda *shape: pltpu.VMEM(shape, LOW)
+    outside = pl.BlockSpec(memory_space=pl.ANY)
+    inside = pl.BlockSpec(memory_space=pltpu.VMEM)
+    rest = (width, 3 * width + 256) if fused else (width, 3 * width)
+    out_shape = [low(bands, band_rows, width), low(items, band_rows, width)]
+    sums = []
+    links = 3 * (bands - 1) * (per + 1)
+    if fused:
+        shapes = [g.shape for g in g_feed] + [rest]
+        out_shape += [jax.ShapeDtypeStruct((s[0] // axis // bands, s[1]), F32) for s in shapes]
+        out_shape += [jax.ShapeDtypeStruct((1, width), F32)]
+        sums = [scratch(*s) for s in shapes[:-1]]
+        for shape in shapes:
+            sums += sum_scratch(axis, bands, shape)
+        links += len(shapes) * sum_links(axis, bands)
+    else:
+        out_shape += [low(*rest), jax.ShapeDtypeStruct((1, width), F32)]
+    local = 8 * per + 3 + 4 + per + 1
     return pl.pallas_call(
-        functools.partial(back_kernel, bands, prev is not None),
-        name="back_attend",
-        out_shape=[jax.ShapeDtypeStruct((band_rows, width), LOW)] * bands
-        + [jax.ShapeDtypeStruct((width, 3 * width), LOW), jax.ShapeDtypeStruct((1, width), F32)],
-        in_specs=[smem()] + vmem(len(args)),
-        out_specs=vmem(bands + 2),
+        functools.partial(rear_kernel, bands, per, axis),
+        name="rear",
+        out_shape=out_shape,
+        in_specs=[smem()] + [inside] * 5 + [outside] * 15,
+        out_specs=[outside] * 2 + [inside] * (len(out_shape) - 2),
         scratch_shapes=[
-            pltpu.VMEM((3 * width, seq), LOW),
-            pltpu.VMEM((width, seq), LOW),
-            pltpu.VMEM((seq, width), F32),
-        ],
-        compiler_params=params(48),
-        cost_estimate=pl.CostEstimate(
-            flops=12 * seq * width * width + 30 * pairs, bytes_accessed=24 * seq * width, transcendentals=0
-        ),
-    )(scalars, *args)
+            scratch(per, seq, width), scratch(per, width, seq), scratch(per, width, seq), scratch(per, width, seq),
+            scratch(per, width, seq), scratch(per, seq, width), scratch(per, width, seq),
+            scratch(width, width), scratch(width, width), scratch(width, width),
+            scratch(*rest), scratch(3 * width, seq), scratch(width, seq), pltpu.VMEM((seq, width), F32),
+            pltpu.VMEM((1, width), F32),
+            pltpu.SemaphoreType.DMA((local,)), pltpu.SemaphoreType.DMA((links,)), pltpu.SemaphoreType.DMA((links,)),
+        ]
+        + sums,
+        compiler_params=pltpu.CompilerParams(vmem_limit_bytes=62 * 2**20, collective_id=1, has_side_effects=True),
+    )(
+        lengths, gain, *tables, log_total, g_norm_ffn, x, query, key, value, attended_t, grad_resid, grad_attended_t,
+        out_last, *weights, *g_feed,
+    )
 
 
 def rope_tables(seq):
@@ -544,6 +800,7 @@
 
 def per_device(
     bands,
+    axis,
     tokens,
     lengths,
     norm_attn,
@@ -563,10 +820,6 @@
     band = lax.axis_index("band")
     cos, sin = rope_tables(seq)
     gain_attn, gain_ffn = norm_attn.reshape(1, width), norm_ffn.reshape(1, width)
-    scalars = [
-        jnp.stack([band, lax.dynamic_index_in_dim(lengths, band * per + item, keepdims=False)]).astype(jnp.int32)
-        for item in range(per)
-    ]
     (
         x, query, key, value, attended_t, log_total, grad_resid, grad_attended_t, out_last, home_early,
         g_gate, g_up, g_down, g_out, g_norm_ffn,
@@ -574,47 +827,38 @@
         bands, lengths, tokens, cotangent, (gain_attn, gain_ffn), (cos, sin),
         (w_query, w_key, w_value, w_out, w_gate, w_up, w_down),
     )
-    backs, prev = [], None
-    for i in range(per):
-        backs.append(
-            back_attend(
-                bands, scalars[i], x[i], grad_resid[i], grad_attended_t[i], attended_t[i], query[i], key[i], value[i], log_total[i],
-                (w_query, w_key, w_value), gain_attn, cos, sin, prev,
-            )
-        )
-        prev = backs[-1][bands:]
-    g_weights, g_norm_attn = prev
-
-    def home(parts):
-        came = [exchange([parts[i][k] for k in range(bands)], bands, 1, 0) for i in range(per)]
-        return merge_items([came[j][k] for k in range(bands) for j in range(per)], band, bands)
-
-    def last_part(shift):
-        return lax.dynamic_slice_in_dim(out_last, band_start(band, shift, bands, band_rows), band_rows, 0)
-
-    came = exchange([last_part(k) for k in range(bands)], bands, 1, 0)
-    early = [[home_early[k * (per - 1) + j] for j in range(per - 1)] for k in range(bands)]
-    output = merge_items([part for k in range(bands) for part in early[k] + [came[k]]], band, bands)
-    grad_tokens = home([b[:bands] for b in backs])
-    axes = ("items", "band")
-    gains = jnp.concatenate([g_norm_attn.T, g_norm_ffn.T], 1)
-    feed_sum = lax.psum_scatter(jnp.concatenate([g_gate, g_up], 1), axes, scatter_dimension=0, tiled=True).astype(F32)
-    down_sum = lax.psum_scatter(g_down, axes, scatter_dimension=0, tiled=True).astype(F32)
-    rest = jnp.concatenate([g_weights, g_out, gains.astype(LOW)], 1)
-    rest_sum = lax.psum_scatter(rest, axes, scatter_dimension=0, tiled=True).astype(F32)
-    ff = w_gate.shape[1]
+    fused = axis if width // axis % 16 == 0 and w_gate.shape[1] // axis % 16 == 0 else 0
+    home_last, home_grad, *sums = rear(
+        bands, fused, lengths, gain_attn, (cos, sin),
+        (x, query, key, value, attended_t, log_total, grad_resid, grad_attended_t),
+        out_last, (w_query, w_key, w_value), (g_gate, g_up, g_down, g_out), g_norm_ffn,
+    )
+    ahead = per - 1
+    output = [home_early[k * ahead + j] if j < ahead else home_last[k] for k in range(bands) for j in range(per)]
+    output = merge_items(output, band, bands)
+    grad_tokens = merge_items([home_grad[at] for at in range(items)], band, bands)
+    if fused:
+        g_gate, g_up, g_down, g_out, rest = sums[:5]
+        g_norm_attn, g_norm_ffn = rest[:, 3 * width], rest[:, 3 * width + 128]
+        g_weights = rest[:, : 3 * width]
+    else:
+        axes = ("items", "band")
+        total = lambda a: lax.psum_scatter(a, axes, scatter_dimension=0, tiled=True).astype(F32)
+        norms = total(jnp.concatenate([sums[1].T, g_norm_ffn.T], 1))
+        g_norm_attn, g_norm_ffn = norms[:, 0], norms[:, 1]
+        g_gate, g_up, g_down, g_out, g_weights = (total(a) for a in (g_gate, g_up, g_down, g_out, sums[0]))
     return (
         output,
         grad_tokens,
-        rest_sum[:, 4 * width],
-        rest_sum[:, :width],
-        rest_sum[:, width : 2 * width],
-        rest_sum[:, 2 * width : 3 * width],
-        rest_sum[:, 3 * width : 4 * width],
-        rest_sum[:, 4 * width + 1],
-        feed_sum[:, :ff],
-        feed_sum[:, ff:],
-        down_sum,
+        g_norm_attn,
+        g_weights[:, :width],
+        g_weights[:, width : 2 * width],
+        g_weights[:, 2 * width : 3 * width],
+        g_out,
+        g_norm_ffn,
+        g_gate,
+        g_up,
+        g_down,
     )
 
 
@@ -623,7 +867,7 @@
     rows = P(("items", "band"), None)
     flat = P(("items", "band"))
     return jax.shard_map(
-        functools.partial(per_device, mesh.shape["band"]),
+        functools.partial(per_device, mesh.shape["band"], mesh.shape["items"]),
         mesh=mesh,
         in_specs=(split, P("items")) + (P(),) * 9 + (split,),
         out_specs=(split, split, flat, rows, rows, rows, rows, flat, rows, rows, rows),

time: 512 us -> 271 us (0.53)
  waiting for transfers between devices: 249 us -> 0 us
  Pallas kernels: 187 us -> 258 us
  starting transfers between devices: 21.8 us -> 0 us
  local copies, waits for them, and re-layouts: 26.9 us -> 8.7 us
  between operations: 14.2 us -> 0.99 us
  other arithmetic: 10.2 us -> 0 us
    reduce_scatter x2 -> x0, waiting for transfers between devices: 117 us -> none  [the longest x1 117 us: per_device(): lax.psum_scatter(jnp.concatenate([g_gate, g_up], 1), axes, scatter_dimens...]
    unnamed x4 -> x0, waiting for transfers between devices: 85.5 us -> none
    pallas_call x2 -> x1, Pallas kernels: 49.4 us -> 121 us  [rear(): pl.pallas_call(functools.partial(rear_kernel, bands, per, axis), name='re...]
    ppermute x9 -> x0, waiting for transfers between devices: 46.8 us -> none  [exchange(): lax.ppermute(parts[shift * per + item], 'band', [(i, (i + shift) % bands)...]
    ppermute x9 -> x0, starting transfers between devices: 21.5 us -> none  [exchange(): lax.ppermute(parts[shift * per + item], 'band', [(i, (i + shift) % bands)...]
    concatenate x1 -> x0, local copies, waits for them, and re-layouts: 7.94 us -> none  [per_device(): rest = jnp.concatenate([g_weights, g_out, gains.astype(LOW)], 1)]
    concatenate x1 -> x0, other arithmetic: 6.31 us -> none  [per_device(): jnp.concatenate([g_gate, g_up], 1)]
  transfers between devices with their start and end apart: 12 -> 0, of which waited for: 6 -> 0; matrix products, arithmetic and copies ran while one was open for 6% -> 0% of each run, Pallas kernels for 10% -> 0%
where the time goes in v3:
time: 271 us; the launch traced here: 268 us
  Pallas kernels  258 us (95%)
  local copies, waits for them, and re-layouts  8.7 us (3%)
    pallas_call x1, Pallas kernels, front(): pl.pallas_call(functools.partial(front_kernel, bands, per), name='front',...  134 us
    pallas_call x1, Pallas kernels, rear(): pl.pallas_call(functools.partial(rear_kernel, bands, per, axis), name='re...  121 us

profile of v3, /device:TPU:0, one launch (start us, length us, event | category | flops | bytes accessed | tf_op | source)
XLA Modules:
  0.0 267.9 jit_solution(15556483209304623687)
XLA Ops:
  0.6 1.3 reshape.47.gain_attn.gain
  1.9 1.3 reshape.48.gain_ffn
  3.2 133.5 %front.1 = (bf16[2,640,768]{2,1,0:T(8,128)(2,1)}, bf16[2,768,640]{2,1,0:T(8,128)(2,1)}, bf16[2,768,640]{2,1,0:T(8,128)(2,1)}, bf16[2,768,640]{2,1,0:T(8,128)(2,1...) custom-call(s32[8]{0:T(128)} %lengths.3, ...), custom_call_target="tpu_custom_call" | custom-call | tf_op jit(solution)/shard_map/front/pallas_call | solution.py:389
  136.7 120.7 %rear.1 = (bf16[4,160,768]{2,1,0:T(8,128)(2,1)}, bf16[8,160,768]{2,1,0:T(8,128)(2,1)}, f32[24,2048]{1,0:T(8,128)}, f32[24,2048]{1,0:T(8,128)}, f32[64,768]{1,0:T...) custom-call(s32[8]{0:T(128)} %lengths.3, f32[1,768]{1,0:T(1,128)} %reshape.47.gain_attn.gain, ...), custom_call_target="tpu_custom_call" | custom-call | tf_op jit(solution)/shard_map/rear/pallas_call | solution.py:773
  257.4 2.1 slice_bitcast_fusion
  259.5 0.0 copy-start
  259.6 2.0 merge_items.3
  261.5 0.0 copy-done
  261.5 0.1 slice_bitcast_fusion.9
  261.6 0.0 copy-start.1
  261.6 0.0 copy-start.5
  261.6 0.0 copy-start.4
  261.6 0.0 copy-start.3
  261.6 0.0 copy-start.2
  261.6 2.0 merge_items.2
  263.6 0.0 copy-done.1
  263.6 0.7 fusion
  264.3 0.6 slice_reduce_fusion
  264.9 0.0 copy-done.5
  264.9 0.6 copy.29
  265.5 0.0 copy-done.4
  265.5 0.7 copy.30
  266.2 0.0 copy-done.3
  266.2 0.7 copy.31
  266.9 0.0 copy-done.2
  266.9 0.7 copy.32
Async XLA Ops:
  259.5 2.0 copy-start
  261.6 2.0 copy-start.1
  261.6 3.3 %copy-start.5 = (f32[24,768]{1,0:T(8,128)S(1)}, f32[24,768]{1,0:T(8,128)}, u32[]{:S(2)}) copy-start(f32[24,768]{1,0:T(8,128)} %get-tuple-element.97) | copy-start | bytes 221188
  261.6 3.9 %copy-start.4 = (f32[24,2048]{1,0:T(8,128)S(1)}, f32[24,2048]{1,0:T(8,128)}, u32[]{:S(2)}) copy-start(f32[24,2048]{1,0:T(8,128)} %get-tuple-element.99) | copy-start | bytes 589828
  261.6 4.6 %copy-start.3 = (f32[24,2048]{1,0:T(8,128)S(1)}, f32[24,2048]{1,0:T(8,128)}, u32[]{:S(2)}) copy-start(f32[24,2048]{1,0:T(8,128)} %get-tuple-element.100) | copy-start | bytes 589828
  261.6 5.3 %copy-start.2 = (f32[64,768]{1,0:T(8,128)S(1)}, f32[64,768]{1,0:T(8,128)}, u32[]{:S(2)}) copy-start(f32[64,768]{1,0:T(8,128)} %get-tuple-element.101) | copy-start | bytes 589828

commit v4 on v2

v4 whole, which is shorter than its diff:
```python
import functools

import jax
import jax.numpy as jnp
import numpy as np
from jax import lax
from jax.experimental import pallas as pl
from jax.experimental.pallas import tpu as pltpu
from jax.sharding import PartitionSpec as P

HEAD_DIM = 64
HALF = HEAD_DIM // 2
EPS = 1e-05
NEG = -1e30
ROPE_BASE = 10000.0
LOG2E = 1.4426950408889634
SCALE = HEAD_DIM**-0.5
BLOCK = 256
F32 = jnp.float32
LOW = jnp.bfloat16
MESH = pl.DeviceIdType.MESH


def dot_nn(left, right):
    return lax.dot_general(left, right, (((1,), (0,)), ((), ())), preferred_element_type=F32)


def dot_nt(left, right):
    return lax.dot_general(left, right, (((1,), (1,)), ((), ())), preferred_element_type=F32)


def dot_tn(left, right):
    return lax.dot_general(left, right, (((0,), (0,)), ((), ())), preferred_element_type=F32)


def vmem(count):
    return [pl.BlockSpec(memory_space=pltpu.VMEM)] * count


def smem():
    return pl.BlockSpec(memory_space=pltpu.SMEM)


def params(mib):
    return pltpu.CompilerParams(vmem_limit_bytes=mib * 2**20)


def log2_of(number):
    return number.bit_length() - 1


def split_order(items, chunk, first):
    size = items * chunk
    row = lax.broadcasted_iota(jnp.int32, (size, size), 0)
    col = lax.broadcasted_iota(jnp.int32, (size, size), 1)
    item = (row >> log2_of(chunk)) + first
    item = jnp.where(item >= items, item - items, item)
    return jnp.where(col == (row & (chunk - 1)) * items + item, 1.0, 0.0).astype(LOW)


def merge_kernel(items, per, chunk, band_ref, *refs):
    ins, out = refs[:-1], refs[-1]
    size, bands = items * chunk, items // per
    row = lax.broadcasted_iota(jnp.int32, (size, size), 0)
    col = lax.broadcasted_iota(jnp.int32, (size, size), 1)
    number = col >> log2_of(chunk)
    source = band_ref[0] - (number >> log2_of(per))
    source = jnp.where(source < 0, source + bands, source)
    item = source * per + (number & (per - 1))
    order = jnp.where(row == (col & (chunk - 1)) * items + item, 1.0, 0.0).astype(LOW)
    for block in range(out.shape[0] // size):
        parts = jnp.concatenate([part[block * chunk : (block + 1) * chunk, :] for part in ins], 0)
        out[block * size : (block + 1) * size, :] = dot_nn(order, parts).astype(LOW)


def merge_items(parts, band, bands):
    items = len(parts)
    band_rows, width = parts[0].shape
    chunk = 32 if band_rows % 32 == 0 else 16
    return pl.pallas_call(
        functools.partial(merge_kernel, items, items // bands, chunk),
        name="merge_items",
        out_shape=jax.ShapeDtypeStruct((band_rows * items, width), LOW),
        in_specs=[smem()] + vmem(items),
        out_specs=vmem(1)[0],
        compiler_params=params(32),
    )(jnp.reshape(band, (1,)), *parts).reshape(band_rows, items, width)


def rope(vector, cos, sin):
    parts = []
    for at in range(0, vector.shape[0], HEAD_DIM):
        lower, upper = vector[at : at + HALF], vector[at + HALF : at + HEAD_DIM]
        parts += [lower * cos - upper * sin, lower * sin + upper * cos]
    return jnp.concatenate(parts, 0)


def query_blocks(seq):
    return [(start, min(start + BLOCK, seq)) for start in range(0, seq, BLOCK)]


def limits(start, stop, length):
    position = start + lax.broadcasted_iota(jnp.int32, (1, stop - start), 1)
    return jnp.minimum(position, length - 1)


def score_parts(keys, queries, start, stop, length):
    parts = []
    if start:
        parts.append((0, BLOCK, dot_tn(keys[:, :BLOCK], queries)))
    first = min(start, BLOCK)
    late = dot_tn(keys[:, first:stop], queries)
    position = first + lax.broadcasted_iota(jnp.int32, late.shape, 0)
    late = jnp.where(position <= limits(start, stop, length), late, NEG)
    parts.append((first, stop, late))
    return parts


def norm_rows(inputs):
    return lax.rsqrt(jnp.mean(inputs * inputs, -1, keepdims=True) + EPS)


def attend_item(length, x, weights, gain, cos, sin, query, key, value, attended_t, attended, log_total, normed, ready):
    seq, width = x.shape
    tile = 128
    for at in range(0, seq, tile):
        inputs = x[at : at + tile, :].astype(F32)
        normed[at : at + tile, :] = (inputs * norm_rows(inputs) * gain).astype(LOW)

    project = 256

    def project_tile(at, _):
        rows = pl.ds(pl.multiple_of(at * project, project), project)
        for part, out, scaled in ((0, query, SCALE * LOG2E), (1, key, 1.0)):
            source = pl.ds(pl.multiple_of(part * width + at * project, project), project)
            out[rows, :] = (rope(dot_nt(weights[source, :], normed[...]), cos[...], sin[...]) * scaled).astype(LOW)
        source = pl.ds(pl.multiple_of(2 * width + at * project, project), project)
        value[rows, :] = dot_nt(weights[source, :], normed[...]).astype(LOW)
        return 0

    lax.fori_loop(0, width // project, project_tile, 0)
    ready()

    def head(at, _):
        for which in range(2):
            number = at * 2 + which
            rows = pl.ds(pl.multiple_of(number * HEAD_DIM, HEAD_DIM), HEAD_DIM)
            keys, values = key[rows, :], value[rows, :]
            for start, stop in query_blocks(seq):
                parts = score_parts(keys, query[rows, start:stop], start, stop, length)
                top = functools.reduce(jnp.maximum, [jnp.max(s, 0, keepdims=True) for _, _, s in parts])
                total = jnp.zeros_like(top)
                acc = jnp.zeros((HEAD_DIM, stop - start), F32)
                for first, last, scores in parts:
                    prob = jnp.exp2(scores - top)
                    total += jnp.sum(prob, 0, keepdims=True)
                    acc += dot_nn(values[:, first:last], prob.astype(LOW))
                attended_t[rows, start:stop] = (acc / total).astype(LOW)
                log_total[number, :, start:stop] = top + jnp.log2(total)
        return 0

    lax.fori_loop(0, width // HEAD_DIM // 2, head, 0)
    for at in range(0, width, project):
        attended[:, at : at + project] = attended_t[at : at + project, :].T


WIDE = 512


def feed_item(follows, x, attended, attended_t, cot, w_out, w_feed, w_down, gain, g_feed, g_down, g_out, g_norm, out, grad_attended_t, scratch, tick, before_out):
    normed, normed_t, resid, out_acc, back_acc = scratch
    seq, width = x.shape
    ff = w_down.shape[0]
    tile = 128

    def put(ref, at, grad):
        if follows:
            grad += ref[at].astype(F32)
        ref[at] = grad.astype(LOW)

    for at in range(0, seq, tile):
        rows = slice(at, at + tile)
        total = x[rows, :].astype(F32) + dot_nn(attended[rows, :], w_out[...])
        resid[rows, :] = total.astype(LOW)
        out_acc[rows, :] = total
        low = (total * norm_rows(total) * gain).astype(LOW)
        normed[rows, :] = low
        normed_t[:, rows] = low.T
    back_acc[...] = jnp.zeros_like(back_acc)

    def chunk(step, _):
        tick(step)
        span = pl.ds(pl.multiple_of(step * WIDE, WIDE), WIDE)
        up_span = pl.ds(pl.multiple_of(ff + step * WIDE, WIDE), WIDE)
        lows = []
        for at in range(0, seq, seq // 2):
            rows = slice(at, at + seq // 2)
            gate = dot_nn(normed[rows, :], w_feed[:, span])
            upward = dot_nn(normed[rows, :], w_feed[:, up_span])
            grad_hidden = dot_nt(cot[rows, :], w_down[span, :])
            sig = 0.5 * jnp.tanh(0.5 * gate) + 0.5
            silu = gate * sig
            hidden = (silu * upward).astype(LOW)
            grad_gate = (grad_hidden * upward * (sig + silu * (1.0 - sig))).astype(LOW)
            grad_upward = (grad_hidden * silu).astype(LOW)
            out_acc[rows, :] += dot_nn(hidden, w_down[span, :])
            back_acc[rows, :] += dot_nt(grad_gate, w_feed[:, span])
            back_acc[rows, :] += dot_nt(grad_upward, w_feed[:, up_span])
            lows.append((hidden, grad_gate, grad_upward))
        hidden, grad_gate, grad_upward = (jnp.concatenate(parts, 0) for parts in zip(*lows))
        put(g_down, (span, slice(None)), dot_nn(hidden.T, cot[...]))
        first = pl.ds(pl.multiple_of(step * 2 * WIDE, WIDE), WIDE)
        second = pl.ds(pl.multiple_of(step * 2 * WIDE + WIDE, WIDE), WIDE)
        put(g_feed, (slice(None), first), dot_nn(normed_t[...], grad_gate))
        put(g_feed, (slice(None), second), dot_nn(normed_t[...], grad_upward))
        return 0

    lax.fori_loop(0, ff // WIDE, chunk, 0)
    norm_sum = jnp.zeros((1, width), F32)
    for at in range(0, seq, tile):
        rows = slice(at, at + tile)
        out[rows, :] = out_acc[rows, :].astype(LOW)
        total, incoming = resid[rows, :].astype(F32), back_acc[rows, :]
        inv = norm_rows(total)
        scaled = total * inv
        norm_sum += jnp.sum(incoming * scaled, 0, keepdims=True)
        weighted = incoming * gain
        grad = cot[rows, :].astype(F32) + inv * (weighted - scaled * jnp.mean(weighted * scaled, -1, keepdims=True))
        cot[rows, :] = grad.astype(LOW)
    g_norm[...] = g_norm[...] + norm_sum if follows else norm_sum
    grad_attended_t[...] = dot_nt(w_out[...], cot[...]).astype(LOW)
    before_out()
    put(g_out, (slice(None), slice(None)), dot_nn(attended_t[...], cot[...]))


GROUP = 256
PAIRS = GROUP // (2 * HEAD_DIM)


def back_item(
    follows, length, x, grad_resid, grad_attended, attended, query, key, value, log_total, weights, gain, cos, sin,
    g_weights, g_norm, grads, normed_t, back, tick, heads_done,
):
    seq, width = x.shape
    blocks = query_blocks(seq)
    tile = 128
    for at in range(0, seq, tile):
        inputs = x[at : at + tile, :].astype(F32)
        normed_t[:, at : at + tile] = (inputs * norm_rows(inputs) * gain).astype(LOW).T
    back[...] = jnp.zeros_like(back)

    def group(number, _):
        def pair(at, _):
            tick(number * PAIRS + at)
            for which in range(2):
                local = at * 2 + which
                head = number * (2 * PAIRS) + local
                rows = pl.ds(pl.multiple_of(head * HEAD_DIM, HEAD_DIM), HEAD_DIM)
                keys, values = key[rows, :], value[rows, :]
                delta_all = jnp.sum(grad_attended[rows, :].astype(F32) * attended[rows, :].astype(F32), 0, keepdims=True)
                key_grads = [0.0] * len(blocks)
                value_grads = [0.0] * len(blocks)
                at_query, at_key, at_value = (
                    pl.ds(pl.multiple_of(part * GROUP + local * HEAD_DIM, HEAD_DIM), HEAD_DIM) for part in range(3)
                )
                for start, stop in blocks:
                    queries, incoming = query[rows, start:stop], grad_attended[rows, start:stop]
                    total = log_total[head, :, start:stop]
                    delta = delta_all[:, start:stop]
                    query_grad = 0.0
                    for first, last, scores in score_parts(keys, queries, start, stop, length):
                        prob = jnp.exp2(scores - total)
                        grad_prob = dot_tn(values[:, first:last], incoming)
                        grad_score = (prob * (grad_prob - delta)).astype(LOW)
                        query_grad += dot_nn(keys[:, first:last], grad_score)
                        key_grad = dot_nt(queries, grad_score)
                        value_grad = dot_nt(incoming, prob.astype(LOW))
                        for piece, (low, high) in enumerate(blocks):
                            if first <= low and high <= last:
                                key_grads[piece] += key_grad[:, low - first : high - first]
                                value_grads[piece] += value_grad[:, low - first : high - first]
                    grads[at_query, start:stop] = (
                        rope(query_grad, cos[:, start:stop], -sin[:, start:stop]) * SCALE
                    ).astype(LOW)
                for (start, stop), key_grad, value_grad in zip(blocks, key_grads, value_grads):
                    grads[at_key, start:stop] = (
                        rope(key_grad, cos[:, start:stop], -sin[:, start:stop]) * (1.0 / LOG2E)
                    ).astype(LOW)
                    grads[at_value, start:stop] = value_grad.astype(LOW)
            return 0

        lax.fori_loop(0, PAIRS, pair, 0)
        turned = grads[...].T
        columns = pl.ds(pl.multiple_of(number * 3 * GROUP, GROUP), 3 * GROUP)
        for at in range(0, width, GROUP):
            rows = slice(at, at + GROUP)
            grad = dot_nn(normed_t[rows, :], turned)
            if follows:
                grad += g_weights[rows, columns].astype(F32)
            g_weights[rows, columns] = grad.astype(LOW)
        total = back[...]
        for part in range(3):
            source = pl.ds(pl.multiple_of(part * width + number * GROUP, GROUP), GROUP)
            total += dot_nn(turned[:, part * GROUP : (part + 1) * GROUP], weights[source, :])
        back[...] = total
        return 0

    lax.fori_loop(0, width // GROUP, group, 0)
    heads_done()
    norm_sum = jnp.zeros((1, width), F32)
    for at in range(0, seq, tile):
        rows = slice(at, at + tile)
        inputs, incoming = x[rows, :].astype(F32), back[rows, :]
        inv = norm_rows(inputs)
        scaled = inputs * inv
        norm_sum += jnp.sum(incoming * scaled, 0, keepdims=True)
        weighted = incoming * gain
        grad = grad_resid[rows, :].astype(F32) + inv * (
            weighted - scaled * jnp.mean(weighted * scaled, -1, keepdims=True)
        )
        grad_resid[rows, :] = grad.astype(LOW)
    g_norm[...] = g_norm[...] + norm_sum if follows else norm_sum


class Links:
    def __init__(self, bands, send, receive):
        self.send, self.receive, self.bands = send, receive, bands
        self.band, self.items = lax.axis_index("band"), lax.axis_index("items")
        self.count = 0

    def take(self, count):
        first = self.count
        self.count += count
        return first

    def other(self, shift):
        return lax.rem(self.band + shift + self.bands, self.bands)

    def greet(self, axis):
        barrier = pltpu.get_barrier_semaphore()
        others = [(self.items, self.other(shift)) for shift in range(1, self.bands)]
        if axis:
            others += [(flipped(self.items, at), self.band) for at in range(log2_of(axis))]
        for other in others:
            pl.semaphore_signal(barrier, inc=1, device_id=other, device_id_type=MESH)
        pl.semaphore_wait(barrier, len(others))

    def copy(self, number, source, target, device):
        return pltpu.make_async_remote_copy(
            src_ref=source,
            dst_ref=target,
            send_sem=self.send.at[number],
            recv_sem=self.receive.at[number],
            device_id=device,
            device_id_type=MESH,
        )


class Exchange:
    def __init__(self, links, source, target, arrival):
        self.links, self.first = links, links.take(links.bands - 1)
        self.source, self.target, self.arrival = source, target, arrival

    def each(self, place):
        for shift in range(1, self.links.bands):
            yield self.links.copy(
                self.first + shift - 1, self.source(shift), place(shift), (self.links.items, self.links.other(shift))
            )

    def start(self):
        for copy in self.each(self.target):
            copy.start()

    def arrived(self):
        for copy in self.each(self.arrival):
            copy.wait_recv()

    def left(self):
        for copy in self.each(self.target):
            copy.wait_send()


def bit(number, at):
    return lax.rem(lax.div(number, 2**at), 2)


def flipped(number, at):
    return number + (1 - 2 * bit(number, at)) * 2**at


def replaced(number, bits, choice):
    for order, at in enumerate(bits):
        number = number + ((choice >> order & 1) - bit(number, at)) * 2**at
    return number


def sum_lanes(axis, stage, columns):
    left = list(range(log2_of(axis)))
    right = [0] + left[:0:-1]
    half = columns // 2
    if stage == 0:
        return [(left[0], left[1:], 0, columns)]
    return [(left[stage], left[stage + 1 :], 0, half), (right[stage], right[stage + 1 :], half, half)]


def band_shape(axis, bands, shape):
    rows = shape[0] // axis // bands
    return (rows, shape[1]) if rows % 16 == 0 else (2 * rows, shape[1] // 2)


def sum_scratch(axis, bands, shape):
    low = lambda *dims: pltpu.VMEM(dims, LOW)
    out = []
    for stage in range(log2_of(axis)):
        for _, bits, _, columns in sum_lanes(axis, stage, shape[1]):
            out.append(low(2 ** len(bits), shape[0] // axis, columns))
    part = band_shape(axis, bands, shape)
    out.append(low(bands, *part))
    for stage in range(log2_of(bands)):
        out.append(low(bands >> stage + 1, *part))
    return out


def sum_links(axis, bands):
    return axis // 2 + 2 * (axis // 2 - 1) + bands - 1


class Summing:
    def __init__(self, links, axis, array, first, columns, scratch, finish):
        self.links, self.axis, self.array, self.finish = links, axis, array, finish
        self.first, self.columns = first, columns
        self.count = log2_of(axis)
        self.stages = self.count + log2_of(links.bands)
        self.scratch = scratch
        self.base = links.take(sum_links(axis, links.bands))
        self.state = 0

    def piece(self, number, first, columns):
        rows = self.array.shape[0] // self.axis
        return self.array.at[pl.ds(pl.multiple_of(number * rows, rows), rows), pl.ds(self.first + first, columns)]

    def flights(self, stage):
        me, band = self.links.items, self.links.band
        number, out = self.base, []
        for at in range(self.stages):
            if at < self.count:
                taken = [0] if at == 0 else [2 * at - 1, 2 * at]
                lanes = sum_lanes(self.axis, at, self.columns)
            else:
                taken = [self.count + at]
                lanes = [(at - self.count, list(range(at - self.count + 1, log2_of(self.links.bands))), 0, 0)]
            for (axis_bit, bits, first, columns), buffer in zip(lanes, taken):
                for choice in range(2 ** len(bits)):
                    if at == stage:
                        came = self.scratch[buffer].at[choice]
                        if at < self.count:
                            other = flipped(me, axis_bit)
                            device = (other, band)
                            sent = self.piece(replaced(other, bits, choice), first, columns)
                            kept = self.piece(replaced(me, bits, choice), first, columns)
                        else:
                            other = flipped(band, axis_bit)
                            device = (me, other)
                            parts = self.scratch[2 * self.count - 1]
                            sent, kept = parts.at[replaced(other, bits, choice)], parts.at[replaced(band, bits, choice)]
                        out.append((self.links.copy(number, sent, came, device), kept, came))
                    number += 1
        return out

    def begin(self, stage):
        for copy, _, _ in self.flights(stage):
            copy.start()

    def end(self, stage):
        flights = self.flights(stage)
        for copy, _, _ in flights:
            copy.wait_recv()
        for _, kept, came in flights:
            if stage == self.stages - 1:
                self.finish(kept[...].astype(F32) + came[...].astype(F32))
                continue
            tile = 16

            def add(step, _, kept=kept, came=came):
                rows = pl.ds(pl.multiple_of(step * tile, tile), tile)
                kept[rows, :] = (kept[rows, :].astype(F32) + came[rows, :].astype(F32)).astype(LOW)
                return 0

            lax.fori_loop(0, kept.shape[0] // tile, add, 0)
        if stage == self.count - 1:
            self.stack()

    def stack(self):
        bands = self.links.bands
        parts = self.scratch[2 * self.count - 1]
        whole = self.piece(self.links.items, 0, self.columns)
        rows = whole.shape[0] // bands
        if parts.shape[1] == rows:
            for number in range(bands):
                parts[number] = whole[number * rows : (number + 1) * rows, :]
            return
        half = self.columns // 2
        left, right = whole[:, :half].astype(F32), whole[:, half:].astype(F32)
        for number in range(bands):
            span = slice(number * rows, (number + 1) * rows)
            parts[number] = jnp.concatenate([left[span], right[span]], 0).astype(LOW)

    def advance(self):
        if self.state > self.stages:
            return
        if self.state > 0:
            self.end(self.state - 1)
        if self.state < self.stages:
            self.begin(self.state)
        self.state += 1

    def close(self):
        for stage in range(self.stages):
            for copy, _, _ in self.flights(stage):
                copy.wait_send()


def block_kernel(bands, per, axis, *refs):
    fused = axis > 0
    lengths, norm_attn, norm_ffn, cos, sin = refs[:5]
    tokens, cotangent, w_query, w_key, w_value, w_out_from, w_gate, w_up, w_down_from = refs[5:14]
    refs = refs[14:]
    home_out, home_grad = refs[:2]
    query_far, key_far, value_far, attended_t_far, grad_attended_t_far, cot_far = refs[2:8]
    refs = refs[8:]
    sums, refs = (refs[:8], refs[8:]) if fused else (refs[:5], refs[5:])
    weights_t, w_out, w_feed, w_down, g_feed, g_down, g_out = refs[:7]
    x, cot, attended, attended_t, query, key, value, grad_attended_t = refs[7:15]
    normed, normed_t, resid, out_acc, back_acc, log_total, g_norm, g_norm_ffn = refs[15:23]
    local, send, receive = refs[23:26]
    sum_refs = refs[26:]
    seq, width = x.shape[1:]
    ff = w_down.shape[0]
    band_rows, items = seq // bands, bands * per
    groups = width // GROUP
    links = Links(bands, send, receive)
    band = links.band
    gain_attn, gain_ffn = norm_attn[...][None, :], norm_ffn[...][None, :]
    started = [0]

    def bring(source, target):
        copy = pltpu.make_async_copy(source, target, local.at[started[0]])
        started[0] += 1
        copy.start()
        return copy

    token_rows = band_rows * items
    raw = g_down.at[pl.ds(0, token_rows)]
    load_tokens = bring(tokens, raw)
    qkv = (g_feed.at[:, pl.ds(0, width)], g_feed.at[:, pl.ds(width, width)], g_feed.at[:, pl.ds(2 * width, width)])
    load_qkv = [bring(source, target) for source, target in zip((w_query, w_key, w_value), qkv)]
    links.greet(axis)

    def own_rows(shift):
        return pl.ds(pl.multiple_of(links.other(shift) * band_rows, band_rows), band_rows)

    chunk = 32 if band_rows % 32 == 0 else 16
    size = items * chunk
    order = split_order(items, chunk, band * per)
    token_send = [attended.at[item] for item in range(per)]
    stages = [normed, resid]
    cot_send = [g_out] + [cot_far.at[item] for item in range(per - 1)]

    def split(kept, sent):
        for block in range(band_rows // chunk):
            moved = dot_nn(order, raw[block * size : (block + 1) * size, :]).astype(LOW)
            rows = pl.ds(pl.multiple_of(band * band_rows + block * chunk, 16), chunk)
            for at in range(items):
                part = moved[at * chunk : (at + 1) * chunk]
                shift, item = at // per, at % per
                if shift == 0:
                    kept[item, rows, :] = part
                else:
                    place = (shift - 1) * band_rows + block * chunk
                    sent[item][place : place + chunk, :] = part

    def scattering(sent, kept, item):
        return Exchange(
            links,
            lambda shift: sent[item].at[pl.ds((shift - 1) * band_rows, band_rows)],
            lambda shift: kept.at[item, own_rows(0)],
            lambda shift: kept.at[item, own_rows(-shift)],
        )

    def returning(source, home, item):
        slot = lambda shift: home.at[shift * per + item]
        return Exchange(links, lambda shift: source.at[item, own_rows(shift)], slot, slot)

    token_links = [scattering(token_send, x, item) for item in range(per)]
    cot_links = [scattering(cot_send, cot, item) for item in range(per)]
    out_links = [returning(attended, home_out, item) for item in range(per)]
    grad_links = [returning(cot, home_grad, item) for item in range(per)]

    load_tokens.wait()
    split(x, token_send)
    token_links[0].start()
    load_cot = bring(cotangent, raw)
    load_rest = [
        bring(w_out_from, w_out),
        bring(w_gate, w_feed.at[:, pl.ds(0, ff)]),
        bring(w_up, w_feed.at[:, pl.ds(ff, ff)]),
        bring(w_down_from, w_down),
    ]
    for part in range(3):
        load_qkv[part].wait()
        for at in range(0, width, 256):
            weights_t[part * width + at : part * width + at + 256, :] = qkv[part][:, at : at + 256].T
    load_cot.wait()
    split(cot, [g_out] + stages[: per - 1])
    late = pl.ds(0, (bands - 1) * band_rows)
    to_far = [bring(stages[item].at[late], cot_far.at[item]) for item in range(per - 1)]

    sums_of = {}
    schedule = {}
    if fused:
        scratch_each = len(sum_scratch(axis, bands, (axis * bands * 16, 256)))
        taken = [0]
        o_gate, o_up, o_down, o_out, o_query, o_key, o_value, o_norm = sums

        def summing(name, array, first, columns, finish):
            sums_of[name] = Summing(
                links, axis, array, first, columns, sum_refs[taken[0] : taken[0] + scratch_each], finish
            )
            taken[0] += scratch_each

        def halves(total):
            rows = total.shape[0] // 2
            return total[:rows], total[rows:]

        for step in range(ff // WIDE):

            def finish_feed(total, step=step):
                span = slice(step * WIDE, (step + 1) * WIDE)
                o_gate[:, span], o_up[:, span] = halves(total)

            summing(("feed", step), g_feed, step * 2 * WIDE, 2 * WIDE, finish_feed)

        def finish_down(total):
            o_down[...] = total

        def finish_out(total):
            o_out[:, : width // 2], o_out[:, width // 2 :] = halves(total)

        def finish_norm(total):
            o_norm[:, :128], o_norm[:, 128:] = halves(total)

        summing("down", g_down, 0, width, finish_down)
        summing("out", g_out, 0, width, finish_out)
        for number in range(groups):

            def finish_group(total, number=number):
                left, right = halves(total)
                at, half = number * GROUP, GROUP // 2
                o_query[:, at : at + GROUP] = left[:, :GROUP]
                o_key[:, at : at + half] = left[:, GROUP:]
                o_key[:, at + half : at + GROUP] = right[:, :half]
                o_value[:, at : at + GROUP] = right[:, half:]

            summing(("back", number), w_feed, number * 3 * GROUP, 3 * GROUP, finish_group)
        summing("norm", w_feed, 3 * width, 256, finish_norm)

    def advance(*names):
        for name in names:
            sums_of[name].advance()

    spills = []

    def spill(pairs):
        spills.extend(bring(source, target) for source, target in pairs)

    def settle():
        while spills:
            spills.pop().wait()

    g_weights = w_feed
    grads = w_feed.at[pl.ds(0, 3 * GROUP), pl.ds(3 * width + 256, seq)]
    for item in range(per):
        last = item == per - 1
        if item == 0:
            token_links[0].arrived()
            cot_links[0].start()
            for copy in to_far:
                copy.wait()
        settle()

        def projected(item=item):
            token_links[item].left()
            if item < per - 1:
                spill(
                    (source, target.at[item])
                    for source, target in ((query, query_far), (key, key_far), (value, value_far))
                )

        attend_item(
            lengths[band * per + item], x.at[item], weights_t, gain_attn, cos, sin, query, key, value, attended_t,
            attended.at[item], log_total.at[item], normed, projected,
        )
        if item == 0:
            for load in load_rest:
                load.wait()
        cot_links[item].arrived()
        if last:
            for ahead in range(per - 1):
                out_links[ahead].start()
        else:
            token_links[item + 1].start()

        def feed_tick(step, item=item, last=last):
            if not last:

                @pl.when(step == ff // WIDE - 1)
                def _():
                    token_links[item + 1].arrived()
                    cot_links[item + 1].start()

            elif fused:
                for at in range(1, ff // WIDE):

                    @pl.when(step == at)
                    def _(at=at):
                        advance(*[("feed", number) for number in range(at)])

        def before_out(item=item):
            if item == 0:
                cot_links[0].left()

        feed_item(
            item > 0, x.at[item], attended.at[item], attended_t, cot.at[item], w_out, w_feed, w_down, gain_ffn,
            g_feed, g_down, g_out, g_norm_ffn, attended.at[item], grad_attended_t,
            (normed, normed_t, resid, out_acc, back_acc), feed_tick, before_out,
        )
        if not last:
            spill(
                (source, target.at[item])
                for source, target in ((attended_t, attended_t_far), (grad_attended_t, grad_attended_t_far))
            )
    out_links[per - 1].start()
    feeds = [("feed", step) for step in range(ff // WIDE)]
    if fused:
        advance(*feeds, "down", "out")
    turns = list(reversed(range(per)))
    reloads = []
    for turn, item in enumerate(turns):
        last = turn == per - 1

        def back_tick(at, turn=turn, last=last):
            if not fused:
                return
            for place, names in plan(turn, last).items():

                @pl.when(at == place)
                def _(names=names):
                    advance(*names)

        def plan(turn, last):
            out = {}
            for place in range(groups * PAIRS):
                names = []
                if turn == 0 and place % 2 == 1:
                    names += feeds
                if turn == 0 and place in (2, 5) or turn == 1 and place in (1, 3, 5):
                    names += ["down", "out"]
                if turn == 1 and place == 0:
                    names += feeds
                if last and place >= PAIRS:
                    names += [("back", number) for number in range(place // PAIRS)]
                if names:
                    out[place] = names
            return out

        def heads_done(turn=turn, last=last):
            if not last:
                following = turns[turn + 1]
                for source, target in (
                    (query_far, query), (key_far, key), (value_far, value), (attended_t_far, attended_t),
                    (grad_attended_t_far, grad_attended_t),
                ):
                    reloads.append(bring(source.at[following], target))
            elif fused:
                advance(*[("back", number) for number in range(groups)])

        back_item(
            turn > 0, lengths[band * per + item], x.at[item], cot.at[item], grad_attended_t, attended_t, query, key,
            value, log_total.at[item], weights_t, gain_attn, cos, sin, g_weights, g_norm, grads, normed_t, back_acc,
            back_tick, heads_done,
        )
        grad_links[item].start()
        while reloads:
            reloads.pop().wait()
    own = []
    for item in range(per):
        own.append(bring(attended.at[item, own_rows(0)], home_out.at[item]))
        own.append(bring(cot.at[item, own_rows(0)], home_grad.at[item]))
    if fused:
        lanes = 128
        pad = jnp.zeros((lanes - 1, width), F32)
        for at, total in enumerate((g_norm, g_norm_ffn)):
            spread = jnp.concatenate([total[...], pad], 0).T
            w_feed[:, 3 * width + at * lanes : 3 * width + (at + 1) * lanes] = spread.astype(LOW)
        every = feeds + ["down", "out"] + [("back", number) for number in range(groups)] + ["norm"]
        while any(sums_of[name].state <= sums_of[name].stages for name in every):
            advance(*every)
        for name in every:
            sums_of[name].close()
    else:
        own += [
            bring(source, target)
            for source, target in zip((g_feed, g_down, g_out, g_weights.at[:, pl.ds(0, 3 * width)]), sums[:4])
        ]
        sums[4][0:1, :] = g_norm[...]
        sums[4][1:2, :] = g_norm_ffn[...]
    for copy in own:
        copy.wait()
    for item in range(per):
        for exchange in (out_links[item], grad_links[item]):
            exchange.arrived()
            exchange.left()
        if item:
            cot_links[item].left()


def block(bands, axis, lengths, tokens, cotangent, gains, tables, weights):
    band_rows, items, width = tokens.shape
    per, seq, ff = items // bands, bands * band_rows, weights[4].shape[1]
    fused = axis > 0
    low = lambda *shape: jax.ShapeDtypeStruct(shape, LOW)
    full = lambda *shape: jax.ShapeDtypeStruct(shape, F32)
    scratch = lambda *shape: pltpu.VMEM(shape, LOW)
    wide = lambda *shape: pltpu.VMEM(shape, F32)
    outside = pl.BlockSpec(memory_space=pl.ANY)
    inside = pl.BlockSpec(memory_space=pltpu.VMEM)
    out_shape = [low(items, band_rows, width)] * 2 + [low(max(per - 1, 1), width, seq)] * 5
    out_shape += [low(max(per - 1, 1), (bands - 1) * band_rows, width)]
    out_specs = [outside] * 8
    extra, links = [], 4 * per * (bands - 1)
    if fused:
        devices = axis * bands
        rows, ff_rows = width // devices, ff // devices
        out_shape += [full(rows, ff), full(rows, ff), full(ff_rows, width)] + [full(rows, width)] * 4 + [full(rows, 256)]
        out_specs += [inside] * 8
        shapes = [(width, 2 * WIDE)] * (ff // WIDE) + [(ff, width), (width, width)]
        shapes += [(width, 3 * GROUP)] * (width // GROUP) + [(width, 256)]
        for shape in shapes:
            extra += sum_scratch(axis, bands, shape)
        links += len(shapes) * sum_links(axis, bands)
    else:
        out_shape += [low(width, 2 * ff), low(ff, width), low(width, width), low(width, 3 * width), full(2, width)]
        out_specs += [outside] * 4 + [inside]
    return pl.pallas_call(
        functools.partial(block_kernel, bands, per, axis),
        name="block",
        out_shape=out_shape,
        in_specs=[smem()] + [inside] * 4 + [outside] * 9,
        out_specs=out_specs,
        scratch_shapes=[
            scratch(3 * width, width), scratch(width, width), scratch(width, 2 * ff), scratch(ff, width),
            scratch(width, 2 * ff), scratch(ff, width), scratch(width, width),
            scratch(per, seq, width), scratch(per, seq, width), scratch(per, seq, width), scratch(width, seq),
            scratch(width, seq), scratch(width, seq), scratch(width, seq), scratch(width, seq),
            scratch(seq, width), scratch(width, seq), scratch(seq, width), wide(seq, width), wide(seq, width),
            wide(per, width // HEAD_DIM, 1, seq), wide(1, width), wide(1, width),
            pltpu.SemaphoreType.DMA((16 + 12 * per,)),
            pltpu.SemaphoreType.DMA((links,)),
            pltpu.SemaphoreType.DMA((links,)),
        ]
        + extra,
        compiler_params=pltpu.CompilerParams(vmem_limit_bytes=64 * 2**20 - 2**16, collective_id=0, has_side_effects=True),
    )(
        lengths, *gains, *tables, tokens.reshape(band_rows * items, width), cotangent.reshape(band_rows * items, width),
        *weights,
    )


def rope_tables(seq):
    frequency = np.exp(-np.log(ROPE_BASE) * (2.0 * np.arange(HALF) / HEAD_DIM))
    angles = frequency[:, None] * np.arange(seq)[None, :]
    return jnp.asarray(np.cos(angles), F32), jnp.asarray(np.sin(angles), F32)


def per_device(
    bands,
    axis,
    tokens,
    lengths,
    norm_attn,
    w_query,
    w_key,
    w_value,
    w_out,
    norm_ffn,
    w_gate,
    w_up,
    w_down,
    cotangent,
):
    band_rows, items, width = tokens.shape
    per = items // bands
    seq = bands * band_rows
    band = lax.axis_index("band")
    fused = axis if width // axis % 16 == 0 and w_gate.shape[1] // axis % 16 == 0 else 0
    home_out, home_grad, *sums = block(
        bands, fused, lengths, tokens, cotangent, (norm_attn, norm_ffn), rope_tables(seq),
        (w_query, w_key, w_value, w_out, w_gate, w_up, w_down),
    )
    sums = sums[6:]
    output = merge_items([home_out[at] for at in range(items)], band, bands)
    grad_tokens = merge_items([home_grad[at] for at in range(items)], band, bands)
    if fused:
        g_gate, g_up, g_down, g_out, g_query, g_key, g_value, norms = sums
        g_norm_attn, g_norm_ffn = norms[:, 0], norms[:, 128]
    else:
        axes = ("items", "band")
        total = lambda a: lax.psum_scatter(a, axes, scatter_dimension=0, tiled=True).astype(F32)
        g_feed, g_down, g_out, g_weights = (total(a) for a in sums[:4])
        norms = total(sums[4].T)
        g_norm_attn, g_norm_ffn = norms[:, 0], norms[:, 1]
        g_gate, g_up = jnp.moveaxis(g_feed.reshape(-1, w_gate.shape[1] // WIDE, 2, WIDE), 2, 0).reshape(2, -1, w_gate.shape[1])
        g_query, g_key, g_value = jnp.moveaxis(g_weights.reshape(-1, width // GROUP, 3, GROUP), 2, 0).reshape(3, -1, width)
    return (
        output,
        grad_tokens,
        g_norm_attn,
        g_query,
        g_key,
        g_value,
        g_out,
        g_norm_ffn,
        g_gate,
        g_up,
        g_down,
    )


def solution(mesh):
    split = P("band", "items", None)
    rows = P(("items", "band"), None)
    flat = P(("items", "band"))
    return jax.shard_map(
        functools.partial(per_device, mesh.shape["band"], mesh.shape["items"]),
        mesh=mesh,
        in_specs=(split, P("items")) + (P(),) * 9 + (split,),
        out_specs=(split, split, flat, rows, rows, rows, rows, flat, rows, rows, rows),
        check_vma=False,
    )
```

time: 512 us -> 260 us (0.51)
  waiting for transfers between devices: 249 us -> 0 us
  Pallas kernels: 187 us -> 246 us
  starting transfers between devices: 21.8 us -> 0 us
  local copies, waits for them, and re-layouts: 26.9 us -> 10.3 us
  between operations: 14.2 us -> 0.89 us
  other arithmetic: 10.2 us -> 0 us
    reduce_scatter x2 -> x0, waiting for transfers between devices: 117 us -> none  [the longest x1 117 us: per_device(): lax.psum_scatter(jnp.concatenate([g_gate, g_up], 1), axes, scatter_dimens...]
    unnamed x4 -> x0, waiting for transfers between devices: 85.5 us -> none
    pallas_call x3 -> x1, Pallas kernels: 183 us -> 242 us  [block(): pl.pallas_call(functools.partial(block_kernel, bands, per, axis), name='b...]
    ppermute x9 -> x0, waiting for transfers between devices: 46.8 us -> none  [exchange(): lax.ppermute(parts[shift * per + item], 'band', [(i, (i + shift) % bands)...]
    ppermute x9 -> x0, starting transfers between devices: 21.5 us -> none  [exchange(): lax.ppermute(parts[shift * per + item], 'band', [(i, (i + shift) % bands)...]
    concatenate x1 -> x0, local copies, waits for them, and re-layouts: 7.94 us -> none  [per_device(): rest = jnp.concatenate([g_weights, g_out, gains.astype(LOW)], 1)]
    concatenate x1 -> x0, other arithmetic: 6.31 us -> none  [per_device(): jnp.concatenate([g_gate, g_up], 1)]
  transfers between devices with their start and end apart: 12 -> 0, of which waited for: 6 -> 0; matrix products, arithmetic and copies ran while one was open for 6% -> 0% of each run, Pallas kernels for 10% -> 0%
where the time goes in v4:
time: 260 us; the launch traced here: 257 us
  Pallas kernels  246 us (95%)
  local copies, waits for them, and re-layouts  10.3 us (4%)
    pallas_call x1, Pallas kernels, block(): pl.pallas_call(functools.partial(block_kernel, bands, per, axis), name='b...  242 us
    unnamed x27, local copies, waits for them, and re-layouts  6.48 us

profile of v4, /device:TPU:0, one launch (start us, length us, event | category | flops | bytes accessed | tf_op | source)
XLA Modules:
  0.0 257.2 jit_solution(8162097955661798805)
XLA Ops:
  0.6 242.1 %block.1 = (bf16[8,160,768]{2,1,0:T(8,128)(2,1)}, bf16[8,160,768]{2,1,0:T(8,128)(2,1)}, bf16[1,768,640]{2,1,0:T(8,128)(2,1)}, bf16[1,768,640]{2,1,0:T(8,128)(2,1...) custom-call(s32[8]{0:T(128)} %refs_0_.1, ...), custom_call_target="tpu_custom_call" | custom-call | tf_op jit(solution)/shard_map/block/pallas_call | solution.py:854
  242.7 3.2 %slice_bitcast_fusion = (bf16[160,768]{1,0:T(8,128)(2,1)S(1)}, bf16[160,768]{1,0:T(8,128)(2,1)S(1)}, bf16[160,768]{1,0:T(8,128)(2,1)S(1)}, bf16[160,768]{1,0:T(8...) fusion(bf16[8,160,768]{2,1,0:T(8,128)(2,1)} %get-tuple-element., ...), kind=kLoop, calls=%fused_computation | loop fusion | bytes 7864320 | tf_op jit(solution)/shard_map/squeeze | solution.py:912
  245.9 0.0 copy-start
  245.9 0.9 copy-done
  246.9 0.0 copy-start.1
  246.9 0.9 copy-done.1
  247.8 2.0 merge_items.3
  249.8 0.0 copy-start.9
  249.8 0.0 copy-start.8
  249.8 0.0 copy-start.7
  249.8 0.0 copy-start.6
  249.8 0.0 copy-start.5
  249.8 0.0 copy-start.4
  249.8 0.0 copy-start.3
  249.8 0.0 copy-start.2
  249.8 2.0 merge_items.2
  251.8 0.0 copy-done.9
  251.8 0.6 slice_reduce_fusion
  252.4 0.0 copy-done.8
  252.4 0.6 copy.32
  253.1 0.0 copy-done.7
  253.1 0.6 copy.33
  253.7 0.0 copy-done.6
  253.7 0.6 copy.34
  254.3 0.0 copy-done.5
  254.3 0.6 copy.35
  255.0 0.0 copy-done.4
  255.0 0.7 copy.36
  255.7 0.0 copy-done.3
  255.7 0.7 copy.37
  256.3 0.0 copy-done.2
  256.3 0.7 copy.38
Async XLA Ops:
  245.9 0.9 copy-start
  246.9 0.9 copy-start.1
  249.8 2.0 copy-start.9
  249.8 2.6 %copy-start.8 = (f32[24,768]{1,0:T(8,128)S(1)}, f32[24,768]{1,0:T(8,128)}, u32[]{:S(2)}) copy-start(f32[24,768]{1,0:T(8,128)} %get-tuple-element.71) | copy-start | bytes 221188
  249.8 3.3 %copy-start.7 = (f32[24,768]{1,0:T(8,128)S(1)}, f32[24,768]{1,0:T(8,128)}, u32[]{:S(2)}) copy-start(f32[24,768]{1,0:T(8,128)} %get-tuple-element.72) | copy-start | bytes 221188
  249.8 3.9 %copy-start.6 = (f32[24,768]{1,0:T(8,128)S(1)}, f32[24,768]{1,0:T(8,128)}, u32[]{:S(2)}) copy-start(f32[24,768]{1,0:T(8,128)} %get-tuple-element.73) | copy-start | bytes 221188
  249.8 4.5 %copy-start.5 = (f32[24,768]{1,0:T(8,128)S(1)}, f32[24,768]{1,0:T(8,128)}, u32[]{:S(2)}) copy-start(f32[24,768]{1,0:T(8,128)} %get-tuple-element.74) | copy-start | bytes 221188
  249.8 5.2 %copy-start.4 = (f32[24,2048]{1,0:T(8,128)S(1)}, f32[24,2048]{1,0:T(8,128)}, u32[]{:S(2)}) copy-start(f32[24,2048]{1,0:T(8,128)} %get-tuple-element.76) | copy-start | bytes 589828
  249.8 5.8 %copy-start.3 = (f32[24,2048]{1,0:T(8,128)S(1)}, f32[24,2048]{1,0:T(8,128)}, u32[]{:S(2)}) copy-start(f32[24,2048]{1,0:T(8,128)} %get-tuple-element.77) | copy-start | bytes 589828
  249.8 6.5 %copy-start.2 = (f32[64,768]{1,0:T(8,128)S(1)}, f32[64,768]{1,0:T(8,128)}, u32[]{:S(2)}) copy-start(f32[64,768]{1,0:T(8,128)} %get-tuple-element.78) | copy-start | bytes 589828

commit v5 on v4

--- a/solution.py
+++ b/solution.py
@@ -58,8 +58,13 @@
     return jnp.where(col == (row & (chunk - 1)) * items + item, 1.0, 0.0).astype(LOW)
 
 
-def merge_kernel(items, per, chunk, band_ref, *refs):
-    ins, out = refs[:-1], refs[-1]
+def merge_kernel(per, chunk, band_ref, *refs):
+    count = (len(refs) - 1) // 4
+    ins, outs, held, made, sem = refs[:count], refs[count : 2 * count], refs[2 * count : 3 * count], refs[3 * count : -1], refs[-1]
+    loads = [pltpu.make_async_copy(ins[at], held[at], sem.at[at]) for at in range(count)]
+    for load in loads:
+        load.start()
+    items, band_rows, width = ins[0].shape
     size, bands = items * chunk, items // per
     row = lax.broadcasted_iota(jnp.int32, (size, size), 0)
     col = lax.broadcasted_iota(jnp.int32, (size, size), 1)
@@ -68,23 +73,36 @@
     source = jnp.where(source < 0, source + bands, source)
     item = source * per + (number & (per - 1))
     order = jnp.where(row == (col & (chunk - 1)) * items + item, 1.0, 0.0).astype(LOW)
-    for block in range(out.shape[0] // size):
-        parts = jnp.concatenate([part[block * chunk : (block + 1) * chunk, :] for part in ins], 0)
-        out[block * size : (block + 1) * size, :] = dot_nn(order, parts).astype(LOW)
-
-
-def merge_items(parts, band, bands):
-    items = len(parts)
-    band_rows, width = parts[0].shape
+    stores = []
+    for at in range(count):
+        loads[at].wait()
+        for block in range(band_rows // chunk):
+            rows = slice(block * size, (block + 1) * size)
+            parts = held[at][:, block * chunk : (block + 1) * chunk, :].reshape(size, width)
+            made[at][rows, :] = dot_nn(order, parts).astype(LOW)
+        stores.append(pltpu.make_async_copy(made[at], outs[at], sem.at[count + at]))
+        stores[-1].start()
+    for store in stores:
+        store.wait()
+
+
+def merge_items(arrays, band, bands):
+    items, band_rows, width = arrays[0].shape
     chunk = 32 if band_rows % 32 == 0 else 16
-    return pl.pallas_call(
-        functools.partial(merge_kernel, items, items // bands, chunk),
+    count = len(arrays)
+    outside = pl.BlockSpec(memory_space=pl.ANY)
+    merged = pl.pallas_call(
+        functools.partial(merge_kernel, items // bands, chunk),
         name="merge_items",
-        out_shape=jax.ShapeDtypeStruct((band_rows * items, width), LOW),
-        in_specs=[smem()] + vmem(items),
-        out_specs=vmem(1)[0],
-        compiler_params=params(32),
-    )(jnp.reshape(band, (1,)), *parts).reshape(band_rows, items, width)
+        out_shape=[jax.ShapeDtypeStruct((band_rows * items, width), LOW)] * count,
+        in_specs=[smem()] + [outside] * count,
+        out_specs=[outside] * count,
+        scratch_shapes=[pltpu.VMEM((items, band_rows, width), LOW)] * count
+        + [pltpu.VMEM((band_rows * items, width), LOW)] * count
+        + [pltpu.SemaphoreType.DMA((2 * count,))],
+        compiler_params=params(60),
+    )(jnp.reshape(band, (1,)), *arrays)
+    return [array.reshape(band_rows, items, width) for array in merged]
 
 
 def rope(vector, cos, sin):
@@ -164,10 +182,12 @@
         attended[:, at : at + project] = attended_t[at : at + project, :].T
 
 
+LANES = 128
+GROUP = 256
 WIDE = 512
 
 
-def feed_item(follows, x, attended, attended_t, cot, w_out, w_feed, w_down, gain, g_feed, g_down, g_out, g_norm, out, grad_attended_t, scratch, tick, before_out):
+def feed_item(follows, x, attended, attended_t, cot, w_out, w_feed, w_down, gain, g_feed, g_down, g_out, g_norm, out, grad_attended_t, scratch, tick):
     normed, normed_t, resid, out_acc, back_acc = scratch
     seq, width = x.shape
     ff = w_down.shape[0]
@@ -195,24 +215,36 @@
         lows = []
         for at in range(0, seq, seq // 2):
             rows = slice(at, at + seq // 2)
-            gate = dot_nn(normed[rows, :], w_feed[:, span])
-            upward = dot_nn(normed[rows, :], w_feed[:, up_span])
-            grad_hidden = dot_nt(cot[rows, :], w_down[span, :])
-            sig = 0.5 * jnp.tanh(0.5 * gate) + 0.5
-            silu = gate * sig
-            hidden = (silu * upward).astype(LOW)
-            grad_gate = (grad_hidden * upward * (sig + silu * (1.0 - sig))).astype(LOW)
-            grad_upward = (grad_hidden * silu).astype(LOW)
+            parts = []
+            for first in range(0, WIDE, WIDE // 2):
+                columns = pl.ds(pl.multiple_of(step * WIDE + first, WIDE // 2), WIDE // 2)
+                up_columns = pl.ds(pl.multiple_of(ff + step * WIDE + first, WIDE // 2), WIDE // 2)
+                gate = dot_nn(normed[rows, :], w_feed[:, columns])
+                upward = dot_nn(normed[rows, :], w_feed[:, up_columns])
+                grad_hidden = dot_nt(cot[rows, :], w_down[columns, :])
+                sig = 0.5 * jnp.tanh(0.5 * gate) + 0.5
+                silu = gate * sig
+                hidden = (silu * upward).astype(LOW)
+                grad_gate = (grad_hidden * upward * (sig + silu * (1.0 - sig))).astype(LOW)
+                grad_upward = (grad_hidden * silu).astype(LOW)
+                parts.append((hidden, grad_gate, grad_upward))
+            hidden, grad_gate, grad_upward = (jnp.concatenate(both, 1) for both in zip(*parts))
             out_acc[rows, :] += dot_nn(hidden, w_down[span, :])
             back_acc[rows, :] += dot_nt(grad_gate, w_feed[:, span])
             back_acc[rows, :] += dot_nt(grad_upward, w_feed[:, up_span])
             lows.append((hidden, grad_gate, grad_upward))
         hidden, grad_gate, grad_upward = (jnp.concatenate(parts, 0) for parts in zip(*lows))
-        put(g_down, (span, slice(None)), dot_nn(hidden.T, cot[...]))
+        half = WIDE // 2
+        for at in range(0, WIDE, half):
+            part = pl.ds(pl.multiple_of(step * WIDE + at, half), half)
+            put(g_down, (part, slice(None)), dot_nn(hidden[:, at : at + half].T, cot[...]))
         first = pl.ds(pl.multiple_of(step * 2 * WIDE, WIDE), WIDE)
         second = pl.ds(pl.multiple_of(step * 2 * WIDE + WIDE, WIDE), WIDE)
-        put(g_feed, (slice(None), first), dot_nn(normed_t[...], grad_gate))
-        put(g_feed, (slice(None), second), dot_nn(normed_t[...], grad_upward))
+        half = width // 2
+        for at in range(0, width, half):
+            part = slice(at, at + half)
+            put(g_feed, (part, first), dot_nn(normed_t[part, :], grad_gate))
+            put(g_feed, (part, second), dot_nn(normed_t[part, :], grad_upward))
         return 0
 
     lax.fori_loop(0, ff // WIDE, chunk, 0)
@@ -228,12 +260,14 @@
         grad = cot[rows, :].astype(F32) + inv * (weighted - scaled * jnp.mean(weighted * scaled, -1, keepdims=True))
         cot[rows, :] = grad.astype(LOW)
     g_norm[...] = g_norm[...] + norm_sum if follows else norm_sum
-    grad_attended_t[...] = dot_nt(w_out[...], cot[...]).astype(LOW)
-    before_out()
-    put(g_out, (slice(None), slice(None)), dot_nn(attended_t[...], cot[...]))
-
-
-GROUP = 256
+    for at in range(0, width, GROUP):
+        rows = slice(at, at + GROUP)
+        grad_attended_t[rows, :] = dot_nt(w_out[rows, :], cot[...]).astype(LOW)
+    for at in range(0, width, GROUP):
+        rows = slice(at, at + GROUP)
+        put(g_out, (rows, slice(0, width)), dot_nn(attended_t[rows, :], cot[...]))
+
+
 PAIRS = GROUP // (2 * HEAD_DIM)
 
 
@@ -298,11 +332,13 @@
             if follows:
                 grad += g_weights[rows, columns].astype(F32)
             g_weights[rows, columns] = grad.astype(LOW)
-        total = back[...]
-        for part in range(3):
-            source = pl.ds(pl.multiple_of(part * width + number * GROUP, GROUP), GROUP)
-            total += dot_nn(turned[:, part * GROUP : (part + 1) * GROUP], weights[source, :])
-        back[...] = total
+        for at in range(0, seq, seq // 2):
+            rows = slice(at, at + seq // 2)
+            total = back[rows, :]
+            for part in range(3):
+                source = pl.ds(pl.multiple_of(part * width + number * GROUP, GROUP), GROUP)
+                total += dot_nn(turned[rows, part * GROUP : (part + 1) * GROUP], weights[source, :])
+            back[rows, :] = total
         return 0
 
     lax.fori_loop(0, width // GROUP, group, 0)
@@ -323,9 +359,11 @@
 
 
 class Links:
-    def __init__(self, bands, send, receive):
+    def __init__(self, bands, axis, send, receive):
         self.send, self.receive, self.bands = send, receive, bands
         self.band, self.items = lax.axis_index("band"), lax.axis_index("items")
+        self.item_bits, self.item_partners = bits_of(self.items, axis) if axis else ((), ())
+        self.band_bits, self.band_partners = bits_of(self.band, bands)
         self.count = 0
 
     def take(self, count):
@@ -336,14 +374,13 @@
     def other(self, shift):
         return lax.rem(self.band + shift + self.bands, self.bands)
 
-    def greet(self, axis):
+    def greet(self):
         barrier = pltpu.get_barrier_semaphore()
         others = [(self.items, self.other(shift)) for shift in range(1, self.bands)]
-        if axis:
-            others += [(flipped(self.items, at), self.band) for at in range(log2_of(axis))]
+        others += [(partner, self.band) for partner in self.item_partners]
         for other in others:
             pl.semaphore_signal(barrier, inc=1, device_id=other, device_id_type=MESH)
-        pl.semaphore_wait(barrier, len(others))
+        return lambda: pl.semaphore_wait(barrier, len(others))
 
     def copy(self, number, source, target, device):
         return pltpu.make_async_remote_copy(
@@ -380,18 +417,9 @@
             copy.wait_send()
 
 
-def bit(number, at):
-    return lax.rem(lax.div(number, 2**at), 2)
-
-
-def flipped(number, at):
-    return number + (1 - 2 * bit(number, at)) * 2**at
-
-
-def replaced(number, bits, choice):
-    for order, at in enumerate(bits):
-        number = number + ((choice >> order & 1) - bit(number, at)) * 2**at
-    return number
+def bits_of(number, size):
+    bits = [lax.rem(lax.div(number, 2**at), 2) for at in range(log2_of(size))]
+    return bits, [number + (1 - 2 * bit) * 2**at for at, bit in enumerate(bits)]
 
 
 def sum_lanes(axis, stage, columns):
@@ -413,58 +441,50 @@
     out = []
     for stage in range(log2_of(axis)):
         for _, bits, _, columns in sum_lanes(axis, stage, shape[1]):
-            out.append(low(2 ** len(bits), shape[0] // axis, columns))
+            out.append(low(*(2,) * len(bits), shape[0] // axis, columns))
     part = band_shape(axis, bands, shape)
-    out.append(low(bands, *part))
+    out.append(low(*(2,) * log2_of(bands), *part))
     for stage in range(log2_of(bands)):
-        out.append(low(bands >> stage + 1, *part))
+        out.append(low(*(2,) * (log2_of(bands) - stage - 1), *part))
     return out
 
 
 def sum_links(axis, bands):
-    return axis // 2 + 2 * (axis // 2 - 1) + bands - 1
+    return 2 * log2_of(axis) + log2_of(bands)
 
 
 class Summing:
     def __init__(self, links, axis, array, first, columns, scratch, finish):
-        self.links, self.axis, self.array, self.finish = links, axis, array, finish
-        self.first, self.columns = first, columns
-        self.count = log2_of(axis)
+        self.links, self.array, self.finish = links, array, finish
+        self.first, self.columns, self.scratch = first, columns, scratch
+        self.axis, self.count = axis, log2_of(axis)
         self.stages = self.count + log2_of(links.bands)
-        self.scratch = scratch
         self.base = links.take(sum_links(axis, links.bands))
         self.state = 0
 
-    def piece(self, number, first, columns):
-        rows = self.array.shape[0] // self.axis
-        return self.array.at[pl.ds(pl.multiple_of(number * rows, rows), rows), pl.ds(self.first + first, columns)]
-
     def flights(self, stage):
-        me, band = self.links.items, self.links.band
-        number, out = self.base, []
-        for at in range(self.stages):
-            if at < self.count:
-                taken = [0] if at == 0 else [2 * at - 1, 2 * at]
-                lanes = sum_lanes(self.axis, at, self.columns)
-            else:
-                taken = [self.count + at]
-                lanes = [(at - self.count, list(range(at - self.count + 1, log2_of(self.links.bands))), 0, 0)]
-            for (axis_bit, bits, first, columns), buffer in zip(lanes, taken):
-                for choice in range(2 ** len(bits)):
-                    if at == stage:
-                        came = self.scratch[buffer].at[choice]
-                        if at < self.count:
-                            other = flipped(me, axis_bit)
-                            device = (other, band)
-                            sent = self.piece(replaced(other, bits, choice), first, columns)
-                            kept = self.piece(replaced(me, bits, choice), first, columns)
-                        else:
-                            other = flipped(band, axis_bit)
-                            device = (me, other)
-                            parts = self.scratch[2 * self.count - 1]
-                            sent, kept = parts.at[replaced(other, bits, choice)], parts.at[replaced(band, bits, choice)]
-                        out.append((self.links.copy(number, sent, came, device), kept, came))
-                    number += 1
+        links = self.links
+        if stage < self.count:
+            rows, wide = self.array.shape
+            view = self.array.reshape(*(2,) * self.count, rows // self.axis, wide)
+            bits, partners, used = links.item_bits, links.item_partners, [0] if stage == 0 else [2 * stage - 1, 2 * stage]
+            lanes = sum_lanes(self.axis, stage, self.columns)
+            first = self.first
+        else:
+            view, first = self.scratch[2 * self.count - 1], 0
+            bits, partners, used = links.band_bits, links.band_partners, [self.count + stage]
+            at = stage - self.count
+            lanes = [(at, list(range(at + 1, len(bits))), 0, view.shape[-1])]
+        out = []
+        for (now, later, start, columns), number in zip(lanes, used):
+            place = lambda own: tuple(
+                slice(None) if at in later else 1 - bits[at] if at == now and not own else bits[at]
+                for at in reversed(range(len(bits)))
+            ) + (slice(None), pl.ds(first + start, columns))
+            partner = partners[now]
+            device = (partner, links.band) if stage < self.count else (links.items, partner)
+            came = self.scratch[number]
+            out.append((links.copy(self.base + number, view.at[place(False)], came, device), view.at[place(True)], came))
         return out
 
     def begin(self, stage):
@@ -479,31 +499,35 @@
             if stage == self.stages - 1:
                 self.finish(kept[...].astype(F32) + came[...].astype(F32))
                 continue
-            tile = 16
-
-            def add(step, _, kept=kept, came=came):
-                rows = pl.ds(pl.multiple_of(step * tile, tile), tile)
-                kept[rows, :] = (kept[rows, :].astype(F32) + came[rows, :].astype(F32)).astype(LOW)
-                return 0
-
-            lax.fori_loop(0, kept.shape[0] // tile, add, 0)
+            rows = came.shape[-2]
+            tile = 48 if rows % 48 == 0 else 32 if rows % 32 == 0 else 16
+            for choice in np.ndindex(*came.shape[:-2]):
+
+                def add(step, _, kept=kept, came=came, choice=choice):
+                    span = choice + (pl.ds(pl.multiple_of(step * tile, tile), tile), slice(None))
+                    kept[span] = (kept[span].astype(F32) + came[span].astype(F32)).astype(LOW)
+                    return 0
+
+                lax.fori_loop(0, rows // tile, add, 0)
         if stage == self.count - 1:
             self.stack()
 
     def stack(self):
-        bands = self.links.bands
-        parts = self.scratch[2 * self.count - 1]
-        whole = self.piece(self.links.items, 0, self.columns)
-        rows = whole.shape[0] // bands
-        if parts.shape[1] == rows:
-            for number in range(bands):
-                parts[number] = whole[number * rows : (number + 1) * rows, :]
+        bands, parts = self.links.bands, self.scratch[2 * self.count - 1]
+        rows = self.array.shape[0] // self.axis
+        start = pl.multiple_of(self.links.items * rows, rows)
+        whole = self.array.at[pl.ds(start, rows), pl.ds(self.first, self.columns)]
+        rows = rows // bands
+        spans = [slice(number * rows, (number + 1) * rows) for number in range(bands)]
+        places = list(np.ndindex(*parts.shape[:-2]))
+        if parts.shape[-2] == rows:
+            for place, span in zip(places, spans):
+                parts[place] = whole[span, :]
             return
         half = self.columns // 2
         left, right = whole[:, :half].astype(F32), whole[:, half:].astype(F32)
-        for number in range(bands):
-            span = slice(number * rows, (number + 1) * rows)
-            parts[number] = jnp.concatenate([left[span], right[span]], 0).astype(LOW)
+        for place, span in zip(places, spans):
+            parts[place] = jnp.concatenate([left[span], right[span]], 0).astype(LOW)
 
     def advance(self):
         if self.state > self.stages:
@@ -528,17 +552,17 @@
     home_out, home_grad = refs[:2]
     query_far, key_far, value_far, attended_t_far, grad_attended_t_far, cot_far = refs[2:8]
     refs = refs[8:]
-    sums, refs = (refs[:8], refs[8:]) if fused else (refs[:5], refs[5:])
+    sums, refs = (refs[:9], refs[9:]) if fused else (refs[:5], refs[5:])
     weights_t, w_out, w_feed, w_down, g_feed, g_down, g_out = refs[:7]
     x, cot, attended, attended_t, query, key, value, grad_attended_t = refs[7:15]
     normed, normed_t, resid, out_acc, back_acc, log_total, g_norm, g_norm_ffn = refs[15:23]
-    local, send, receive = refs[23:26]
-    sum_refs = refs[26:]
+    w_own, w_total, local, send, receive = refs[23:28]
+    sum_refs = refs[28:]
     seq, width = x.shape[1:]
     ff = w_down.shape[0]
     band_rows, items = seq // bands, bands * per
     groups = width // GROUP
-    links = Links(bands, send, receive)
+    links = Links(bands, axis, send, receive)
     band = links.band
     gain_attn, gain_ffn = norm_attn[...][None, :], norm_ffn[...][None, :]
     started = [0]
@@ -554,7 +578,7 @@
     load_tokens = bring(tokens, raw)
     qkv = (g_feed.at[:, pl.ds(0, width)], g_feed.at[:, pl.ds(width, width)], g_feed.at[:, pl.ds(2 * width, width)])
     load_qkv = [bring(source, target) for source, target in zip((w_query, w_key, w_value), qkv)]
-    links.greet(axis)
+    all_here = links.greet()
 
     def own_rows(shift):
         return pl.ds(pl.multiple_of(links.other(shift) * band_rows, band_rows), band_rows)
@@ -564,7 +588,7 @@
     order = split_order(items, chunk, band * per)
     token_send = [attended.at[item] for item in range(per)]
     stages = [normed, resid]
-    cot_send = [g_out] + [cot_far.at[item] for item in range(per - 1)]
+    cot_send = [g_out.at[:, pl.ds(0, width)]] + [cot_far.at[item] for item in range(per - 1)]
 
     def split(kept, sent):
         for block in range(band_rows // chunk):
@@ -598,6 +622,7 @@
 
     load_tokens.wait()
     split(x, token_send)
+    all_here()
     token_links[0].start()
     load_cot = bring(cotangent, raw)
     load_rest = [
@@ -610,8 +635,24 @@
         load_qkv[part].wait()
         for at in range(0, width, 256):
             weights_t[part * width + at : part * width + at + 256, :] = qkv[part][:, at : at + 256].T
+        if fused:
+            own = w_own.shape[0]
+            device = links.items * bands + band
+            if part == 0:
+                halves_of = axis * bands // 2
+                column = jnp.concatenate([gain_attn, jnp.zeros((LANES - 1, width), F32)], 0).T
+                out_acc[: width // 2, :LANES] = column[: width // 2]
+                out_acc[: width // 2, LANES : 2 * LANES] = column[width // 2 :]
+                at = pl.multiple_of(lax.rem(device, halves_of) * own, 8)
+                both = out_acc[pl.ds(at, own), : 2 * LANES]
+                own_gain = 1.0 / jnp.where(device < halves_of, both[:, :1], both[:, LANES : LANES + 1])
+            both = qkv[part][pl.ds(pl.multiple_of(lax.div(device, 2) * (2 * own), 16), 2 * own), :].astype(F32)
+            mine = jnp.where(lax.rem(device, 2) == 0, both[:own], both[own:]) * own_gain
+            for number in range(groups):
+                at = (number * 3 + part) * GROUP
+                w_own[:, at : at + GROUP] = mine[:, number * GROUP : (number + 1) * GROUP]
     load_cot.wait()
-    split(cot, [g_out] + stages[: per - 1])
+    split(cot, cot_send[:1] + stages[: per - 1])
     late = pl.ds(0, (bands - 1) * band_rows)
     to_far = [bring(stages[item].at[late], cot_far.at[item]) for item in range(per - 1)]
 
@@ -620,7 +661,8 @@
     if fused:
         scratch_each = len(sum_scratch(axis, bands, (axis * bands * 16, 256)))
         taken = [0]
-        o_gate, o_up, o_down, o_out, o_query, o_key, o_value, o_norm = sums
+        o_gate, o_up, o_down, o_out, o_query, o_key, o_value, o_norm_ffn, o_norm_attn = sums
+        w_total[...] = jnp.zeros_like(w_total)
 
         def summing(name, array, first, columns, finish):
             sums_of[name] = Summing(
@@ -644,25 +686,28 @@
             o_down[...] = total
 
         def finish_out(total):
-            o_out[:, : width // 2], o_out[:, width // 2 :] = halves(total)
-
-        def finish_norm(total):
-            o_norm[:, :128], o_norm[:, 128:] = halves(total)
+            left, right = halves(total)
+            half = left.shape[1]
+            o_out[:, :half] = left
+            o_out[:, half:] = right[:, : width - half]
+            o_norm_ffn[...] = right[:, width - half : width - half + LANES].T[:1, :]
 
         summing("down", g_down, 0, width, finish_down)
-        summing("out", g_out, 0, width, finish_out)
+        summing("out", g_out, 0, width + 2 * LANES, finish_out)
         for number in range(groups):
 
             def finish_group(total, number=number):
                 left, right = halves(total)
                 at, half = number * GROUP, GROUP // 2
+                own = w_own[:, 3 * at : 3 * at + 3 * GROUP]
+                middle = left.shape[1]
+                w_total[...] += jnp.sum(left * own[:, :middle] + right * own[:, middle:], -1, keepdims=True)
                 o_query[:, at : at + GROUP] = left[:, :GROUP]
                 o_key[:, at : at + half] = left[:, GROUP:]
                 o_key[:, at + half : at + GROUP] = right[:, :half]
                 o_value[:, at : at + GROUP] = right[:, half:]
 
             summing(("back", number), w_feed, number * 3 * GROUP, 3 * GROUP, finish_group)
-        summing("norm", w_feed, 3 * width, 256, finish_norm)
 
     def advance(*names):
         for name in names:
@@ -678,7 +723,7 @@
             spills.pop().wait()
 
     g_weights = w_feed
-    grads = w_feed.at[pl.ds(0, 3 * GROUP), pl.ds(3 * width + 256, seq)]
+    grads = w_feed.at[pl.ds(0, 3 * GROUP), pl.ds(3 * width, seq)]
     for item in range(per):
         last = item == per - 1
         if item == 0:
@@ -704,11 +749,10 @@
             for load in load_rest:
                 load.wait()
         cot_links[item].arrived()
-        if last:
-            for ahead in range(per - 1):
-                out_links[ahead].start()
-        else:
+        if not last:
             token_links[item + 1].start()
+        elif per > 1:
+            out_links[item - 1].start()
 
         def feed_tick(step, item=item, last=last):
             if not last:
@@ -725,24 +769,25 @@
                     def _(at=at):
                         advance(*[("feed", number) for number in range(at)])
 
-        def before_out(item=item):
-            if item == 0:
-                cot_links[0].left()
-
+        cot_links[item].left()
         feed_item(
             item > 0, x.at[item], attended.at[item], attended_t, cot.at[item], w_out, w_feed, w_down, gain_ffn,
             g_feed, g_down, g_out, g_norm_ffn, attended.at[item], grad_attended_t,
-            (normed, normed_t, resid, out_acc, back_acc), feed_tick, before_out,
+            (normed, normed_t, resid, out_acc, back_acc), feed_tick,
         )
         if not last:
             spill(
                 (source, target.at[item])
                 for source, target in ((attended_t, attended_t_far), (grad_attended_t, grad_attended_t_far))
             )
+    feeds = [("feed", step) for step in range(ff // WIDE)]
+    backs = [("back", number) for number in range(groups)]
+    if fused:
+        column = jnp.concatenate([g_norm_ffn[...], jnp.zeros((LANES - 1, width), F32)], 0).T
+        g_out[:, width : width + LANES] = column.astype(LOW)
+        g_out[:, width + LANES :] = jnp.zeros((width, LANES), LOW)
+        advance(*feeds, "down", "out")
     out_links[per - 1].start()
-    feeds = [("feed", step) for step in range(ff // WIDE)]
-    if fused:
-        advance(*feeds, "down", "out")
     turns = list(reversed(range(per)))
     reloads = []
     for turn, item in enumerate(turns):
@@ -758,20 +803,19 @@
                     advance(*names)
 
         def plan(turn, last):
-            out = {}
-            for place in range(groups * PAIRS):
-                names = []
-                if turn == 0 and place % 2 == 1:
-                    names += feeds
-                if turn == 0 and place in (2, 5) or turn == 1 and place in (1, 3, 5):
-                    names += ["down", "out"]
-                if turn == 1 and place == 0:
-                    names += feeds
-                if last and place >= PAIRS:
-                    names += [("back", number) for number in range(place // PAIRS)]
-                if names:
-                    out[place] = names
-            return out
+            out = {place: [] for place in range(groups * PAIRS)}
+            if turn == 0:
+                out[1] = feeds[1:]
+                out[3] = feeds[2:] + ["down", "out"]
+                out[5] = feeds[3:]
+            if turn == 1:
+                out[2] = feeds + ["down", "out"]
+                out[4] = ["down", "out"]
+            if last:
+                for number in range(groups - 1):
+                    for place in range((number + 1) * PAIRS, groups * PAIRS):
+                        out[place].append(backs[number])
+            return {place: names for place, names in out.items() if names}
 
         def heads_done(turn=turn, last=last):
             if not last:
@@ -782,7 +826,7 @@
                 ):
                     reloads.append(bring(source.at[following], target))
             elif fused:
-                advance(*[("back", number) for number in range(groups)])
+                advance(*backs[1:])
 
         back_item(
             turn > 0, lengths[band * per + item], x.at[item], cot.at[item], grad_attended_t, attended_t, query, key,
@@ -797,20 +841,22 @@
         own.append(bring(attended.at[item, own_rows(0)], home_out.at[item]))
         own.append(bring(cot.at[item, own_rows(0)], home_grad.at[item]))
     if fused:
-        lanes = 128
-        pad = jnp.zeros((lanes - 1, width), F32)
-        for at, total in enumerate((g_norm, g_norm_ffn)):
-            spread = jnp.concatenate([total[...], pad], 0).T
-            w_feed[:, 3 * width + at * lanes : 3 * width + (at + 1) * lanes] = spread.astype(LOW)
-        every = feeds + ["down", "out"] + [("back", number) for number in range(groups)] + ["norm"]
+        every = feeds + ["down", "out"] + backs
+        first, *_, last = backs
+        for names in ([last] + backs[1:-1], [last], ["down", "out", first], [last], backs[1:-1], [last]):
+            advance(*names)
         while any(sums_of[name].state <= sums_of[name].stages for name in every):
-            advance(*every)
+            least = min(sums_of[name].state for name in every)
+            advance(*[name for name in every if sums_of[name].state == least])
+        o_norm_attn[...] = w_total[...].T[:1, :]
         for name in every:
             sums_of[name].close()
     else:
         own += [
             bring(source, target)
-            for source, target in zip((g_feed, g_down, g_out, g_weights.at[:, pl.ds(0, 3 * width)]), sums[:4])
+            for source, target in zip(
+                (g_feed, g_down, g_out.at[:, pl.ds(0, width)], g_weights.at[:, pl.ds(0, 3 * width)]), sums[:4]
+            )
         ]
         sums[4][0:1, :] = g_norm[...]
         sums[4][1:2, :] = g_norm_ffn[...]
@@ -820,8 +866,6 @@
         for exchange in (out_links[item], grad_links[item]):
             exchange.arrived()
             exchange.left()
-        if item:
-            cot_links[item].left()
 
 
 def block(bands, axis, lengths, tokens, cotangent, gains, tables, weights):
@@ -841,10 +885,10 @@
     if fused:
         devices = axis * bands
         rows, ff_rows = width // devices, ff // devices
-        out_shape += [full(rows, ff), full(rows, ff), full(ff_rows, width)] + [full(rows, width)] * 4 + [full(rows, 256)]
-        out_specs += [inside] * 8
-        shapes = [(width, 2 * WIDE)] * (ff // WIDE) + [(ff, width), (width, width)]
-        shapes += [(width, 3 * GROUP)] * (width // GROUP) + [(width, 256)]
+        out_shape += [full(rows, ff), full(rows, ff), full(ff_rows, width)] + [full(rows, width)] * 4 + [full(1, rows)] * 2
+        out_specs += [inside] * 9
+        shapes = [(width, 2 * WIDE)] * (ff // WIDE) + [(ff, width), (width, width + 2 * LANES)]
+        shapes += [(width, 3 * GROUP)] * (width // GROUP)
         for shape in shapes:
             extra += sum_scratch(axis, bands, shape)
         links += len(shapes) * sum_links(axis, bands)
@@ -859,11 +903,12 @@
         out_specs=out_specs,
         scratch_shapes=[
             scratch(3 * width, width), scratch(width, width), scratch(width, 2 * ff), scratch(ff, width),
-            scratch(width, 2 * ff), scratch(ff, width), scratch(width, width),
+            scratch(width, 2 * ff), scratch(ff, width), scratch(width, width + 2 * LANES),
             scratch(per, seq, width), scratch(per, seq, width), scratch(per, seq, width), scratch(width, seq),
             scratch(width, seq), scratch(width, seq), scratch(width, seq), scratch(width, seq),
             scratch(seq, width), scratch(width, seq), scratch(seq, width), wide(seq, width), wide(seq, width),
             wide(per, width // HEAD_DIM, 1, seq), wide(1, width), wide(1, width),
+            wide(max(width // (max(axis, 1) * bands), 8), 3 * width), wide(max(width // (max(axis, 1) * bands), 8), LANES),
             pltpu.SemaphoreType.DMA((16 + 12 * per,)),
             pltpu.SemaphoreType.DMA((links,)),
             pltpu.SemaphoreType.DMA((links,)),
@@ -902,17 +947,17 @@
     per = items // bands
     seq = bands * band_rows
     band = lax.axis_index("band")
-    fused = axis if width // axis % 16 == 0 and w_gate.shape[1] // axis % 16 == 0 else 0
+    whole_tiles = width // axis % 16 == 0 and width // axis // bands % 16 == 8 and w_gate.shape[1] // axis // bands % 16 == 0
+    fused = axis if whole_tiles else 0
     home_out, home_grad, *sums = block(
         bands, fused, lengths, tokens, cotangent, (norm_attn, norm_ffn), rope_tables(seq),
         (w_query, w_key, w_value, w_out, w_gate, w_up, w_down),
     )
     sums = sums[6:]
-    output = merge_items([home_out[at] for at in range(items)], band, bands)
-    grad_tokens = merge_items([home_grad[at] for at in range(items)], band, bands)
+    output, grad_tokens = merge_items([home_out, home_grad], band, bands)
     if fused:
-        g_gate, g_up, g_down, g_out, g_query, g_key, g_value, norms = sums
-        g_norm_attn, g_norm_ffn = norms[:, 0], norms[:, 128]
+        g_gate, g_up, g_down, g_out, g_query, g_key, g_value, g_norm_ffn, g_norm_attn = sums
+        g_norm_attn, g_norm_ffn = g_norm_attn.reshape(-1), g_norm_ffn.reshape(-1)
     else:
         axes = ("items", "band")
         total = lambda a: lax.psum_scatter(a, axes, scatter_dimension=0, tiled=True).astype(F32)

time: 260 us -> 223 us (0.86)
  Pallas kernels: 246 us -> 214 us
  local copies, waits for them, and re-layouts: 10.3 us -> 5.62 us
    pallas_call x1, Pallas kernels: 242 us -> 209 us  [block(): pl.pallas_call(functools.partial(block_kernel, bands, per, axis), name='b...]
    squeeze x1 -> x0, local copies, waits for them, and re-layouts: 3.23 us -> none  [per_device(): home_grad[at]]
where the time goes in v5:
time: 223 us; the launch traced here: 220 us
  Pallas kernels  214 us (96%)
  local copies, waits for them, and re-layouts  5.62 us (3%)
    pallas_call x1, Pallas kernels, block(): pl.pallas_call(functools.partial(block_kernel, bands, per, axis), name='b...  209 us
    unnamed x27, local copies, waits for them, and re-layouts  5.62 us

profile of v5, /device:TPU:0, one launch (start us, length us, event | category | flops | bytes accessed | tf_op | source)
XLA Modules:
  0.0 220.1 jit_solution(11724560528697282824)
XLA Ops:
  0.6 209.1 %block.1 = (bf16[8,160,768]{2,1,0:T(8,128)(2,1)}, bf16[8,160,768]{2,1,0:T(8,128)(2,1)}, bf16[1,768,640]{2,1,0:T(8,128)(2,1)}, bf16[1,768,640]{2,1,0:T(8,128)(2,1...) custom-call(s32[8]{0:T(128)} %refs_0_.1, ...), custom_call_target="tpu_custom_call" | custom-call | tf_op jit(solution)/shard_map/block/pallas_call | solution.py:898
  209.8 0.0 copy-start.8
  209.8 0.0 copy-start.6
  209.8 0.0 copy-start.5
  209.8 0.0 copy-start.4
  209.8 0.0 copy-start.3
  209.9 0.0 copy-start.7
  209.9 0.0 copy-start.2
  209.9 0.0 copy-start.1
  209.9 0.0 copy-start
  209.9 4.4 %merge_items.1 = (bf16[1280,768]{1,0:T(8,128)(2,1)}, bf16[1280,768]{1,0:T(8,128)(2,1)}) custom-call(s32[1]{0:T(128)} %bitcast.band_ref, bf16[8,160,768]{2,1,0:T(8,128)(2,1)} %get-tuple-element.24.refs_0_, bf16[8,160,768]{2,1,0:T(8,128)(2,1)} %get-tuple-element.25.refs_1_), custom_call_target="tpu_custom_call" | custom-call | tf_op jit(solution)/shard_map/merge_items/pallas_call | solution.py:94
  214.3 0.0 copy-done.8
  214.3 0.5 copy.34
  214.8 0.0 copy-done.6
  214.8 0.6 copy.35
  215.4 0.0 copy-done.5
  215.5 0.6 copy.36
  216.1 0.0 copy-done.4
  216.1 0.6 copy.37
  216.7 0.0 copy-done.3
  216.7 0.6 copy.38
  217.4 0.0 copy-done.7
  217.4 0.5 copy.39
  217.9 0.0 copy-done.2
  217.9 0.7 copy.40
  218.6 0.0 copy-done.1
  218.6 0.7 copy.41
  219.2 0.0 copy-done
  219.2 0.7 copy.42
Async XLA Ops:
  209.8 4.5 %copy-start.8 = (f32[1,24]{1,0:T(1,128)S(1)}, f32[1,24]{1,0:T(1,128)}, u32[]{:S(2)}) copy-start(f32[1,24]{1,0:T(1,128)} %get-tuple-element.28) | copy-start | bytes 292
  209.8 5.0 %copy-start.6 = (f32[24,768]{1,0:T(8,128)S(1)}, f32[24,768]{1,0:T(8,128)}, u32[]{:S(2)}) copy-start(f32[24,768]{1,0:T(8,128)} %get-tuple-element.51) | copy-start | bytes 221188
  209.8 5.6 %copy-start.5 = (f32[24,768]{1,0:T(8,128)S(1)}, f32[24,768]{1,0:T(8,128)}, u32[]{:S(2)}) copy-start(f32[24,768]{1,0:T(8,128)} %get-tuple-element.52) | copy-start | bytes 221188
  209.8 6.3 %copy-start.4 = (f32[24,768]{1,0:T(8,128)S(1)}, f32[24,768]{1,0:T(8,128)}, u32[]{:S(2)}) copy-start(f32[24,768]{1,0:T(8,128)} %get-tuple-element.53) | copy-start | bytes 221188
  209.8 6.9 %copy-start.3 = (f32[24,768]{1,0:T(8,128)S(1)}, f32[24,768]{1,0:T(8,128)}, u32[]{:S(2)}) copy-start(f32[24,768]{1,0:T(8,128)} %get-tuple-element.54) | copy-start | bytes 221188
  209.9 7.5 %copy-start.7 = (f32[1,24]{1,0:T(1,128)S(1)}, f32[1,24]{1,0:T(1,128)}, u32[]{:S(2)}) copy-start(f32[1,24]{1,0:T(1,128)} %get-tuple-element.33) | copy-start | bytes 292
  209.9 8.0 %copy-start.2 = (f32[24,2048]{1,0:T(8,128)S(1)}, f32[24,2048]{1,0:T(8,128)}, u32[]{:S(2)}) copy-start(f32[24,2048]{1,0:T(8,128)} %get-tuple-element.56) | copy-start | bytes 589828
  209.9 8.7 %copy-start.1 = (f32[24,2048]{1,0:T(8,128)S(1)}, f32[24,2048]{1,0:T(8,128)}, u32[]{:S(2)}) copy-start(f32[24,2048]{1,0:T(8,128)} %get-tuple-element.57) | copy-start | bytes 589828
  209.9 9.4 %copy-start = (f32[64,768]{1,0:T(8,128)S(1)}, f32[64,768]{1,0:T(8,128)}, u32[]{:S(2)}) copy-start(f32[64,768]{1,0:T(8,128)} %get-tuple-element.58) | copy-start | bytes 589828

commit v6 on v5

--- a/solution.py
+++ b/solution.py
@@ -58,14 +58,25 @@
     return jnp.where(col == (row & (chunk - 1)) * items + item, 1.0, 0.0).astype(LOW)
 
 
-def merge_kernel(per, chunk, band_ref, *refs):
-    count = (len(refs) - 1) // 4
-    ins, outs, held, made, sem = refs[:count], refs[count : 2 * count], refs[2 * count : 3 * count], refs[3 * count : -1], refs[-1]
-    loads = [pltpu.make_async_copy(ins[at], held[at], sem.at[at]) for at in range(count)]
-    for load in loads:
-        load.start()
+def merge_kernel(per, chunk, passed, flat, band_ref, *refs):
+    count = passed + flat + 2
+    ins, outs, refs = refs[:count], refs[count : 2 * count], refs[2 * count :]
+    held, made, sem, through = refs[:2], refs[2:4], refs[4], refs[5:]
     items, band_rows, width = ins[0].shape
-    size, bands = items * chunk, items // per
+    size, bands, blocks = items * chunk, items // per, band_rows // chunk
+    started = []
+
+    def bring(source, target):
+        copy = pltpu.make_async_copy(source, target, sem.at[len(started)])
+        started.append(copy)
+        copy.start()
+        return copy
+
+    loads = [bring(ins[at], held[at]) for at in range(2)]
+    passing = [bring(source, place) for source, place in zip(ins[2 : 2 + passed], through)]
+    stores = []
+    for at in range(2 + passed, count):
+        outs[at][...] = ins[at][0, :]
     row = lax.broadcasted_iota(jnp.int32, (size, size), 0)
     col = lax.broadcasted_iota(jnp.int32, (size, size), 1)
     number = col >> log2_of(chunk)
@@ -73,36 +84,40 @@
     source = jnp.where(source < 0, source + bands, source)
     item = source * per + (number & (per - 1))
     order = jnp.where(row == (col & (chunk - 1)) * items + item, 1.0, 0.0).astype(LOW)
-    stores = []
-    for at in range(count):
+    for at in range(2):
         loads[at].wait()
-        for block in range(band_rows // chunk):
-            rows = slice(block * size, (block + 1) * size)
+        for block in range(blocks):
             parts = held[at][:, block * chunk : (block + 1) * chunk, :].reshape(size, width)
-            made[at][rows, :] = dot_nn(order, parts).astype(LOW)
-        stores.append(pltpu.make_async_copy(made[at], outs[at], sem.at[count + at]))
-        stores[-1].start()
+            made[at][block * size : (block + 1) * size, :] = dot_nn(order, parts).astype(LOW)
+        stores.append(bring(made[at], outs[at]))
+        if at == 0:
+            for copy, place, out in zip(passing, through, outs[2 : 2 + passed]):
+                copy.wait()
+                stores.append(bring(place, out))
     for store in stores:
         store.wait()
 
 
-def merge_items(arrays, band, bands):
+def merge_items(arrays, passed, flat, band, bands):
     items, band_rows, width = arrays[0].shape
     chunk = 32 if band_rows % 32 == 0 else 16
-    count = len(arrays)
     outside = pl.BlockSpec(memory_space=pl.ANY)
+    inside = pl.BlockSpec(memory_space=pltpu.VMEM)
     merged = pl.pallas_call(
-        functools.partial(merge_kernel, items // bands, chunk),
+        functools.partial(merge_kernel, items // bands, chunk, len(passed), len(flat)),
         name="merge_items",
-        out_shape=[jax.ShapeDtypeStruct((band_rows * items, width), LOW)] * count,
-        in_specs=[smem()] + [outside] * count,
-        out_specs=[outside] * count,
-        scratch_shapes=[pltpu.VMEM((items, band_rows, width), LOW)] * count
-        + [pltpu.VMEM((band_rows * items, width), LOW)] * count
-        + [pltpu.SemaphoreType.DMA((2 * count,))],
+        out_shape=[jax.ShapeDtypeStruct((band_rows * items, width), LOW)] * 2
+        + [jax.ShapeDtypeStruct(array.shape, array.dtype) for array in passed]
+        + [jax.ShapeDtypeStruct(array.shape[1:], array.dtype) for array in flat],
+        in_specs=[smem()] + [outside] * (2 + len(passed)) + [inside] * len(flat),
+        out_specs=[outside] * (2 + len(passed)) + [inside] * len(flat),
+        scratch_shapes=[pltpu.VMEM((items, band_rows, width), LOW)] * 2
+        + [pltpu.VMEM((band_rows * items, width), LOW)] * 2
+        + [pltpu.SemaphoreType.DMA((4 * (band_rows // chunk) + 2 * len(passed),))]
+        + [pltpu.VMEM(array.shape, array.dtype) for array in passed],
         compiler_params=params(60),
-    )(jnp.reshape(band, (1,)), *arrays)
-    return [array.reshape(band_rows, items, width) for array in merged]
+    )(jnp.reshape(band, (1,)), *arrays, *passed, *flat)
+    return [array.reshape(band_rows, items, width) for array in merged[:2]], merged[2:]
 
 
 def rope(vector, cos, sin):
@@ -552,7 +567,7 @@
     home_out, home_grad = refs[:2]
     query_far, key_far, value_far, attended_t_far, grad_attended_t_far, cot_far = refs[2:8]
     refs = refs[8:]
-    sums, refs = (refs[:9], refs[9:]) if fused else (refs[:5], refs[5:])
+    sums, refs = (refs[:9], refs[9:]) if fused else (refs[:6], refs[6:])
     weights_t, w_out, w_feed, w_down, g_feed, g_down, g_out = refs[:7]
     x, cot, attended, attended_t, query, key, value, grad_attended_t = refs[7:15]
     normed, normed_t, resid, out_acc, back_acc, log_total, g_norm, g_norm_ffn = refs[15:23]
@@ -858,8 +873,8 @@
                 (g_feed, g_down, g_out.at[:, pl.ds(0, width)], g_weights.at[:, pl.ds(0, 3 * width)]), sums[:4]
             )
         ]
-        sums[4][0:1, :] = g_norm[...]
-        sums[4][1:2, :] = g_norm_ffn[...]
+        sums[4][...] = g_norm_ffn[...]
+        sums[5][...] = g_norm[...]
     for copy in own:
         copy.wait()
     for item in range(per):
@@ -893,8 +908,8 @@
             extra += sum_scratch(axis, bands, shape)
         links += len(shapes) * sum_links(axis, bands)
     else:
-        out_shape += [low(width, 2 * ff), low(ff, width), low(width, width), low(width, 3 * width), full(2, width)]
-        out_specs += [outside] * 4 + [inside]
+        out_shape += [low(width, 2 * ff), low(ff, width), low(width, width), low(width, 3 * width)] + [full(1, width)] * 2
+        out_specs += [outside] * 4 + [inside] * 2
     return pl.pallas_call(
         functools.partial(block_kernel, bands, per, axis),
         name="block",
@@ -954,16 +969,16 @@
         (w_query, w_key, w_value, w_out, w_gate, w_up, w_down),
     )
     sums = sums[6:]
-    output, grad_tokens = merge_items([home_out, home_grad], band, bands)
     if fused:
+        (output, grad_tokens), sums = merge_items([home_out, home_grad], sums[:-2], sums[-2:], band, bands)
         g_gate, g_up, g_down, g_out, g_query, g_key, g_value, g_norm_ffn, g_norm_attn = sums
-        g_norm_attn, g_norm_ffn = g_norm_attn.reshape(-1), g_norm_ffn.reshape(-1)
     else:
+        (output, grad_tokens), norms = merge_items([home_out, home_grad], [], sums[-2:], band, bands)
         axes = ("items", "band")
         total = lambda a: lax.psum_scatter(a, axes, scatter_dimension=0, tiled=True).astype(F32)
         g_feed, g_down, g_out, g_weights = (total(a) for a in sums[:4])
-        norms = total(sums[4].T)
-        g_norm_attn, g_norm_ffn = norms[:, 0], norms[:, 1]
+        norms = total(jnp.stack(norms, 1))
+        g_norm_ffn, g_norm_attn = norms[:, 0], norms[:, 1]
         g_gate, g_up = jnp.moveaxis(g_feed.reshape(-1, w_gate.shape[1] // WIDE, 2, WIDE), 2, 0).reshape(2, -1, w_gate.shape[1])
         g_query, g_key, g_value = jnp.moveaxis(g_weights.reshape(-1, width // GROUP, 3, GROUP), 2, 0).reshape(3, -1, width)
     return (

time: 223 us -> 219 us (0.982)
  local copies, waits for them, and re-layouts: 5.62 us -> 0 us
    unnamed x27 -> x0, local copies, waits for them, and re-layouts: 5.62 us -> none
where the time goes in v6:
time: 219 us; the launch traced here: 216 us
  Pallas kernels  215 us (98%)
    pallas_call x1, Pallas kernels, block(): pl.pallas_call(functools.partial(block_kernel, bands, per, axis), name='b...  209 us
    pallas_call x1, Pallas kernels, merge_items(): pl.pallas_call(functools.partial(merge_kernel, items // bands, chunk, len...  5.93 us

profile of v6, /device:TPU:0, one launch (start us, length us, event | category | flops | bytes accessed | tf_op | source)
XLA Modules:
  0.0 215.9 jit_solution(11937890896732572008)
XLA Ops:
  0.6 209.2 %block.1 = (bf16[8,160,768]{2,1,0:T(8,128)(2,1)}, bf16[8,160,768]{2,1,0:T(8,128)(2,1)}, bf16[1,768,640]{2,1,0:T(8,128)(2,1)}, bf16[1,768,640]{2,1,0:T(8,128)(2,1...) custom-call(s32[8]{0:T(128)} %refs_0_.1, ...), custom_call_target="tpu_custom_call" | custom-call | tf_op jit(solution)/shard_map/block/pallas_call | solution.py:913
  209.8 5.9 %merge_items.1 = (bf16[1280,768]{1,0:T(8,128)(2,1)}, bf16[1280,768]{1,0:T(8,128)(2,1)}, f32[24,2048]{1,0:T(8,128)}, f32[24,2048]{1,0:T(8,128)}, f32[64,768]{1,0:...) custom-call(s32[1]{0:T(128)} %bitcast.band_ref, ...), custom_call_target="tpu_custom_call" | custom-call | tf_op jit(solution)/shard_map/merge_items/pallas_call | solution.py:106

commit v7 on v6

--- a/solution.py
+++ b/solution.py
@@ -49,13 +49,13 @@
     return number.bit_length() - 1
 
 
-def split_order(items, chunk, first):
-    size = items * chunk
-    row = lax.broadcasted_iota(jnp.int32, (size, size), 0)
-    col = lax.broadcasted_iota(jnp.int32, (size, size), 1)
-    item = (row >> log2_of(chunk)) + first
-    item = jnp.where(item >= items, item - items, item)
-    return jnp.where(col == (row & (chunk - 1)) * items + item, 1.0, 0.0).astype(LOW)
+def split_order(bands, per, chunk, band, item):
+    items = bands * per
+    row = lax.broadcasted_iota(jnp.int32, (bands * chunk, items * chunk), 0)
+    col = lax.broadcasted_iota(jnp.int32, (bands * chunk, items * chunk), 1)
+    other = (row >> log2_of(chunk)) + band
+    other = jnp.where(other >= bands, other - bands, other)
+    return jnp.where(col == (row & (chunk - 1)) * items + other * per + item, 1.0, 0.0).astype(LOW)
 
 
 def merge_kernel(per, chunk, passed, flat, band_ref, *refs):
@@ -175,8 +175,8 @@
     ready()
 
     def head(at, _):
-        for which in range(2):
-            number = at * 2 + which
+        for which in range(4):
+            number = at * 4 + which
             rows = pl.ds(pl.multiple_of(number * HEAD_DIM, HEAD_DIM), HEAD_DIM)
             keys, values = key[rows, :], value[rows, :]
             for start, stop in query_blocks(seq):
@@ -192,7 +192,7 @@
                 log_total[number, :, start:stop] = top + jnp.log2(total)
         return 0
 
-    lax.fori_loop(0, width // HEAD_DIM // 2, head, 0)
+    lax.fori_loop(0, width // HEAD_DIM // 4, head, 0)
     for at in range(0, width, project):
         attended[:, at : at + project] = attended_t[at : at + project, :].T
 
@@ -202,7 +202,7 @@
 WIDE = 512
 
 
-def feed_item(follows, x, attended, attended_t, cot, w_out, w_feed, w_down, gain, g_feed, g_down, g_out, g_norm, out, grad_attended_t, scratch, tick):
+def feed_item(follows, x, attended, attended_t, cot, w_out, w_feed, w_down, gain, g_feed, g_down, g_out, g_norm, out, grad_attended_t, scratch, cot_ready, tick, out_done):
     normed, normed_t, resid, out_acc, back_acc = scratch
     seq, width = x.shape
     ff = w_down.shape[0]
@@ -222,6 +222,7 @@
         normed[rows, :] = low
         normed_t[:, rows] = low.T
     back_acc[...] = jnp.zeros_like(back_acc)
+    cot_ready()
 
     def chunk(step, _):
         tick(step)
@@ -263,10 +264,12 @@
         return 0
 
     lax.fori_loop(0, ff // WIDE, chunk, 0)
+    for at in range(0, seq, tile):
+        out[at : at + tile, :] = out_acc[at : at + tile, :].astype(LOW)
+    out_done()
     norm_sum = jnp.zeros((1, width), F32)
     for at in range(0, seq, tile):
         rows = slice(at, at + tile)
-        out[rows, :] = out_acc[rows, :].astype(LOW)
         total, incoming = resid[rows, :].astype(F32), back_acc[rows, :]
         inv = norm_rows(total)
         scaled = total * inv
@@ -510,6 +513,7 @@
         flights = self.flights(stage)
         for copy, _, _ in flights:
             copy.wait_recv()
+            copy.wait_send()
         for _, kept, came in flights:
             if stage == self.stages - 1:
                 self.finish(kept[...].astype(F32) + came[...].astype(F32))
@@ -520,7 +524,7 @@
 
                 def add(step, _, kept=kept, came=came, choice=choice):
                     span = choice + (pl.ds(pl.multiple_of(step * tile, tile), tile), slice(None))
-                    kept[span] = (kept[span].astype(F32) + came[span].astype(F32)).astype(LOW)
+                    kept[span] = kept[span] + came[span]
                     return 0
 
                 lax.fori_loop(0, rows // tile, add, 0)
@@ -552,11 +556,6 @@
         if self.state < self.stages:
             self.begin(self.state)
         self.state += 1
-
-    def close(self):
-        for stage in range(self.stages):
-            for copy, _, _ in self.flights(stage):
-                copy.wait_send()
 
 
 def block_kernel(bands, per, axis, *refs):
@@ -589,8 +588,11 @@
         return copy
 
     token_rows = band_rows * items
+    chunk = 32 if band_rows % 32 == 0 else 16
+    size = items * chunk
     raw = g_down.at[pl.ds(0, token_rows)]
-    load_tokens = bring(tokens, raw)
+    spans = [pl.ds(at, size) for at in range(0, token_rows, size)]
+    load_tokens = [bring(tokens.at[span], raw.at[span]) for span in spans]
     qkv = (g_feed.at[:, pl.ds(0, width)], g_feed.at[:, pl.ds(width, width)], g_feed.at[:, pl.ds(2 * width, width)])
     load_qkv = [bring(source, target) for source, target in zip((w_query, w_key, w_value), qkv)]
     all_here = links.greet()
@@ -598,25 +600,20 @@
     def own_rows(shift):
         return pl.ds(pl.multiple_of(links.other(shift) * band_rows, band_rows), band_rows)
 
-    chunk = 32 if band_rows % 32 == 0 else 16
-    size = items * chunk
-    order = split_order(items, chunk, band * per)
     token_send = [attended.at[item] for item in range(per)]
     stages = [normed, resid]
     cot_send = [g_out.at[:, pl.ds(0, width)]] + [cot_far.at[item] for item in range(per - 1)]
 
-    def split(kept, sent):
+    def split(kept, sent, item, loads=()):
+        order = split_order(bands, per, chunk, band, item)
         for block in range(band_rows // chunk):
+            if loads:
+                loads[block].wait()
             moved = dot_nn(order, raw[block * size : (block + 1) * size, :]).astype(LOW)
-            rows = pl.ds(pl.multiple_of(band * band_rows + block * chunk, 16), chunk)
-            for at in range(items):
-                part = moved[at * chunk : (at + 1) * chunk]
-                shift, item = at // per, at % per
-                if shift == 0:
-                    kept[item, rows, :] = part
-                else:
-                    place = (shift - 1) * band_rows + block * chunk
-                    sent[item][place : place + chunk, :] = part
+            kept[item, pl.ds(pl.multiple_of(band * band_rows + block * chunk, 16), chunk), :] = moved[:chunk]
+            for shift in range(1, bands):
+                place = (shift - 1) * band_rows + block * chunk
+                sent[place : place + chunk, :] = moved[shift * chunk : (shift + 1) * chunk]
 
     def scattering(sent, kept, item):
         return Exchange(
@@ -635,10 +632,11 @@
     out_links = [returning(attended, home_out, item) for item in range(per)]
     grad_links = [returning(cot, home_grad, item) for item in range(per)]
 
-    load_tokens.wait()
-    split(x, token_send)
+    split(x, token_send[0], 0, load_tokens)
     all_here()
     token_links[0].start()
+    for item in range(1, per):
+        split(x, token_send[item], item)
     load_cot = bring(cotangent, raw)
     load_rest = [
         bring(w_out_from, w_out),
@@ -667,7 +665,8 @@
                 at = (number * 3 + part) * GROUP
                 w_own[:, at : at + GROUP] = mine[:, number * GROUP : (number + 1) * GROUP]
     load_cot.wait()
-    split(cot, cot_send[:1] + stages[: per - 1])
+    for item in range(per):
+        split(cot, stages[item - 1] if item else cot_send[0], item)
     late = pl.ds(0, (bands - 1) * band_rows)
     to_far = [bring(stages[item].at[late], cot_far.at[item]) for item in range(per - 1)]
 
@@ -763,11 +762,13 @@
         if item == 0:
             for load in load_rest:
                 load.wait()
-        cot_links[item].arrived()
-        if not last:
-            token_links[item + 1].start()
-        elif per > 1:
-            out_links[item - 1].start()
+        def cot_ready(item=item, last=last):
+            cot_links[item].arrived()
+            if not last:
+                token_links[item + 1].start()
+            elif per > 1:
+                out_links[item - 1].start()
+            cot_links[item].left()
 
         def feed_tick(step, item=item, last=last):
             if not last:
@@ -784,11 +785,10 @@
                     def _(at=at):
                         advance(*[("feed", number) for number in range(at)])
 
-        cot_links[item].left()
         feed_item(
             item > 0, x.at[item], attended.at[item], attended_t, cot.at[item], w_out, w_feed, w_down, gain_ffn,
             g_feed, g_down, g_out, g_norm_ffn, attended.at[item], grad_attended_t,
-            (normed, normed_t, resid, out_acc, back_acc), feed_tick,
+            (normed, normed_t, resid, out_acc, back_acc), cot_ready, feed_tick, out_links[item].start if last else lambda: None,
         )
         if not last:
             spill(
@@ -802,7 +802,6 @@
         g_out[:, width : width + LANES] = column.astype(LOW)
         g_out[:, width + LANES :] = jnp.zeros((width, LANES), LOW)
         advance(*feeds, "down", "out")
-    out_links[per - 1].start()
     turns = list(reversed(range(per)))
     reloads = []
     for turn, item in enumerate(turns):
@@ -864,8 +863,6 @@
             least = min(sums_of[name].state for name in every)
             advance(*[name for name in every if sums_of[name].state == least])
         o_norm_attn[...] = w_total[...].T[:1, :]
-        for name in every:
-            sums_of[name].close()
     else:
         own += [
             bring(source, target)
@@ -924,7 +921,7 @@
             scratch(seq, width), scratch(width, seq), scratch(seq, width), wide(seq, width), wide(seq, width),
             wide(per, width // HEAD_DIM, 1, seq), wide(1, width), wide(1, width),
             wide(max(width // (max(axis, 1) * bands), 8), 3 * width), wide(max(width // (max(axis, 1) * bands), 8), LANES),
-            pltpu.SemaphoreType.DMA((16 + 12 * per,)),
+            pltpu.SemaphoreType.DMA((32 + 12 * per,)),
             pltpu.SemaphoreType.DMA((links,)),
             pltpu.SemaphoreType.DMA((links,)),
         ]

time: 219 us -> 217 us (level)
  no operation moved by 1% of the time
where the time goes in v7:
time: 217 us; the launch traced here: 214 us
  Pallas kernels  213 us (98%)
    pallas_call x1, Pallas kernels, block(): pl.pallas_call(functools.partial(block_kernel, bands, per, axis), name='b...  207 us
    pallas_call x1, Pallas kernels, merge_items(): pl.pallas_call(functools.partial(merge_kernel, items // bands, chunk, len...  5.93 us

profile of v7, /device:TPU:0, one launch (start us, length us, event | category | flops | bytes accessed | tf_op | source)
XLA Modules:
  0.0 214.0 jit_solution(6092887535356109439)
XLA Ops:
  0.6 207.1 %block.1 = (bf16[8,160,768]{2,1,0:T(8,128)(2,1)}, bf16[8,160,768]{2,1,0:T(8,128)(2,1)}, bf16[1,768,640]{2,1,0:T(8,128)(2,1)}, bf16[1,768,640]{2,1,0:T(8,128)(2,1...) custom-call(s32[8]{0:T(128)} %refs_0_.1, ...), custom_call_target="tpu_custom_call" | custom-call | tf_op jit(solution)/shard_map/block/pallas_call | solution.py:910
  207.8 5.9 %merge_items.1 = (bf16[1280,768]{1,0:T(8,128)(2,1)}, bf16[1280,768]{1,0:T(8,128)(2,1)}, f32[24,2048]{1,0:T(8,128)}, f32[24,2048]{1,0:T(8,128)}, f32[64,768]{1,0:...) custom-call(s32[1]{0:T(128)} %bitcast.band_ref, ...), custom_call_target="tpu_custom_call" | custom-call | tf_op jit(solution)/shard_map/merge_items/pallas_call | solution.py:106

commit v8 on v7

--- a/solution.py
+++ b/solution.py
@@ -840,7 +840,7 @@
                 ):
                     reloads.append(bring(source.at[following], target))
             elif fused:
-                advance(*backs[1:])
+                advance(backs[-1])
 
         back_item(
             turn > 0, lengths[band * per + item], x.at[item], cot.at[item], grad_attended_t, attended_t, query, key,
@@ -857,7 +857,7 @@
     if fused:
         every = feeds + ["down", "out"] + backs
         first, *_, last = backs
-        for names in ([last] + backs[1:-1], [last], ["down", "out", first], [last], backs[1:-1], [last]):
+        for names in ([last] + backs[1:-1], [last] + backs[1:-1], ["down", "out", first], [last], backs[1:-1], [last]):
             advance(*names)
         while any(sums_of[name].state <= sums_of[name].stages for name in every):
             least = min(sums_of[name].state for name in every)

time: 217 us -> 217 us (level)
  no operation moved by 1% of the time
where the time goes in v8:
time: 217 us; the launch traced here: 214 us
  Pallas kernels  213 us (98%)
    pallas_call x1, Pallas kernels, block(): pl.pallas_call(functools.partial(block_kernel, bands, per, axis), name='b...  207 us
    pallas_call x1, Pallas kernels, merge_items(): pl.pallas_call(functools.partial(merge_kernel, items // bands, chunk, len...  5.93 us

profile of v8, /device:TPU:0, one launch (start us, length us, event | category | flops | bytes accessed | tf_op | source)
XLA Modules:
  0.0 214.0 jit_solution(6204243548671607597)
XLA Ops:
  0.6 207.1 %block.1 = (bf16[8,160,768]{2,1,0:T(8,128)(2,1)}, bf16[8,160,768]{2,1,0:T(8,128)(2,1)}, bf16[1,768,640]{2,1,0:T(8,128)(2,1)}, bf16[1,768,640]{2,1,0:T(8,128)(2,1...) custom-call(s32[8]{0:T(128)} %refs_0_.1, ...), custom_call_target="tpu_custom_call" | custom-call | tf_op jit(solution)/shard_map/block/pallas_call | solution.py:910
  207.8 5.9 %merge_items.1 = (bf16[1280,768]{1,0:T(8,128)(2,1)}, bf16[1280,768]{1,0:T(8,128)(2,1)}, f32[24,2048]{1,0:T(8,128)}, f32[24,2048]{1,0:T(8,128)}, f32[64,768]{1,0:...) custom-call(s32[1]{0:T(128)} %bitcast.band_ref, ...), custom_call_target="tpu_custom_call" | custom-call | tf_op jit(solution)/shard_map/merge_items/pallas_call | solution.py:106
